TPU v7x, 32 devices: a whole 2x2x4 slice. The times are simulated.
32 devices in a mesh: section: 2 (over x), blk: 16 (over z, y, core).
Axes of the slice: x: 2, y: 2, z: 4, core: 2. Of those that a mesh axis runs over, the one named last changes fastest.
Arguments:
- raw_traces: bfloat16 [128, 8192], P('blk', 'section'), may hold values from -6 to 6
- valid_mask: int32 [128, 8], P('blk', 'section'), may hold values from 0 to 1, as said below
- block_order: int32 [16], replicated, may hold values from 0 to 15, each once
Outputs:
- correlations: float32 [16, 128, 256], P('section', 'blk')
Inputs may be any that keep to these rules, and one draw needn't show every extreme that they name: `valid_mask`: a station either has no valid segment at all, or each of its segments is valid independently. `block_order`: each block index once.
All inputs are finite; a program needn't handle non-finite values.
Results may differ from a plain program's by a relative error of at most 0.0063.
Values may be sent and summed in bfloat16 or wider, within the bound.
No kernel may reach another device: no remote copies, remote signals or barrier semaphores. Data moves between devices by JAX's collectives and lax.ppermute only.
A program may use at most 64 MiB of HBM per device.

v0:
```python
import math

import jax
import jax.numpy as jnp
import numpy as np
from jax import lax
from jax.experimental import pallas as pl
from jax.experimental.pallas import tpu as pltpu
from jax.sharding import PartitionSpec as P

L = 1024
NF = 384
BIN_LO = 8
LAGS = 256
TAPS = 33
HW = 50
WF = 32
ST = 8
SEGS = 8
BLK = 256
ROWS = SEGS * L // BLK
PAD = 128

F32 = jnp.float32
BF16 = jnp.bfloat16


def halves(table):
    high = table.astype(BF16)
    low = (table - high.astype(np.float64)).astype(BF16)
    return high, low


def filter_table():
    k = np.arange(TAPS, dtype=np.float64) - (TAPS - 1) // 2
    low, high = BIN_LO / L, (BIN_LO + NF) / L
    window = 0.5 + 0.5 * np.cos(2.0 * math.pi * k / (TAPS + 1))
    taps = window * (2 * high * np.sinc(2 * high * k) - 2 * low * np.sinc(2 * low * k))
    shift = BLK // 2 + np.arange(BLK)[None, :] - np.arange(2 * BLK)[:, None] + (TAPS - 1) // 2
    inside = (shift >= 0) & (shift < TAPS)
    table = np.where(inside, taps[np.clip(shift, 0, TAPS - 1)], 0.0)
    return np.concatenate(halves(table), axis=1)


def mean_table():
    shift = BLK // 2 + np.arange(BLK)[None, :] - np.arange(2 * BLK)[:, None]
    return (np.abs(shift) <= HW).astype(BF16)


def smooth_table():
    bins = np.arange(NF)
    return (np.abs(bins[:, None] - bins[None, :]) <= WF).astype(BF16)


def forward_table():
    phase = np.mod(np.arange(L)[:, None] * (BIN_LO + np.arange(NF))[None, :], L) * (2.0 * math.pi / L)
    return np.concatenate([np.cos(phase), -np.sin(phase)], axis=1).astype(BF16)


def lag_table():
    shifts = np.arange(LAGS)[None, :] - LAGS // 2
    phase = np.mod((BIN_LO + np.arange(NF))[:, None] * shifts, L) * (2.0 * math.pi / L)
    table = np.concatenate([np.cos(phase), -np.sin(phase)], axis=0) / math.sqrt(NF)
    return halves(table)


def dot(a, b):
    return jnp.dot(a, b, preferred_element_type=F32)


def split(a):
    high = a.astype(BF16)
    return high, (a - high.astype(F32)).astype(BF16)


def spread(parts):
    half = parts[0].shape[1] - PAD
    rows = []
    for part in parts:
        rows += [part[:, i * BLK : (i + 1) * BLK].astype(F32) for i in range(half // BLK)]
    return rows


def mask_columns(parts):
    half = parts[0].shape[1] - PAD
    per = half // L
    tiles = [part[:, half:].astype(F32) for part in parts]
    column = jnp.concatenate([tile[:, g : g + 1] for tile in tiles for g in range(per)], axis=0)
    return tiles, column


def whitened_blocks(blocks, columns, taps, mean, table, smooth):
    count = len(blocks)
    zero = jnp.zeros((ST, BLK), F32)
    x = jnp.concatenate([t for rows in blocks for t in [zero, zero, *rows, zero, zero]], axis=0)
    n = x.shape[0]
    half = BLK // 2
    window = jnp.concatenate(
        [x[: n - 2 * ST, half:], x[ST : n - ST], x[2 * ST :, :half]], axis=1
    ).astype(BF16)
    both = dot(window, taps)
    filtered = both[:, :BLK] + both[:, BLK:]
    m = filtered.shape[0]
    size = jnp.abs(filtered)
    window = jnp.concatenate(
        [size[: m - 2 * ST, half:], size[ST : m - ST], size[2 * ST :, :half]], axis=1
    )
    high, low = split(window)
    total = dot(high, mean) + dot(low, mean)
    normal = filtered[ST : m - ST] / (total * (1.0 / (2 * HW + 1)) + 1e-06)
    span = (ROWS + 4) * ST
    per = L // BLK
    framed = []
    for b in range(count):
        part = normal[b * span : b * span + ROWS * ST].reshape(SEGS, per, ST, BLK)
        framed.append(
            jnp.concatenate([part[:, q].reshape(SEGS * ST, BLK) for q in range(per)], axis=1)
        )
    framed = jnp.concatenate(framed, axis=0).astype(BF16)
    spectra = dot(framed, table)
    real, imag = spectra[:, :NF], spectra[:, NF:]
    amplitude = jnp.sqrt(real * real + imag * imag)
    high, low = split(amplitude)
    smoothed = dot(high, smooth) + dot(low, smooth)
    factor = jnp.concatenate(columns, axis=0) / (smoothed * (1.0 / (2 * WF + 1)) + 1e-06)
    return jnp.concatenate([real * factor, imag * factor], axis=1).astype(BF16).astype(F32)


def kernel(own0, own1, src0, src1, taps, mean, table, smooth, lag_high, lag_low, out):
    own, src = (own0[...], own1[...]), (src0[...], src1[...])
    own_masks, own_column = mask_columns(own)
    src_masks, src_column = mask_columns(src)
    white = whitened_blocks(
        [spread(own), spread(src)], [own_column, src_column], taps[...], mean[...], table[...], smooth[...]
    )
    size = SEGS * ST
    recv, sent = white[:size], white[size:]
    rows, counts = [], []
    for n in range(ST):
        real = jnp.zeros((ST, NF), F32)
        imag = jnp.zeros((ST, NF), F32)
        for g in range(SEGS):
            line = sent[g * ST + n : g * ST + n + 1]
            tile = recv[g * ST : (g + 1) * ST]
            sr, si = line[:, :NF], line[:, NF:]
            rr, ri = tile[:, :NF], tile[:, NF:]
            real += rr * sr + ri * si
            imag += ri * sr - rr * si
        rows.append(jnp.concatenate([real, imag], axis=1))
        common = sum(s[n : n + 1] * r for s, r in zip(src_masks, own_masks))
        counts.append(jnp.sum(common, axis=1, keepdims=True))
    high, low = split(jnp.concatenate(rows, axis=0))
    both = dot(jnp.concatenate([high, low], axis=0), lag_high[...])
    lagged = both[:size] + both[size:] + dot(high, lag_low[...])
    lagged = lagged / jnp.maximum(jnp.concatenate(counts, axis=0), 1.0)
    out[...] = lagged.reshape(ST, ST, LAGS)


def correlate(own, src):
    tables = [filter_table(), mean_table(), forward_table(), smooth_table(), *lag_table()]
    return pl.pallas_call(
        kernel,
        out_shape=jax.ShapeDtypeStruct((ST, ST, LAGS), F32),
        in_specs=[pl.BlockSpec(memory_space=pltpu.VMEM)] * (4 + len(tables)),
        out_specs=pl.BlockSpec(memory_space=pltpu.VMEM),
        compiler_params=pltpu.CompilerParams(vmem_limit_bytes=32 * 1024 * 1024),
    )(*own, *src, *[jnp.asarray(t) for t in tables])


def shards(raw_traces, valid_mask, block_order):
    section = lax.axis_index("section")
    blocks = lax.axis_size("blk")
    me = lax.axis_index("blk")
    root = block_order[section]
    mask = jnp.pad(valid_mask.astype(BF16), ((0, 0), (0, PAD - valid_mask.shape[1])))
    mine = jnp.concatenate([raw_traces, mask], axis=1)
    other = lax.ppermute(mine, "section", [(0, 1), (1, 0)])
    own = (jnp.where(section == 0, mine, other), jnp.where(section == 0, other, mine))
    held = jnp.concatenate(own, axis=1)
    step = 1
    while step < blocks:
        got = lax.ppermute(held, "blk", [(i, i ^ step) for i in range(blocks)])
        held = jnp.where((me ^ root) & step == 0, held, got)
        step *= 2
    src = jnp.split(held, 2, axis=1)
    return correlate(own, src)


def solution(mesh):
    return jax.shard_map(
        shards,
        mesh=mesh,
        in_specs=(P("blk", "section"), P("blk", "section"), P()),
        out_specs=P("section", "blk", None),
        check_vma=False,
    )
```

profile of v0, /device:TPU:0, one launch (start us, length us, event | category | flops | bytes accessed | tf_op | source)
XLA Modules:
  0.0 36.4 jit_solution(8140846126807462927)
XLA Ops:
  0.0 0.0 copy-start.1
  0.0 0.0 copy-start
  0.0 0.0 copy-start.2
  0.0 0.8 %convert_element_type.5 = bf16[8,4]{0,1:T(4,128)(2,1)S(1)} convert(s32[8,4]{0,1:T(4,128)} %param.10) | non-fusion elementwise | flops 32 | bytes 192 | tf_op jit(solution)/shard_map/convert_element_type | solution.py:175
  0.8 0.1 copy.11
  0.9 0.8 %fusion.1 = bf16[8,4224]{1,0:T(8,128)(2,1)S(1)} fusion(bf16[8,4]{1,0:T(8,128)(2,1)S(1)} %copy.11, bf16[8,4096]{1,0:T(8,128)(2,1)} %param.9), kind=kLoop, calls=%fused_computation.7 | loop fusion | flops 202752 | bytes 133184 | tf_op jit(solution)/shard_map/concatenate | solution.py:176
  1.8 2.9 %collective-permute-start = (bf16[8,4224]{1,0:T(8,128)(2,1)S(1)}, bf16[8,4224]{1,0:T(8,128)(2,1)S(1)}, u32[]{:S(2)}, u32[]{:S(2)}) collective-permute-start(bf16[8,4224]{1,0:T(8,128)(2,1)S(1)} %fusion.1), channel_id=1, source_target_pairs={{0,16},{16,0},{1,17},{17,1},{2,18},{18,2},{3,19},{19,3},{4,20},{20... | collective-permute-start | bytes 202760 | tf_op jit(solution)/shard_map/ppermute | solution.py:177
  4.7 2.3 %collective-permute-done = bf16[8,4224]{1,0:T(8,128)(2,1)S(1)} collective-permute-done((bf16[8,4224]{1,0:T(8,128)(2,1)S(1)}, bf16[8,4224]{1,0:T(8,128)(2,1)S(1)}, u32[]{:S(2)}, u32[]{:S(2)}) %collective-permute-start) | collective-permute-done | bytes 67616 | tf_op jit(solution)/shard_map/ppermute | solution.py:177
  7.0 0.9 %broadcast_select_fusion.4 = (bf16[8,4224]{1,0:T(8,128)(2,1)S(1)}, bf16[8,4224]{1,0:T(8,128)(2,1)S(1)}) fusion(bf16[8,4224]{1,0:T(8,128)(2,1)S(1)} %collective-permute-done, pred[]{:T(512)S(6)} %eq.16, bf16[8,4]{1,0:T(8,128)(2,1)S(1)} %copy.11, bf16[8,4096]{1,0:T(8,128)(2,1)} %param.9), kind=kLoop, calls=%fused_computation.8 | loop fusion | flops 270336 | bytes 268353 | tf_op jit(solution)/shard_map/jit(_where)/select_n | solution.py:178
  7.9 0.1 collective-permute-start.1
  8.0 1.2 %dynamic_slice.3 = s32[1]{0:T(128)} dynamic-slice(s32[16]{0:T(128)} %param.11, s32[]{:T(128)S(6)} %select_n.44), dynamic_slice_sizes={1} | dynamic-slice | bytes 12 | tf_op jit(solution)/shard_map/dynamic_slice | solution.py:174
  9.9 0.0 collective-permute-done.1
  9.9 2.1 %collective-permute-start.2 = (bf16[8,8448]{1,0:T(8,128)(2,1)S(1)}, bf16[8,8448]{1,0:T(8,128)(2,1)S(1)}, u32[]{:S(2)}, u32[]{:S(2)}) collective-permute-start(bf16[8,8448]{1,0:T(8,128)(2,1)S(1)} %broadcast_select_fusion), channel_id=1, source_target_pairs={{0,2},{1,3},{2,0},{3,1},{4,6},{5,7},{6,4},{7,5},{8,10},{9,11},{10,... | collective-permute-start | bytes 405512 | tf_op jit(solution)/shard_map/ppermute | solution.py:182
  12.0 4.2 %collective-permute-done.2 = bf16[8,8448]{1,0:T(8,128)(2,1)S(1)} collective-permute-done((bf16[8,8448]{1,0:T(8,128)(2,1)S(1)}, bf16[8,8448]{1,0:T(8,128)(2,1)S(1)}, u32[]{:S(2)}, u32[]{:S(2)}) %collective-permute-start.2) | collective-permute-done | bytes 135200 | tf_op jit(solution)/shard_map/ppermute | solution.py:182
  16.3 1.9 %collective-permute-start.3 = (bf16[8,8448]{1,0:T(8,128)(2,1)S(1)}, bf16[8,8448]{1,0:T(8,128)(2,1)S(1)}, u32[]{:S(2)}, u32[]{:S(2)}) collective-permute-start(bf16[8,8448]{1,0:T(8,128)(2,1)S(1)} %broadcast_select_fusion.1), channel_id=1, source_target_pairs={{0,4},{1,5},{2,6},{3,7},{4,0},{5,1},{6,2},{7,3},{8,12},{9,13},{10,... | collective-permute-start | bytes 405512 | tf_op jit(solution)/shard_map/ppermute | solution.py:182
  18.2 3.6 %collective-permute-done.3 = bf16[8,8448]{1,0:T(8,128)(2,1)S(1)} collective-permute-done((bf16[8,8448]{1,0:T(8,128)(2,1)S(1)}, bf16[8,8448]{1,0:T(8,128)(2,1)S(1)}, u32[]{:S(2)}, u32[]{:S(2)}) %collective-permute-start.3) | collective-permute-done | bytes 135200 | tf_op jit(solution)/shard_map/ppermute | solution.py:182
  21.8 2.7 %collective-permute-start.4 = (bf16[8,8448]{1,0:T(8,128)(2,1)S(1)}, bf16[8,8448]{1,0:T(8,128)(2,1)S(1)}, u32[]{:S(2)}, u32[]{:S(2)}) collective-permute-start(bf16[8,8448]{1,0:T(8,128)(2,1)S(1)} %broadcast_select_fusion.2), channel_id=1, source_target_pairs={{0,8},{1,9},{2,10},{3,11},{4,12},{5,13},{6,14},{7,15},{8,0},{9,1},... | collective-permute-start | bytes 405512 | tf_op jit(solution)/shard_map/ppermute | solution.py:182
  24.4 5.7 %collective-permute-done.4 = bf16[8,8448]{1,0:T(8,128)(2,1)S(1)} collective-permute-done((bf16[8,8448]{1,0:T(8,128)(2,1)S(1)}, bf16[8,8448]{1,0:T(8,128)(2,1)S(1)}, u32[]{:S(2)}, u32[]{:S(2)}) %collective-permute-start.4) | collective-permute-done | bytes 135200 | tf_op jit(solution)/shard_map/ppermute | solution.py:182
  30.2 0.0 copy-done.1
  30.2 0.0 copy-done
  30.2 0.0 copy-done.2
  30.2 0.0 copy-start.3
  30.3 1.0 %copy-done.3 = bf16[768,256]{1,0:T(8,128)(2,1)S(1)} copy-done((bf16[768,256]{1,0:T(8,128)(2,1)S(1)}, bf16[768,256]{1,0:T(8,128)(2,1)}, u32[]{:S(2)}) %copy-start.3) | copy-done | bytes 393240
  31.2 0.0 copy-start.4
  31.3 1.0 %copy-done.4 = bf16[384,384]{1,0:T(8,128)(2,1)S(1)} copy-done((bf16[384,384]{1,0:T(8,128)(2,1)S(1)}, bf16[384,384]{1,0:T(8,128)(2,1)}, u32[]{:S(2)}) %copy-start.4) | copy-done | bytes 294936
  32.2 0.0 copy-start.5
  32.2 0.9 %copy-done.5 = bf16[512,256]{1,0:T(8,128)(2,1)S(1)} copy-done((bf16[512,256]{1,0:T(8,128)(2,1)S(1)}, bf16[512,256]{1,0:T(8,128)(2,1)}, u32[]{:S(2)}) %copy-start.5) | copy-done | bytes 262168
  33.2 3.2 %shard_map.91 = f32[8,8,256]{2,1,0:T(8,128)} custom-call(bf16[8,4224]{1,0:T(8,128)(2,1)S(1)} %get-tuple-element.8.own0, bf16[8,4224]{1,0:T(8,128)(2,1)S(1)} %get-tuple-element.7.own1, bf16[8,4224]{1,0:T(8,128)(2,1)S(1)} %get-tuple-element.6.src0, bf16[8,4224]{1,0:T(8,128)(2,1)S(1)} %get-tuple-element.5.src1, bf16[512,512]{1,0:T(8,128)(2,1)S(1)} %copy-done.1, ...), custom_call_target="tpu_custom_call" | custom-call | tf_op jit(solution)/shard_map/pallas_call | solution.py:161
  (6 shorter events, 0.1 us)
Async XLA Ops:
  0.0 30.2 %copy-start.1 = (bf16[512,512]{1,0:T(8,128)(2,1)S(1)}, bf16[512,512]{1,0:T(8,128)(2,1)}, u32[]{:S(2)}) copy-start(bf16[512,512]{1,0:T(8,128)(2,1)} %constant.35.clone.taps) | copy-start | bytes 1572868
  0.0 30.2 %copy-start = (bf16[1024,768]{1,0:T(8,128)(2,1)S(1)}, bf16[1024,768]{1,0:T(8,128)(2,1)}, u32[]{:S(2)}) copy-start(bf16[1024,768]{1,0:T(8,128)(2,1)} %constant.37.clone.table) | copy-start | bytes 4718596
  0.0 30.2 %copy-start.2 = (bf16[768,256]{1,0:T(8,128)(2,1)S(1)}, bf16[768,256]{1,0:T(8,128)(2,1)}, u32[]{:S(2)}) copy-start(bf16[768,256]{1,0:T(8,128)(2,1)} %constant.39.clone.lag_high) | copy-start | bytes 1179652
  1.8 5.2 %collective-permute-start = (bf16[8,4224]{1,0:T(8,128)(2,1)S(1)}, bf16[8,4224]{1,0:T(8,128)(2,1)S(1)}, u32[]{:S(2)}, u32[]{:S(2)}) collective-permute-start(bf16[8,4224]{1,0:T(8,128)(2,1)S(1)} %fusion.1), channel_id=1, source_target_pairs={{0,16},{16,0},{1,17},{17,1},{2,18},{18,2},{3,19},{19,3},{4,20},{20... | collective-permute-start | bytes 202760 | tf_op jit(solution)/shard_map/ppermute | solution.py:177
  7.9 2.0 %collective-permute-start.1 = (bf16[8,8448]{1,0:T(8,128)(2,1)S(1)}, bf16[8,8448]{1,0:T(8,128)(2,1)S(1)}, u32[]{:S(2)}, u32[]{:S(2)}) collective-permute-start(bf16[8,8448]{1,0:T(8,128)(2,1)S(1)} %pad_maximum_fusion), channel_id=1, source_target_pairs={{0,1},{1,0},{2,3},{3,2},{4,5},{5,4},{6,7},{7,6},{8,9},{9,8},{10,11... | collective-permute-start | bytes 405512 | tf_op jit(solution)/shard_map/ppermute | solution.py:182
  9.9 6.4 %collective-permute-start.2 = (bf16[8,8448]{1,0:T(8,128)(2,1)S(1)}, bf16[8,8448]{1,0:T(8,128)(2,1)S(1)}, u32[]{:S(2)}, u32[]{:S(2)}) collective-permute-start(bf16[8,8448]{1,0:T(8,128)(2,1)S(1)} %broadcast_select_fusion), channel_id=1, source_target_pairs={{0,2},{1,3},{2,0},{3,1},{4,6},{5,7},{6,4},{7,5},{8,10},{9,11},{10,... | collective-permute-start | bytes 405512 | tf_op jit(solution)/shard_map/ppermute | solution.py:182
  16.3 5.5 %collective-permute-start.3 = (bf16[8,8448]{1,0:T(8,128)(2,1)S(1)}, bf16[8,8448]{1,0:T(8,128)(2,1)S(1)}, u32[]{:S(2)}, u32[]{:S(2)}) collective-permute-start(bf16[8,8448]{1,0:T(8,128)(2,1)S(1)} %broadcast_select_fusion.1), channel_id=1, source_target_pairs={{0,4},{1,5},{2,6},{3,7},{4,0},{5,1},{6,2},{7,3},{8,12},{9,13},{10,... | collective-permute-start | bytes 405512 | tf_op jit(solution)/shard_map/ppermute | solution.py:182
  21.8 8.4 %collective-permute-start.4 = (bf16[8,8448]{1,0:T(8,128)(2,1)S(1)}, bf16[8,8448]{1,0:T(8,128)(2,1)S(1)}, u32[]{:S(2)}, u32[]{:S(2)}) collective-permute-start(bf16[8,8448]{1,0:T(8,128)(2,1)S(1)} %broadcast_select_fusion.2), channel_id=1, source_target_pairs={{0,8},{1,9},{2,10},{3,11},{4,12},{5,13},{6,14},{7,15},{8,0},{9,1},... | collective-permute-start | bytes 405512 | tf_op jit(solution)/shard_map/ppermute | solution.py:182
  30.2 1.0 %copy-start.3 = (bf16[768,256]{1,0:T(8,128)(2,1)S(1)}, bf16[768,256]{1,0:T(8,128)(2,1)}, u32[]{:S(2)}) copy-start(bf16[768,256]{1,0:T(8,128)(2,1)} %constant.40.clone.lag_low) | copy-start | bytes 1179652
  31.2 1.0 %copy-start.4 = (bf16[384,384]{1,0:T(8,128)(2,1)S(1)}, bf16[384,384]{1,0:T(8,128)(2,1)}, u32[]{:S(2)}) copy-start(bf16[384,384]{1,0:T(8,128)(2,1)} %constant.38.clone.smooth) | copy-start | bytes 884740
  32.2 0.9 %copy-start.5 = (bf16[512,256]{1,0:T(8,128)(2,1)S(1)}, bf16[512,256]{1,0:T(8,128)(2,1)}, u32[]{:S(2)}) copy-start(bf16[512,256]{1,0:T(8,128)(2,1)} %constant.36.clone.mean) | copy-start | bytes 786436
where the time goes:
time: 36.7 us; the launch traced here: 36.4 us
  waiting for transfers between devices  15.8 us (43%)
  starting transfers between devices  9.66 us (26%)
  local copies, waits for them, and re-layouts  4.26 us (12%)
  Pallas kernels  3.2 us (9%)
  other arithmetic  2.66 us (7%)
  between operations  0.74 us (2%)
    ppermute x4, waiting for transfers between devices, shards(): got = lax.ppermute(held, 'blk', [(i, i ^ step) for i in range(blocks)])  13.6 us
    ppermute x4, starting transfers between devices, shards(): got = lax.ppermute(held, 'blk', [(i, i ^ step) for i in range(blocks)])  6.72 us
    pallas_call x1, Pallas kernels, correlate(): pl.pallas_call(kernel, out_shape=jax.ShapeDtypeStruct((ST, ST, LAGS), F32...  3.2 us
    ppermute x1, starting transfers between devices, shards(): other = lax.ppermute(mine, 'section', [(0, 1), (1, 0)])  2.94 us
    unnamed x12, local copies, waits for them, and re-layouts  2.91 us
    ppermute x1, waiting for transfers between devices, shards(): other = lax.ppermute(mine, 'section', [(0, 1), (1, 0)])  2.26 us
    dynamic_slice x1, local copies, waits for them, and re-layouts, shards(): root = block_order[section]  1.24 us
    select_n x1, other arithmetic, shards(): jnp.where(section == 0, other, mine)  0.87 us
  transfers between devices with their start and end apart: 5, of which 4 were waited for; matrix products, arithmetic and copies ran while one was open for 3% of the time, Pallas kernels for 0%

commit v1 on v0

v1 whole, which is shorter than its diff:
```python
import math

import jax
import jax.numpy as jnp
import numpy as np
from jax import lax
from jax.experimental import pallas as pl
from jax.experimental.pallas import tpu as pltpu
from jax.sharding import PartitionSpec as P

L = 1024
NF = 384
BIN_LO = 8
LAGS = 256
TAPS = 33
HW = 50
WF = 32
ST = 8
SEGS = 8
BLK = 256
ROWS = SEGS * L // BLK
PAD = 128
LANES = 128

F32 = jnp.float32
BF16 = jnp.bfloat16


def halves(table):
    high = table.astype(BF16)
    low = (table - high.astype(np.float64)).astype(BF16)
    return high, low


def filter_table():
    k = np.arange(TAPS, dtype=np.float64) - (TAPS - 1) // 2
    low, high = BIN_LO / L, (BIN_LO + NF) / L
    window = 0.5 + 0.5 * np.cos(2.0 * math.pi * k / (TAPS + 1))
    taps = window * (2 * high * np.sinc(2 * high * k) - 2 * low * np.sinc(2 * low * k))
    shift = BLK // 2 + np.arange(BLK)[None, :] - np.arange(2 * BLK)[:, None] + (TAPS - 1) // 2
    inside = (shift >= 0) & (shift < TAPS)
    table = np.where(inside, taps[np.clip(shift, 0, TAPS - 1)], 0.0)
    return np.concatenate(halves(table), axis=1)


def mean_table():
    shift = BLK // 2 + np.arange(BLK)[None, :] - np.arange(2 * BLK)[:, None]
    return (np.abs(shift) <= HW).astype(BF16)


def smooth_table():
    bins = np.arange(NF)
    return (np.abs(bins[:, None] - bins[None, :]) <= WF).astype(BF16)


def forward_table():
    phase = np.mod(np.arange(L)[:, None] * (BIN_LO + np.arange(NF))[None, :], L) * (2.0 * math.pi / L)
    return np.concatenate([np.cos(phase), -np.sin(phase)], axis=1).astype(BF16)


def lag_table():
    shifts = np.arange(LAGS)[None, :] - LAGS // 2
    phase = np.mod((BIN_LO + np.arange(NF))[:, None] * shifts, L) * (2.0 * math.pi / L)
    table = np.concatenate([np.cos(phase), -np.sin(phase)], axis=0) / math.sqrt(NF)
    return halves(table)


def dot(a, b):
    return jnp.dot(a, b, preferred_element_type=F32)


def split(a):
    high = a.astype(BF16)
    return high, (a - high.astype(F32)).astype(BF16)


def spread(parts):
    rows = []
    for part in parts:
        half = part.shape[1] - PAD
        rows += [part[:, i * BLK : (i + 1) * BLK].astype(F32) for i in range(half // BLK)]
    return rows


def mask_rows(parts):
    per = (parts[0].shape[1] - PAD) // L
    return jnp.concatenate([p[:, p.shape[1] - PAD :].astype(F32)[:per] for p in parts], axis=0)


def mask_column(mask):
    diagonal = lax.broadcasted_iota(jnp.int32, (ST, LANES), 0) == lax.broadcasted_iota(
        jnp.int32, (ST, LANES), 1
    )
    tiles = [jnp.where(diagonal, mask[g : g + 1], 0.0) for g in range(SEGS)]
    return jnp.sum(jnp.concatenate(tiles, axis=0), axis=1, keepdims=True)


def whitened(parts, column, table):
    zero = jnp.zeros((2 * ST, BLK), F32)
    x = jnp.concatenate([zero, *spread(parts), zero], axis=0)
    n = x.shape[0]
    half = BLK // 2
    window = jnp.concatenate(
        [x[: n - 2 * ST, half:], x[ST : n - ST], x[2 * ST :, :half]], axis=1
    ).astype(BF16)
    both = dot(window, table(0))
    filtered = both[:, :BLK] + both[:, BLK:]
    m = filtered.shape[0]
    size = jnp.abs(filtered)
    window = jnp.concatenate(
        [size[: m - 2 * ST, half:], size[ST : m - ST], size[2 * ST :, :half]], axis=1
    )
    high, low = split(window)
    mean = table(1)
    total = dot(high, mean) + dot(low, mean)
    normal = filtered[ST : m - ST] / (total * (1.0 / (2 * HW + 1)) + 1e-06)
    per = L // BLK
    normal = normal.reshape(SEGS, per, ST, BLK)
    framed = jnp.concatenate([normal[:, q].reshape(SEGS * ST, BLK) for q in range(per)], axis=1)
    spectra = dot(framed.astype(BF16), table(2))
    real, imag = spectra[:, :NF], spectra[:, NF:]
    amplitude = jnp.sqrt(real * real + imag * imag)
    high, low = split(amplitude)
    smooth = table(3)
    smoothed = dot(high, smooth) + dot(low, smooth)
    factor = column / (smoothed * (1.0 / (2 * WF + 1)) + 1e-06)
    return jnp.concatenate([real * factor, imag * factor], axis=1).astype(BF16)


def pack(raw, mask, order, mine, wanted, carried, order_here, mask_here, sems):
    half = raw.shape[1]
    away = (wanted, carried)
    copies = [
        pltpu.make_async_copy(order, order_here, sems.at[0]),
        pltpu.make_async_copy(mask, mask_here, sems.at[1]),
        pltpu.make_async_copy(raw, mine.at[:, pl.ds(0, half)], sems.at[2]),
    ]
    for copy in copies:
        copy.start()
    mine[:, half:] = jnp.zeros((ST, PAD), BF16)
    me = lax.axis_index("blk")
    copies[0].wait()
    for i, source in enumerate((lax.axis_index("section"), me & 1)):
        away[i][...] = jnp.full(away[i].shape, order_here[source] ^ me, jnp.int32)
    copies[1].wait()
    segs, stations = mask.shape
    mine[:segs, half : half + stations] = mask_here[...].astype(F32).astype(BF16)
    copies[2].wait()


def ordered(swap, one, two):
    one, two = one[...], two[...]
    return jnp.where(swap == 0, one, two), jnp.where(swap == 0, two, one)


def receivers(mine, other, *refs):
    tables, (white, masks, *held, sems) = refs[:6], refs[6:]
    copies = [pltpu.make_async_copy(t, h, sems.at[i]) for i, (t, h) in enumerate(zip(tables, held))]
    for copy in copies:
        copy.start()
    parts = ordered(lax.axis_index("section"), mine, other)
    column = mask_column(mask_rows(parts))
    masks[...] = jnp.broadcast_to(column, masks.shape)

    def table(i):
        copies[i].wait()
        return held[i][...]

    white[...] = whitened(parts, column, table)
    copies[4].wait()
    copies[5].wait()


def correlate(held, twin, white, masks, *refs):
    tables, out = refs[:-1], refs[-1]
    parts = ordered(lax.axis_index("blk") & 1, held, twin)
    sent_mask = mask_rows(parts)
    column = mask_column(sent_mask)
    sent = whitened(parts, column, lambda i: tables[i][...]).astype(F32)
    lag_high, lag_low = tables[4:]
    recv = white[...].astype(F32)
    size = SEGS * ST
    common = sum(masks[g * ST : (g + 1) * ST] * sent_mask[g : g + 1] for g in range(SEGS))
    rows, counts = [], []
    for n in range(ST):
        real = jnp.zeros((ST, NF), F32)
        imag = jnp.zeros((ST, NF), F32)
        for g in range(SEGS):
            line = sent[g * ST + n : g * ST + n + 1]
            tile = recv[g * ST : (g + 1) * ST]
            sr, si = line[:, :NF], line[:, NF:]
            rr, ri = tile[:, :NF], tile[:, NF:]
            real += rr * sr + ri * si
            imag += ri * sr - rr * si
        rows.append(jnp.concatenate([real, imag], axis=1))
        counts.append(common[:, n : n + 1])
    high, low = split(jnp.concatenate(rows, axis=0))
    both = dot(jnp.concatenate([high, low], axis=0), lag_high[...])
    lagged = both[:size] + both[size:] + dot(high, lag_low[...])
    lagged = lagged / jnp.maximum(jnp.concatenate(counts, axis=0), 1.0)
    out[...] = lagged.reshape(ST, ST, LAGS)


VMEM = pl.BlockSpec(memory_space=pltpu.VMEM)
HBM = pl.BlockSpec(memory_space=pltpu.HBM)


def call(body, out_shape, in_specs, arrays, scratch=(), flops=0):
    size = sum(a.size * a.dtype.itemsize for a in arrays)
    arrays = [
        pltpu.with_memory_space_constraint(a, pltpu.HBM) if spec is HBM else a
        for a, spec in zip(arrays, in_specs)
    ]
    return pl.pallas_call(
        body,
        out_shape=out_shape,
        in_specs=in_specs,
        out_specs=jax.tree.map(lambda _: VMEM, out_shape),
        scratch_shapes=scratch,
        cost_estimate=pl.CostEstimate(flops=flops, bytes_accessed=size, transcendentals=0),
        compiler_params=pltpu.CompilerParams(vmem_limit_bytes=16 * 1024 * 1024),
    )(*arrays)


def shaped(*shape, dtype=BF16):
    return jax.ShapeDtypeStruct(shape, dtype)


def exchange(x, flip, axis="blk"):
    devices = lax.axis_size(axis)
    return lax.ppermute(x, axis, [(i, i ^ flip) for i in range(devices)])


def crossing(x, bit):
    axes = ("section", "blk")
    blocks = lax.axis_size("blk")
    near, far = [], []
    for s in range(2):
        for b in range(blocks):
            here = s * blocks + b
            if s == b % 2:
                near.append((here, s * blocks + (b ^ bit)))
            else:
                there = (1 - s) * blocks
                near.append((here, there + (b ^ 1)))
                far.append((here, there + (b ^ 1 ^ bit)))
    return lax.ppermute(x, axes, near), lax.ppermute(x, axes, far)


def shards(raw_traces, valid_mask, block_order):
    section = lax.axis_index("section")
    blocks = lax.axis_size("blk")
    me = lax.axis_index("blk")
    core = me & 1
    half = raw_traces.shape[1]
    width = half + PAD
    mine, away_wanted, away_carried = call(
        pack,
        [shaped(ST, width)] + [shaped(ST, width, dtype=jnp.int32)] * 2,
        [HBM] * 3,
        [raw_traces, valid_mask.T, block_order],
        [
            pltpu.SMEM(block_order.shape, jnp.int32),
            pltpu.VMEM(valid_mask.shape[::-1], jnp.int32),
            pltpu.SemaphoreType.DMA((3,)),
        ],
    )

    twin = exchange(mine, 1)
    held = jnp.where(away_carried & 1 == 0, mine, twin)
    bits = [1 << i for i in range(1, blocks.bit_length() - 1)]
    last = bits.pop()
    other = None
    while bits:
        flips, bits = bits[:2], bits[2:]
        low, steps = flips[0], 1 << len(flips)
        got = [exchange(held, low * k) for k in range(1, steps)]
        if other is None:
            other = exchange(mine, 1, "section")
        rel = away_carried & (low * (steps - 1))
        for k in range(1, steps):
            held = jnp.where(rel == low * k, got[k - 1], held)
    tables = [filter_table(), mean_table(), forward_table(), smooth_table(), *lag_table()]
    tables = [jnp.asarray(t) for t in tables]
    held, other = lax.optimization_barrier((held, other))
    near, far = crossing(held, last)
    white, masks, *tables = call(
        receivers,
        [shaped(SEGS * ST, 2 * NF), shaped(SEGS * ST, LANES, dtype=F32)]
        + [shaped(*t.shape) for t in tables],
        [VMEM] * 2 + [HBM] * len(tables),
        [mine, other, *tables],
        [pltpu.SemaphoreType.DMA((len(tables),))],
        flops=10**9,
    )
    near, far, white, masks = lax.optimization_barrier((near, far, white, masks))
    same = away_wanted & last == 0
    held = jnp.where(core == section, jnp.where(same, held, near), jnp.where(same, near, far))
    twin = exchange(held, 1)
    return call(
        correlate,
        shaped(ST, ST, LAGS, dtype=F32),
        [VMEM] * 10,
        [held, twin, white, masks, *tables],
        flops=10**9,
    )


def solution(mesh):
    return jax.shard_map(
        shards,
        mesh=mesh,
        in_specs=(P("blk", "section"), P("blk", "section"), P()),
        out_specs=P("section", "blk", None),
        check_vma=False,
    )
```

time: 36.7 us -> 24.3 us (0.66)
  waiting for transfers between devices: 15.8 us -> 4.23 us
  local copies, waits for them, and re-layouts: 4.26 us -> 0 us
  starting transfers between devices: 9.66 us -> 13.5 us
  Pallas kernels: 3.2 us -> 6.18 us
  other arithmetic: 2.66 us -> 0.15 us
  between operations: 0.74 us -> 0.06 us
    ppermute x5 -> x8, waiting for transfers between devices: 15.8 us -> 4.23 us  [the longest x6 4.23 us: exchange(): return lax.ppermute(x, axis, [(i, i ^ flip) for i in range(devices)])]
    ppermute x5 -> x8, starting transfers between devices: 9.66 us -> 13.5 us  [the longest x6 9.94 us: exchange(): return lax.ppermute(x, axis, [(i, i ^ flip) for i in range(devices)])]
    pallas_call x1 -> x3, Pallas kernels: 3.2 us -> 6.18 us  [call(): pl.pallas_call(body, out_shape=out_shape, in_specs=in_specs, out_specs=ja...]
    unnamed x12 -> x0, local copies, waits for them, and re-layouts: 2.91 us -> none
    dynamic_slice x1 -> x0, local copies, waits for them, and re-layouts: 1.24 us -> none  [shards(): root = block_order[section]]
    concatenate x2 -> x0, other arithmetic: 0.86 us -> none  [the longest x1 0.84 us: shards(): mine = jnp.concatenate([raw_traces, mask], axis=1)]
    convert_element_type x1 -> x0, other arithmetic: 0.83 us -> none  [shards(): valid_mask.astype(BF16)]
    select_n x5 -> x3, other arithmetic: 0.97 us -> 0.15 us  [the longest x1 0.06 us: shards(): held = jnp.where(rel == low * k, got[k - 1], held)]
  transfers between devices with their start and end apart: 5 -> 8, of which waited for: 4 -> 6; matrix products, arithmetic and copies ran while one was open for 3% -> 0% of each run, Pallas kernels for 0% -> 11%
where the time goes in v1:
time: 24.3 us; the launch traced here: 24.1 us
  starting transfers between devices  13.5 us (56%)
  Pallas kernels  6.18 us (25%)
  waiting for transfers between devices  4.23 us (17%)
    ppermute x6, starting transfers between devices, exchange(): return lax.ppermute(x, axis, [(i, i ^ flip) for i in range(devices)])  9.94 us
    pallas_call x3, Pallas kernels, call(): pl.pallas_call(body, out_shape=out_shape, in_specs=in_specs, out_specs=ja...  6.18 us
    ppermute x6, waiting for transfers between devices, exchange(): return lax.ppermute(x, axis, [(i, i ^ flip) for i in range(devices)])  4.23 us
    ppermute x2, starting transfers between devices, crossing(): return (lax.ppermute(x, axes, near), lax.ppermute(x, axes, far))  3.56 us
  transfers between devices with their start and end apart: 8, of which 6 were waited for; matrix products, arithmetic and copies ran while one was open for 0% of the time, Pallas kernels for 11%

profile of v1, /device:TPU:0, one launch (start us, length us, event | category | flops | bytes accessed | tf_op | source)
XLA Modules:
  0.0 24.1 jit_solution(2096845093096420680)
XLA Ops:
  0.0 0.9 %shard_map.91 = (bf16[8,4224]{1,0:T(8,128)(2,1)S(1)}, s32[8,4224]{1,0:T(8,128)S(1)}, s32[8,4224]{1,0:T(8,128)S(1)}) custom-call(bf16[8,4096]{1,0:T(8,128)(2,1)} %raw.1, s32[4,8]{1,0:T(4,128)} %bitcast.1, s32[16]{0:T(128)} %order.1), custom_call_target="tpu_custom_call" | custom-call | bytes 65728 | tf_op jit(solution)/shard_map/pallas_call | solution.py:214
  0.9 0.5 %collective-permute-start = (bf16[8,4224]{1,0:T(8,128)(2,1)S(1)}, bf16[8,4224]{1,0:T(8,128)(2,1)S(1)}, u32[]{:S(2)}, u32[]{:S(2)}) collective-permute-start(bf16[8,4224]{1,0:T(8,128)(2,1)S(1)} %get-tuple-element.24.mine), channel_id=1, source_target_pairs={{0,1},{1,0},{2,3},{3,2},{4,5},{5,4},{6,7},{7,6},{8,9},{9,8},{10,11... | collective-permute-start | bytes 202760 | tf_op jit(solution)/shard_map/ppermute | solution.py:231
  1.4 0.9 %collective-permute-done = bf16[8,4224]{1,0:T(8,128)(2,1)S(1)} collective-permute-done((bf16[8,4224]{1,0:T(8,128)(2,1)S(1)}, bf16[8,4224]{1,0:T(8,128)(2,1)S(1)}, u32[]{:S(2)}, u32[]{:S(2)}) %collective-permute-start) | collective-permute-done | bytes 67616 | tf_op jit(solution)/shard_map/ppermute | solution.py:231
  2.4 3.9 %collective-permute-start.1 = (bf16[8,4224]{1,0:T(8,128)(2,1)S(1)}, bf16[8,4224]{1,0:T(8,128)(2,1)S(1)}, u32[]{:S(2)}, u32[]{:S(2)}) collective-permute-start(bf16[8,4224]{1,0:T(8,128)(2,1)S(1)} %fusion), channel_id=1, source_target_pairs={{0,6},{1,7},{2,4},{3,5},{4,2},{5,3},{6,0},{7,1},{8,14},{9,15},{10,... | collective-permute-start | bytes 202760 | tf_op jit(solution)/shard_map/ppermute | solution.py:231
  6.3 0.4 %collective-permute-start.2 = (bf16[8,4224]{1,0:T(8,128)(2,1)S(1)}, bf16[8,4224]{1,0:T(8,128)(2,1)S(1)}, u32[]{:S(2)}, u32[]{:S(2)}) collective-permute-start(bf16[8,4224]{1,0:T(8,128)(2,1)S(1)} %fusion), channel_id=1, source_target_pairs={{0,4},{1,5},{2,6},{3,7},{4,0},{5,1},{6,2},{7,3},{8,12},{9,13},{10,... | collective-permute-start | bytes 202760 | tf_op jit(solution)/shard_map/ppermute | solution.py:231
  6.7 0.2 collective-permute-start.3
  6.9 1.8 %collective-permute-start.4 = (bf16[8,4224]{1,0:T(8,128)(2,1)S(1)}, bf16[8,4224]{1,0:T(8,128)(2,1)S(1)}, u32[]{:S(2)}, u32[]{:S(2)}) collective-permute-start(bf16[8,4224]{1,0:T(8,128)(2,1)S(1)} %get-tuple-element.24.mine), channel_id=1, source_target_pairs={{0,16},{16,0},{1,17},{17,1},{2,18},{18,2},{3,19},{19,3},{4,20},{20... | collective-permute-start | bytes 202760 | tf_op jit(solution)/shard_map/ppermute | solution.py:231
  8.7 0.1 collective-permute-done.1
  8.8 1.8 %collective-permute-done.2 = bf16[8,4224]{1,0:T(8,128)(2,1)S(1)} collective-permute-done((bf16[8,4224]{1,0:T(8,128)(2,1)S(1)}, bf16[8,4224]{1,0:T(8,128)(2,1)S(1)}, u32[]{:S(2)}, u32[]{:S(2)}) %collective-permute-start.2) | collective-permute-done | bytes 67616 | tf_op jit(solution)/shard_map/ppermute | solution.py:231
  10.6 0.4 %collective-permute-done.3 = bf16[8,4224]{1,0:T(8,128)(2,1)S(1)} collective-permute-done((bf16[8,4224]{1,0:T(8,128)(2,1)S(1)}, bf16[8,4224]{1,0:T(8,128)(2,1)S(1)}, u32[]{:S(2)}, u32[]{:S(2)}) %collective-permute-start.3) | collective-permute-done | bytes 67616 | tf_op jit(solution)/shard_map/ppermute | solution.py:231
  11.0 0.1 compare_select_fusion.2
  11.1 0.1 collective-permute-done.4.other
  11.2 2.9 %collective-permute-start.5 = (bf16[8,4224]{1,0:T(8,128)(2,1)S(1)}, bf16[8,4224]{1,0:T(8,128)(2,1)S(1)}, u32[]{:S(2)}, u32[]{:S(2)}) collective-permute-start(bf16[8,4224]{1,0:T(8,128)(2,1)S(1)} %compare_select_fusion.2), channel_id=1, source_target_pairs={{0,8},{1,16},{2,10},{3,18},{4,12},{5,20},{6,14},{7,22},{8,0},{9,24... | collective-permute-start | bytes 202760 | tf_op jit(solution)/shard_map/ppermute | solution.py:247
  14.1 0.7 %collective-permute-start.6 = (bf16[8,4224]{1,0:T(8,128)(2,1)S(1)}, bf16[8,4224]{1,0:T(8,128)(2,1)S(1)}, u32[]{:S(2)}, u32[]{:S(2)}) collective-permute-start(bf16[8,4224]{1,0:T(8,128)(2,1)S(1)} %compare_select_fusion.2), channel_id=1, source_target_pairs={{1,24},{3,26},{5,28},{7,30},{9,16},{11,18},{13,20},{15,22},{16,9},... | collective-permute-start | bytes 202760 | tf_op jit(solution)/shard_map/ppermute | solution.py:247
  14.8 2.7 %shard_map.92 = (bf16[64,768]{1,0:T(8,128)(2,1)S(1)}, f32[64,128]{1,0:T(8,128)S(1)}, bf16[512,512]{1,0:T(8,128)(2,1)S(1)}, bf16[512,256]{1,0:T(8,128)(2,1)S(1)},...) custom-call(bf16[8,4224]{1,0:T(8,128)(2,1)S(1)} %get-tuple-element.2, ...), custom_call_target="tpu_custom_call" | custom-call | flops 1000000000 | bytes 3575808 | tf_op jit(solution)/shard_map/pallas_call | solution.py:214
  17.5 0.0 collective-permute-done.5
  17.6 0.0 collective-permute-done.6
  17.6 0.1 select_select_fusion.held
  17.6 3.0 %collective-permute-start.7 = (bf16[8,4224]{1,0:T(8,128)(2,1)S(1)}, bf16[8,4224]{1,0:T(8,128)(2,1)S(1)}, u32[]{:S(2)}, u32[]{:S(2)}) collective-permute-start(bf16[8,4224]{1,0:T(8,128)(2,1)S(1)} %select_select_fusion.held), channel_id=1, source_target_pairs={{0,1},{1,0},{2,3},{3,2},{4,5},{5,4},{6,7},{7,6},{8,9},{9,8},{10,11... | collective-permute-start | bytes 202760 | tf_op jit(solution)/shard_map/ppermute | solution.py:231
  20.7 0.9 %collective-permute-done.7.twin = bf16[8,4224]{1,0:T(8,128)(2,1)S(1)} collective-permute-done((bf16[8,4224]{1,0:T(8,128)(2,1)S(1)}, bf16[8,4224]{1,0:T(8,128)(2,1)S(1)}, u32[]{:S(2)}, u32[]{:S(2)}) %collective-permute-start.7) | collective-permute-done | bytes 67616 | tf_op jit(solution)/shard_map/ppermute | solution.py:231
  21.6 2.6 %shard_map.93 = f32[8,8,256]{2,1,0:T(8,128)} custom-call(bf16[8,4224]{1,0:T(8,128)(2,1)S(1)} %select_select_fusion.held, bf16[8,4224]{1,0:T(8,128)(2,1)S(1)} %collective-permute-done.7.twin, bf16[64,768]{1,0:T(8,128)(2,1)S(1)} %get-tuple-element.31.white, f32[64,128]{1,0:T(8,128)S(1)} %get-tuple-element.32.masks, ...), custom_call_target="tpu_custom_call" | custom-call | flops 1000000000 | bytes 3706880 | tf_op jit(solution)/shard_map/pallas_call | solution.py:214
  (1 shorter events, 0.0 us)
Async XLA Ops:
  0.9 1.4 %collective-permute-start = (bf16[8,4224]{1,0:T(8,128)(2,1)S(1)}, bf16[8,4224]{1,0:T(8,128)(2,1)S(1)}, u32[]{:S(2)}, u32[]{:S(2)}) collective-permute-start(bf16[8,4224]{1,0:T(8,128)(2,1)S(1)} %get-tuple-element.24.mine), channel_id=1, source_target_pairs={{0,1},{1,0},{2,3},{3,2},{4,5},{5,4},{6,7},{7,6},{8,9},{9,8},{10,11... | collective-permute-start | bytes 202760 | tf_op jit(solution)/shard_map/ppermute | solution.py:231
  2.4 6.5 %collective-permute-start.1 = (bf16[8,4224]{1,0:T(8,128)(2,1)S(1)}, bf16[8,4224]{1,0:T(8,128)(2,1)S(1)}, u32[]{:S(2)}, u32[]{:S(2)}) collective-permute-start(bf16[8,4224]{1,0:T(8,128)(2,1)S(1)} %fusion), channel_id=1, source_target_pairs={{0,6},{1,7},{2,4},{3,5},{4,2},{5,3},{6,0},{7,1},{8,14},{9,15},{10,... | collective-permute-start | bytes 202760 | tf_op jit(solution)/shard_map/ppermute | solution.py:231
  6.3 4.3 %collective-permute-start.2 = (bf16[8,4224]{1,0:T(8,128)(2,1)S(1)}, bf16[8,4224]{1,0:T(8,128)(2,1)S(1)}, u32[]{:S(2)}, u32[]{:S(2)}) collective-permute-start(bf16[8,4224]{1,0:T(8,128)(2,1)S(1)} %fusion), channel_id=1, source_target_pairs={{0,4},{1,5},{2,6},{3,7},{4,0},{5,1},{6,2},{7,3},{8,12},{9,13},{10,... | collective-permute-start | bytes 202760 | tf_op jit(solution)/shard_map/ppermute | solution.py:231
  6.7 4.3 %collective-permute-start.3 = (bf16[8,4224]{1,0:T(8,128)(2,1)S(1)}, bf16[8,4224]{1,0:T(8,128)(2,1)S(1)}, u32[]{:S(2)}, u32[]{:S(2)}) collective-permute-start(bf16[8,4224]{1,0:T(8,128)(2,1)S(1)} %fusion), channel_id=1, source_target_pairs={{0,2},{1,3},{2,0},{3,1},{4,6},{5,7},{6,4},{7,5},{8,10},{9,11},{10,... | collective-permute-start | bytes 202760 | tf_op jit(solution)/shard_map/ppermute | solution.py:231
  6.9 4.3 %collective-permute-start.4 = (bf16[8,4224]{1,0:T(8,128)(2,1)S(1)}, bf16[8,4224]{1,0:T(8,128)(2,1)S(1)}, u32[]{:S(2)}, u32[]{:S(2)}) collective-permute-start(bf16[8,4224]{1,0:T(8,128)(2,1)S(1)} %get-tuple-element.24.mine), channel_id=1, source_target_pairs={{0,16},{16,0},{1,17},{17,1},{2,18},{18,2},{3,19},{19,3},{4,20},{20... | collective-permute-start | bytes 202760 | tf_op jit(solution)/shard_map/ppermute | solution.py:231
  11.2 6.3 %collective-permute-start.5 = (bf16[8,4224]{1,0:T(8,128)(2,1)S(1)}, bf16[8,4224]{1,0:T(8,128)(2,1)S(1)}, u32[]{:S(2)}, u32[]{:S(2)}) collective-permute-start(bf16[8,4224]{1,0:T(8,128)(2,1)S(1)} %compare_select_fusion.2), channel_id=1, source_target_pairs={{0,8},{1,16},{2,10},{3,18},{4,12},{5,20},{6,14},{7,22},{8,0},{9,24... | collective-permute-start | bytes 202760 | tf_op jit(solution)/shard_map/ppermute | solution.py:247
  14.1 3.4 %collective-permute-start.6 = (bf16[8,4224]{1,0:T(8,128)(2,1)S(1)}, bf16[8,4224]{1,0:T(8,128)(2,1)S(1)}, u32[]{:S(2)}, u32[]{:S(2)}) collective-permute-start(bf16[8,4224]{1,0:T(8,128)(2,1)S(1)} %compare_select_fusion.2), channel_id=1, source_target_pairs={{1,24},{3,26},{5,28},{7,30},{9,16},{11,18},{13,20},{15,22},{16,9},... | collective-permute-start | bytes 202760 | tf_op jit(solution)/shard_map/ppermute | solution.py:247
  17.6 3.9 %collective-permute-start.7 = (bf16[8,4224]{1,0:T(8,128)(2,1)S(1)}, bf16[8,4224]{1,0:T(8,128)(2,1)S(1)}, u32[]{:S(2)}, u32[]{:S(2)}) collective-permute-start(bf16[8,4224]{1,0:T(8,128)(2,1)S(1)} %select_select_fusion.held), channel_id=1, source_target_pairs={{0,1},{1,0},{2,3},{3,2},{4,5},{5,4},{6,7},{7,6},{8,9},{9,8},{10,11... | collective-permute-start | bytes 202760 | tf_op jit(solution)/shard_map/ppermute | solution.py:231

commit v2 on v1

--- a/solution.py
+++ b/solution.py
@@ -54,7 +54,7 @@
 
 
 def forward_table():
-    phase = np.mod(np.arange(L)[:, None] * (BIN_LO + np.arange(NF))[None, :], L) * (2.0 * math.pi / L)
+    phase = np.mod(np.arange(BLK)[:, None] * (BIN_LO + np.arange(NF))[None, :], L) * (2.0 * math.pi / L)
     return np.concatenate([np.cos(phase), -np.sin(phase)], axis=1).astype(BF16)
 
 
@@ -93,6 +93,19 @@
     )
     tiles = [jnp.where(diagonal, mask[g : g + 1], 0.0) for g in range(SEGS)]
     return jnp.sum(jnp.concatenate(tiles, axis=0), axis=1, keepdims=True)
+
+
+def quarters(parts):
+    parts = parts.reshape(SEGS, L // BLK, ST, 2 * NF)
+    q0, q1, q2, q3 = (parts[:, q].reshape(SEGS * ST, 2 * NF) for q in range(L // BLK))
+    turn = (BIN_LO + lax.broadcasted_iota(jnp.int32, (1, 2 * NF), 1)) % 4
+    even = turn % 2 == 0
+    here = jnp.where(even, q0 + q2, q0 - q2)
+    there = jnp.where(even, q1 + q3, q1 - q3)
+    there = jnp.where(turn >= 2, -there, there)
+    real, imag = there[:, :NF], there[:, NF:]
+    even = even[:, :NF]
+    return here[:, :NF] + jnp.where(even, real, imag), here[:, NF:] + jnp.where(even, imag, -real)
 
 
 def whitened(parts, column, table):
@@ -114,15 +127,11 @@
     mean = table(1)
     total = dot(high, mean) + dot(low, mean)
     normal = filtered[ST : m - ST] / (total * (1.0 / (2 * HW + 1)) + 1e-06)
-    per = L // BLK
-    normal = normal.reshape(SEGS, per, ST, BLK)
-    framed = jnp.concatenate([normal[:, q].reshape(SEGS * ST, BLK) for q in range(per)], axis=1)
-    spectra = dot(framed.astype(BF16), table(2))
-    real, imag = spectra[:, :NF], spectra[:, NF:]
+    real, imag = quarters(dot(normal.astype(BF16), table(2)))
     amplitude = jnp.sqrt(real * real + imag * imag)
     high, low = split(amplitude)
-    smooth = table(3)
-    smoothed = dot(high, smooth) + dot(low, smooth)
+    both = dot(jnp.concatenate([high, low], axis=0), table(3))
+    smoothed = both[: SEGS * ST] + both[SEGS * ST :]
     factor = column / (smoothed * (1.0 / (2 * WF + 1)) + 1e-06)
     return jnp.concatenate([real * factor, imag * factor], axis=1).astype(BF16)
 
@@ -266,7 +275,11 @@
         ],
     )
 
-    twin = exchange(mine, 1)
+    raw_twin, mask_twin = exchange(raw_traces, 1), exchange(valid_mask.T, 1)
+    raw_twin, mask_twin, mine, away_wanted, away_carried = lax.optimization_barrier((raw_twin, mask_twin, mine, away_wanted, away_carried))
+    twin = lax.pad(raw_twin, jnp.zeros((), BF16), ((0, 0, 0), (0, PAD, 0)))
+    rest = ((0, ST - valid_mask.shape[1], 0), (half, PAD - ST, 0))
+    twin += lax.pad(mask_twin.astype(BF16), jnp.zeros((), BF16), rest)
     held = jnp.where(away_carried & 1 == 0, mine, twin)
     bits = [1 << i for i in range(1, blocks.bit_length() - 1)]
     last = bits.pop()
@@ -282,7 +295,6 @@
             held = jnp.where(rel == low * k, got[k - 1], held)
     tables = [filter_table(), mean_table(), forward_table(), smooth_table(), *lag_table()]
     tables = [jnp.asarray(t) for t in tables]
-    held, other = lax.optimization_barrier((held, other))
     near, far = crossing(held, last)
     white, masks, *tables = call(
         receivers,

time: 24.3 us -> 23 us (0.947)
  waiting for transfers between devices: 4.23 us -> 3.62 us
  Pallas kernels: 6.18 us -> 5.76 us
  starting transfers between devices: 13.5 us -> 13.2 us
    ppermute x6 -> x7, waiting for transfers between devices: 4.23 us -> 3.62 us  [exchange(): return lax.ppermute(x, axis, [(i, i ^ flip) for i in range(devices)])]
    pallas_call x3, Pallas kernels: 6.18 us -> 5.76 us  [call(): pl.pallas_call(body, out_shape=out_shape, in_specs=in_specs, out_specs=ja...]
    ppermute x2, starting transfers between devices: 3.56 us -> 3.31 us  [crossing(): return (lax.ppermute(x, axes, near), lax.ppermute(x, axes, far))]
    ppermute x6 -> x7, starting transfers between devices: 9.94 us -> 9.94 us  [exchange(): return lax.ppermute(x, axis, [(i, i ^ flip) for i in range(devices)])]
  transfers between devices with their start and end apart: 8 -> 9, of which waited for: 6 -> 5; matrix products, arithmetic and copies ran while one was open for 0% -> 0% of each run, Pallas kernels for 11% -> 15%
where the time goes in v2:
time: 23 us; the launch traced here: 22.8 us
  starting transfers between devices  13.2 us (57%)
  Pallas kernels  5.76 us (25%)
  waiting for transfers between devices  3.62 us (16%)
    ppermute x7, starting transfers between devices, exchange(): return lax.ppermute(x, axis, [(i, i ^ flip) for i in range(devices)])  9.94 us
    pallas_call x3, Pallas kernels, call(): pl.pallas_call(body, out_shape=out_shape, in_specs=in_specs, out_specs=ja...  5.76 us
    ppermute x7, waiting for transfers between devices, exchange(): return lax.ppermute(x, axis, [(i, i ^ flip) for i in range(devices)])  3.62 us
    ppermute x2, starting transfers between devices, crossing(): return (lax.ppermute(x, axes, near), lax.ppermute(x, axes, far))  3.31 us
  transfers between devices with their start and end apart: 9, of which 5 were waited for; matrix products, arithmetic and copies ran while one was open for 0% of the time, Pallas kernels for 15%

profile of v2, /device:TPU:0, one launch (start us, length us, event | category | flops | bytes accessed | tf_op | source)
XLA Modules:
  0.0 22.8 jit_solution(6890692519392527235)
XLA Ops:
  0.0 0.5 %collective-permute-start = (bf16[8,4096]{1,0:T(8,128)(2,1)}, bf16[8,4096]{1,0:T(8,128)(2,1)S(1)}, u32[]{:S(2)}, u32[]{:S(2)}) collective-permute-start(bf16[8,4096]{1,0:T(8,128)(2,1)} %raw.1), channel_id=1, source_target_pairs={{0,1},{1,0},{2,3},{3,2},{4,5},{5,4},{6,7},{7,6},{8,9},{9,8},{10,11... | collective-permute-start | bytes 196616 | tf_op jit(solution)/shard_map/ppermute | solution.py:240
  0.5 0.1 collective-permute-start.1
  0.5 0.9 %shard_map.91 = (bf16[8,4224]{1,0:T(8,128)(2,1)S(1)}, s32[8,4224]{1,0:T(8,128)S(1)}, s32[8,4224]{1,0:T(8,128)S(1)}) custom-call(bf16[8,4096]{1,0:T(8,128)(2,1)} %raw.1, s32[4,8]{1,0:T(4,128)} %bitcast.2, s32[16]{0:T(128)} %order.1), custom_call_target="tpu_custom_call" | custom-call | bytes 65728 | tf_op jit(solution)/shard_map/pallas_call | solution.py:223
  1.4 0.4 %collective-permute-done.1 = s32[4,8]{1,0:T(4,128)S(1)} collective-permute-done((s32[4,8]{1,0:T(4,128)}, s32[4,8]{1,0:T(4,128)S(1)}, u32[]{:S(2)}, u32[]{:S(2)}) %collective-permute-start.1) | collective-permute-done | bytes 160 | tf_op jit(solution)/shard_map/ppermute | solution.py:240
  1.8 0.0 collective-permute-done
  1.9 3.8 %collective-permute-start.2 = (bf16[8,4224]{1,0:T(8,128)(2,1)S(1)}, bf16[8,4224]{1,0:T(8,128)(2,1)S(1)}, u32[]{:S(2)}, u32[]{:S(2)}) collective-permute-start(bf16[8,4224]{1,0:T(8,128)(2,1)S(1)} %fusion), channel_id=1, source_target_pairs={{0,6},{1,7},{2,4},{3,5},{4,2},{5,3},{6,0},{7,1},{8,14},{9,15},{10,... | collective-permute-start | bytes 202760 | tf_op jit(solution)/shard_map/ppermute | solution.py:240
  5.6 0.4 %collective-permute-start.3 = (bf16[8,4224]{1,0:T(8,128)(2,1)S(1)}, bf16[8,4224]{1,0:T(8,128)(2,1)S(1)}, u32[]{:S(2)}, u32[]{:S(2)}) collective-permute-start(bf16[8,4224]{1,0:T(8,128)(2,1)S(1)} %fusion), channel_id=1, source_target_pairs={{0,4},{1,5},{2,6},{3,7},{4,0},{5,1},{6,2},{7,3},{8,12},{9,13},{10,... | collective-permute-start | bytes 202760 | tf_op jit(solution)/shard_map/ppermute | solution.py:240
  6.1 0.2 collective-permute-start.4
  6.3 1.8 %collective-permute-start.7 = (bf16[8,4224]{1,0:T(8,128)(2,1)S(1)}, bf16[8,4224]{1,0:T(8,128)(2,1)S(1)}, u32[]{:S(2)}, u32[]{:S(2)}) collective-permute-start(bf16[8,4224]{1,0:T(8,128)(2,1)S(1)} %get-tuple-element.30.mine), channel_id=1, source_target_pairs={{0,16},{16,0},{1,17},{17,1},{2,18},{18,2},{3,19},{19,3},{4,20},{20... | collective-permute-start | bytes 202760 | tf_op jit(solution)/shard_map/ppermute | solution.py:240
  8.1 0.2 collective-permute-done.2
  8.3 1.6 %collective-permute-done.3 = bf16[8,4224]{1,0:T(8,128)(2,1)S(1)} collective-permute-done((bf16[8,4224]{1,0:T(8,128)(2,1)S(1)}, bf16[8,4224]{1,0:T(8,128)(2,1)S(1)}, u32[]{:S(2)}, u32[]{:S(2)}) %collective-permute-start.3) | collective-permute-done | bytes 67616 | tf_op jit(solution)/shard_map/ppermute | solution.py:240
  9.9 0.4 %collective-permute-done.4 = bf16[8,4224]{1,0:T(8,128)(2,1)S(1)} collective-permute-done((bf16[8,4224]{1,0:T(8,128)(2,1)S(1)}, bf16[8,4224]{1,0:T(8,128)(2,1)S(1)}, u32[]{:S(2)}, u32[]{:S(2)}) %collective-permute-start.4) | collective-permute-done | bytes 67616 | tf_op jit(solution)/shard_map/ppermute | solution.py:240
  10.4 0.1 compare_select_fusion.2
  10.4 2.7 %collective-permute-start.5 = (bf16[8,4224]{1,0:T(8,128)(2,1)S(1)}, bf16[8,4224]{1,0:T(8,128)(2,1)S(1)}, u32[]{:S(2)}, u32[]{:S(2)}) collective-permute-start(bf16[8,4224]{1,0:T(8,128)(2,1)S(1)} %compare_select_fusion.2), channel_id=1, source_target_pairs={{0,8},{1,16},{2,10},{3,18},{4,12},{5,20},{6,14},{7,22},{8,0},{9,24... | collective-permute-start | bytes 202760 | tf_op jit(solution)/shard_map/ppermute | solution.py:256
  13.1 0.7 %collective-permute-start.6 = (bf16[8,4224]{1,0:T(8,128)(2,1)S(1)}, bf16[8,4224]{1,0:T(8,128)(2,1)S(1)}, u32[]{:S(2)}, u32[]{:S(2)}) collective-permute-start(bf16[8,4224]{1,0:T(8,128)(2,1)S(1)} %compare_select_fusion.2), channel_id=1, source_target_pairs={{1,24},{3,26},{5,28},{7,30},{9,16},{11,18},{13,20},{15,22},{16,9},... | collective-permute-start | bytes 202760 | tf_op jit(solution)/shard_map/ppermute | solution.py:256
  13.8 0.0 collective-permute-done.7.other
  13.8 2.6 %shard_map.92 = (bf16[64,768]{1,0:T(8,128)(2,1)S(1)}, f32[64,128]{1,0:T(8,128)S(1)}, bf16[512,512]{1,0:T(8,128)(2,1)S(1)}, bf16[512,256]{1,0:T(8,128)(2,1)S(1)},...) custom-call(bf16[8,4224]{1,0:T(8,128)(2,1)S(1)} %get-tuple-element.3, ...), custom_call_target="tpu_custom_call" | custom-call | flops 1000000000 | bytes 2396160 | tf_op jit(solution)/shard_map/pallas_call | solution.py:223
  16.3 0.0 collective-permute-done.5
  16.3 0.0 collective-permute-done.6
  16.3 0.1 select_select_fusion.held
  16.4 3.2 %collective-permute-start.8 = (bf16[8,4224]{1,0:T(8,128)(2,1)S(1)}, bf16[8,4224]{1,0:T(8,128)(2,1)S(1)}, u32[]{:S(2)}, u32[]{:S(2)}) collective-permute-start(bf16[8,4224]{1,0:T(8,128)(2,1)S(1)} %select_select_fusion.held), channel_id=1, source_target_pairs={{0,1},{1,0},{2,3},{3,2},{4,5},{5,4},{6,7},{7,6},{8,9},{9,8},{10,11... | collective-permute-start | bytes 202760 | tf_op jit(solution)/shard_map/ppermute | solution.py:240
  19.6 0.9 %collective-permute-done.8.twin = bf16[8,4224]{1,0:T(8,128)(2,1)S(1)} collective-permute-done((bf16[8,4224]{1,0:T(8,128)(2,1)S(1)}, bf16[8,4224]{1,0:T(8,128)(2,1)S(1)}, u32[]{:S(2)}, u32[]{:S(2)}) %collective-permute-start.8) | collective-permute-done | bytes 67616 | tf_op jit(solution)/shard_map/ppermute | solution.py:240
  20.5 2.3 %shard_map.93 = f32[8,8,256]{2,1,0:T(8,128)} custom-call(bf16[8,4224]{1,0:T(8,128)(2,1)S(1)} %select_select_fusion.held, bf16[8,4224]{1,0:T(8,128)(2,1)S(1)} %collective-permute-done.8.twin, bf16[64,768]{1,0:T(8,128)(2,1)S(1)} %get-tuple-element.37.white, f32[64,128]{1,0:T(8,128)S(1)} %get-tuple-element.38.masks, ...), custom_call_target="tpu_custom_call" | custom-call | flops 1000000000 | bytes 2527232 | tf_op jit(solution)/shard_map/pallas_call | solution.py:223
  (2 shorter events, 0.0 us)
Async XLA Ops:
  0.0 1.8 %collective-permute-start = (bf16[8,4096]{1,0:T(8,128)(2,1)}, bf16[8,4096]{1,0:T(8,128)(2,1)S(1)}, u32[]{:S(2)}, u32[]{:S(2)}) collective-permute-start(bf16[8,4096]{1,0:T(8,128)(2,1)} %raw.1), channel_id=1, source_target_pairs={{0,1},{1,0},{2,3},{3,2},{4,5},{5,4},{6,7},{7,6},{8,9},{9,8},{10,11... | collective-permute-start | bytes 196616 | tf_op jit(solution)/shard_map/ppermute | solution.py:240
  0.5 1.4 %collective-permute-start.1 = (s32[4,8]{1,0:T(4,128)}, s32[4,8]{1,0:T(4,128)S(1)}, u32[]{:S(2)}, u32[]{:S(2)}) collective-permute-start(s32[4,8]{1,0:T(4,128)} %bitcast.1), channel_id=1, source_target_pairs={{0,1},{1,0},{2,3},{3,2},{4,5},{5,4},{6,7},{7,6},{8,9},{9,8},{10,11... | collective-permute-start | bytes 392 | tf_op jit(solution)/shard_map/ppermute | solution.py:240
  1.9 6.4 %collective-permute-start.2 = (bf16[8,4224]{1,0:T(8,128)(2,1)S(1)}, bf16[8,4224]{1,0:T(8,128)(2,1)S(1)}, u32[]{:S(2)}, u32[]{:S(2)}) collective-permute-start(bf16[8,4224]{1,0:T(8,128)(2,1)S(1)} %fusion), channel_id=1, source_target_pairs={{0,6},{1,7},{2,4},{3,5},{4,2},{5,3},{6,0},{7,1},{8,14},{9,15},{10,... | collective-permute-start | bytes 202760 | tf_op jit(solution)/shard_map/ppermute | solution.py:240
  5.6 4.3 %collective-permute-start.3 = (bf16[8,4224]{1,0:T(8,128)(2,1)S(1)}, bf16[8,4224]{1,0:T(8,128)(2,1)S(1)}, u32[]{:S(2)}, u32[]{:S(2)}) collective-permute-start(bf16[8,4224]{1,0:T(8,128)(2,1)S(1)} %fusion), channel_id=1, source_target_pairs={{0,4},{1,5},{2,6},{3,7},{4,0},{5,1},{6,2},{7,3},{8,12},{9,13},{10,... | collective-permute-start | bytes 202760 | tf_op jit(solution)/shard_map/ppermute | solution.py:240
  6.1 4.3 %collective-permute-start.4 = (bf16[8,4224]{1,0:T(8,128)(2,1)S(1)}, bf16[8,4224]{1,0:T(8,128)(2,1)S(1)}, u32[]{:S(2)}, u32[]{:S(2)}) collective-permute-start(bf16[8,4224]{1,0:T(8,128)(2,1)S(1)} %fusion), channel_id=1, source_target_pairs={{0,2},{1,3},{2,0},{3,1},{4,6},{5,7},{6,4},{7,5},{8,10},{9,11},{10,... | collective-permute-start | bytes 202760 | tf_op jit(solution)/shard_map/ppermute | solution.py:240
  6.3 7.5 %collective-permute-start.7 = (bf16[8,4224]{1,0:T(8,128)(2,1)S(1)}, bf16[8,4224]{1,0:T(8,128)(2,1)S(1)}, u32[]{:S(2)}, u32[]{:S(2)}) collective-permute-start(bf16[8,4224]{1,0:T(8,128)(2,1)S(1)} %get-tuple-element.30.mine), channel_id=1, source_target_pairs={{0,16},{16,0},{1,17},{17,1},{2,18},{18,2},{3,19},{19,3},{4,20},{20... | collective-permute-start | bytes 202760 | tf_op jit(solution)/shard_map/ppermute | solution.py:240
  10.4 5.9 %collective-permute-start.5 = (bf16[8,4224]{1,0:T(8,128)(2,1)S(1)}, bf16[8,4224]{1,0:T(8,128)(2,1)S(1)}, u32[]{:S(2)}, u32[]{:S(2)}) collective-permute-start(bf16[8,4224]{1,0:T(8,128)(2,1)S(1)} %compare_select_fusion.2), channel_id=1, source_target_pairs={{0,8},{1,16},{2,10},{3,18},{4,12},{5,20},{6,14},{7,22},{8,0},{9,24... | collective-permute-start | bytes 202760 | tf_op jit(solution)/shard_map/ppermute | solution.py:256
  13.1 3.2 %collective-permute-start.6 = (bf16[8,4224]{1,0:T(8,128)(2,1)S(1)}, bf16[8,4224]{1,0:T(8,128)(2,1)S(1)}, u32[]{:S(2)}, u32[]{:S(2)}) collective-permute-start(bf16[8,4224]{1,0:T(8,128)(2,1)S(1)} %compare_select_fusion.2), channel_id=1, source_target_pairs={{1,24},{3,26},{5,28},{7,30},{9,16},{11,18},{13,20},{15,22},{16,9},... | collective-permute-start | bytes 202760 | tf_op jit(solution)/shard_map/ppermute | solution.py:256
  16.4 4.1 %collective-permute-start.8 = (bf16[8,4224]{1,0:T(8,128)(2,1)S(1)}, bf16[8,4224]{1,0:T(8,128)(2,1)S(1)}, u32[]{:S(2)}, u32[]{:S(2)}) collective-permute-start(bf16[8,4224]{1,0:T(8,128)(2,1)S(1)} %select_select_fusion.held), channel_id=1, source_target_pairs={{0,1},{1,0},{2,3},{3,2},{4,5},{5,4},{6,7},{7,6},{8,9},{9,8},{10,11... | collective-permute-start | bytes 202760 | tf_op jit(solution)/shard_map/ppermute | solution.py:240

commit v3 on v2

--- a/solution.py
+++ b/solution.py
@@ -22,6 +22,8 @@
 PAD = 128
 LANES = 128
 
+EARLY = 3
+
 F32 = jnp.float32
 BF16 = jnp.bfloat16
 
@@ -30,6 +32,13 @@
     high = table.astype(BF16)
     low = (table - high.astype(np.float64)).astype(BF16)
     return high, low
+
+
+def band(values):
+    reach = len(values) // 2
+    shift = LANES + np.arange(LANES)[None, :] - np.arange(3 * LANES)[:, None] + reach
+    inside = (shift >= 0) & (shift < len(values))
+    return np.where(inside, values[np.clip(shift, 0, len(values) - 1)], 0.0)
 
 
 def filter_table():
@@ -37,20 +46,15 @@
     low, high = BIN_LO / L, (BIN_LO + NF) / L
     window = 0.5 + 0.5 * np.cos(2.0 * math.pi * k / (TAPS + 1))
     taps = window * (2 * high * np.sinc(2 * high * k) - 2 * low * np.sinc(2 * low * k))
-    shift = BLK // 2 + np.arange(BLK)[None, :] - np.arange(2 * BLK)[:, None] + (TAPS - 1) // 2
-    inside = (shift >= 0) & (shift < TAPS)
-    table = np.where(inside, taps[np.clip(shift, 0, TAPS - 1)], 0.0)
-    return np.concatenate(halves(table), axis=1)
+    return np.concatenate(halves(band(taps)), axis=1)
 
 
 def mean_table():
-    shift = BLK // 2 + np.arange(BLK)[None, :] - np.arange(2 * BLK)[:, None]
-    return (np.abs(shift) <= HW).astype(BF16)
+    return band(np.ones(2 * HW + 1)).astype(BF16)
 
 
 def smooth_table():
-    bins = np.arange(NF)
-    return (np.abs(bins[:, None] - bins[None, :]) <= WF).astype(BF16)
+    return band(np.ones(2 * WF + 1)).astype(BF16)
 
 
 def forward_table():
@@ -59,7 +63,7 @@
 
 
 def lag_table():
-    shifts = np.arange(LAGS)[None, :] - LAGS // 2
+    shifts = np.arange(LAGS // 2)[None, :]
     phase = np.mod((BIN_LO + np.arange(NF))[:, None] * shifts, L) * (2.0 * math.pi / L)
     table = np.concatenate([np.cos(phase), -np.sin(phase)], axis=0) / math.sqrt(NF)
     return halves(table)
@@ -116,45 +120,62 @@
     window = jnp.concatenate(
         [x[: n - 2 * ST, half:], x[ST : n - ST], x[2 * ST :, :half]], axis=1
     ).astype(BF16)
-    both = dot(window, table(0))
-    filtered = both[:, :BLK] + both[:, BLK:]
+    taps = table(0)
+    columns = []
+    for i in range(2):
+        both = dot(window[:, i * half : i * half + 3 * half], taps)
+        columns.append(both[:, :half] + both[:, half:])
+    filtered = jnp.concatenate(columns, axis=1)
     m = filtered.shape[0]
     size = jnp.abs(filtered)
     window = jnp.concatenate(
         [size[: m - 2 * ST, half:], size[ST : m - ST], size[2 * ST :, :half]], axis=1
     )
     high, low = split(window)
-    mean = table(1)
+    mean, zero = table(1), jnp.zeros((half, half), BF16)
+    mean = jnp.concatenate(
+        [jnp.concatenate([mean, zero], axis=0), jnp.concatenate([zero, mean], axis=0)], axis=1
+    )
     total = dot(high, mean) + dot(low, mean)
     normal = filtered[ST : m - ST] / (total * (1.0 / (2 * HW + 1)) + 1e-06)
-    real, imag = quarters(dot(normal.astype(BF16), table(2)))
+    real, imag = quarters(dot(normal.astype(BF16), table(3)))
     amplitude = jnp.sqrt(real * real + imag * imag)
     high, low = split(amplitude)
-    both = dot(jnp.concatenate([high, low], axis=0), table(3))
+    smooth = table(2)
+    zero = jnp.zeros((half, half), BF16)
+    smooth = jnp.concatenate(
+        [
+            jnp.concatenate([smooth[half:], zero], axis=0),
+            smooth,
+            jnp.concatenate([zero, smooth[: 2 * half]], axis=0),
+        ],
+        axis=1,
+    )
+    both = dot(jnp.concatenate([high, low], axis=0), smooth)
     smoothed = both[: SEGS * ST] + both[SEGS * ST :]
     factor = column / (smoothed * (1.0 / (2 * WF + 1)) + 1e-06)
     return jnp.concatenate([real * factor, imag * factor], axis=1).astype(BF16)
 
 
-def pack(raw, mask, order, mine, wanted, carried, order_here, mask_here, sems):
+def pack(raw, mask, order, *refs):
+    count = (len(refs) - 6) // 2
+    tables, (mine, wanted, carried), held = refs[:count], refs[count : count + 3], refs[count + 3 : -3]
+    order_here, mask_here, sems = refs[-3:]
     half = raw.shape[1]
-    away = (wanted, carried)
-    copies = [
-        pltpu.make_async_copy(order, order_here, sems.at[0]),
-        pltpu.make_async_copy(mask, mask_here, sems.at[1]),
-        pltpu.make_async_copy(raw, mine.at[:, pl.ds(0, half)], sems.at[2]),
-    ]
+    ends = [(order, order_here), (mask, mask_here), (raw, mine.at[:, pl.ds(0, half)]), *zip(tables, held)]
+    copies = [pltpu.make_async_copy(a, b, sems.at[i]) for i, (a, b) in enumerate(ends)]
     for copy in copies:
         copy.start()
     mine[:, half:] = jnp.zeros((ST, PAD), BF16)
     me = lax.axis_index("blk")
     copies[0].wait()
-    for i, source in enumerate((lax.axis_index("section"), me & 1)):
-        away[i][...] = jnp.full(away[i].shape, order_here[source] ^ me, jnp.int32)
+    for away, source in ((wanted, lax.axis_index("section")), (carried, me & 1)):
+        away[...] = jnp.full(away.shape, order_here[source] ^ me, jnp.int32)
     copies[1].wait()
     segs, stations = mask.shape
     mine[:segs, half : half + stations] = mask_here[...].astype(F32).astype(BF16)
-    copies[2].wait()
+    for copy in copies[2:]:
+        copy.wait()
 
 
 def ordered(swap, one, two):
@@ -163,21 +184,25 @@
 
 
 def receivers(mine, other, *refs):
-    tables, (white, masks, *held, sems) = refs[:6], refs[6:]
-    copies = [pltpu.make_async_copy(t, h, sems.at[i]) for i, (t, h) in enumerate(zip(tables, held))]
+    early, late, held, (white, masks, sems) = refs[:EARLY], refs[EARLY:6], refs[8:-1], (*refs[6:8], refs[-1])
+    copies = [pltpu.make_async_copy(a, b, sems.at[i]) for i, (a, b) in enumerate(zip(late, held))]
     for copy in copies:
         copy.start()
+    waiting = list(copies)
+
+    def table(i):
+        if i < EARLY:
+            return early[i][...]
+        copies[i - EARLY].wait()
+        waiting.remove(copies[i - EARLY])
+        return held[i - EARLY][...]
+
     parts = ordered(lax.axis_index("section"), mine, other)
     column = mask_column(mask_rows(parts))
     masks[...] = jnp.broadcast_to(column, masks.shape)
-
-    def table(i):
-        copies[i].wait()
-        return held[i][...]
-
     white[...] = whitened(parts, column, table)
-    copies[4].wait()
-    copies[5].wait()
+    for copy in waiting:
+        copy.wait()
 
 
 def correlate(held, twin, white, masks, *refs):
@@ -203,9 +228,16 @@
             imag += ri * sr - rr * si
         rows.append(jnp.concatenate([real, imag], axis=1))
         counts.append(common[:, n : n + 1])
-    high, low = split(jnp.concatenate(rows, axis=0))
+    stack = jnp.concatenate(rows, axis=0)
+    bins = lax.broadcasted_iota(jnp.int32, (1, NF), 1) % 8
+    cos = sum(jnp.where(bins == i, math.cos(math.pi * i / 4), 0.0) for i in range(8))
+    sin = sum(jnp.where(bins == i, math.sin(math.pi * i / 4), 0.0) for i in range(8))
+    real, imag = stack[:, :NF], stack[:, NF:]
+    turned = jnp.concatenate([real * cos + imag * sin, imag * cos - real * sin], axis=1)
+    high, low = split(jnp.concatenate([turned, stack], axis=0))
     both = dot(jnp.concatenate([high, low], axis=0), lag_high[...])
-    lagged = both[:size] + both[size:] + dot(high, lag_low[...])
+    lagged = both[: 2 * size] + both[2 * size :] + dot(high, lag_low[...])
+    lagged = jnp.concatenate([lagged[:size], lagged[size:]], axis=1)
     lagged = lagged / jnp.maximum(jnp.concatenate(counts, axis=0), 1.0)
     out[...] = lagged.reshape(ST, ST, LAGS)
 
@@ -259,61 +291,67 @@
 def shards(raw_traces, valid_mask, block_order):
     section = lax.axis_index("section")
     blocks = lax.axis_size("blk")
-    me = lax.axis_index("blk")
-    core = me & 1
+    core = lax.axis_index("blk") & 1
     half = raw_traces.shape[1]
     width = half + PAD
-    mine, away_wanted, away_carried = call(
+    tables = [filter_table(), mean_table(), smooth_table(), forward_table(), *lag_table()]
+    tables = [jnp.asarray(t) for t in tables]
+    early, late = tables[:EARLY], tables[EARLY:]
+    mine, away_wanted, away_carried, *early = call(
         pack,
-        [shaped(ST, width)] + [shaped(ST, width, dtype=jnp.int32)] * 2,
-        [HBM] * 3,
-        [raw_traces, valid_mask.T, block_order],
+        [shaped(ST, width)]
+        + [shaped(ST, width, dtype=jnp.int32)] * 2
+        + [shaped(*t.shape) for t in early],
+        [HBM] * (3 + EARLY),
+        [raw_traces, valid_mask.T, block_order, *early],
         [
             pltpu.SMEM(block_order.shape, jnp.int32),
             pltpu.VMEM(valid_mask.shape[::-1], jnp.int32),
-            pltpu.SemaphoreType.DMA((3,)),
+            pltpu.SemaphoreType.DMA((3 + EARLY,)),
         ],
     )
 
-    raw_twin, mask_twin = exchange(raw_traces, 1), exchange(valid_mask.T, 1)
-    raw_twin, mask_twin, mine, away_wanted, away_carried = lax.optimization_barrier((raw_twin, mask_twin, mine, away_wanted, away_carried))
-    twin = lax.pad(raw_twin, jnp.zeros((), BF16), ((0, 0, 0), (0, PAD, 0)))
+    raw_twin, mask_twin, mine, away_wanted, away_carried = lax.optimization_barrier(
+        (exchange(raw_traces, 1), exchange(valid_mask.T, 1), mine, away_wanted, away_carried)
+    )
+    nothing = jnp.zeros((), BF16)
     rest = ((0, ST - valid_mask.shape[1], 0), (half, PAD - ST, 0))
-    twin += lax.pad(mask_twin.astype(BF16), jnp.zeros((), BF16), rest)
+    twin = lax.pad(raw_twin, nothing, ((0, 0, 0), (0, PAD, 0)))
+    twin += lax.pad(mask_twin.astype(BF16), nothing, rest)
     held = jnp.where(away_carried & 1 == 0, mine, twin)
+
     bits = [1 << i for i in range(1, blocks.bit_length() - 1)]
     last = bits.pop()
-    other = None
+    near, far = crossing(held, last)
+    other = exchange(mine, 1, "section")
+    same = away_wanted & last == 0
+    held = jnp.where(core == section, jnp.where(same, held, near), jnp.where(same, near, far))
+
+    white = masks = None
     while bits:
         flips, bits = bits[:2], bits[2:]
-        low, steps = flips[0], 1 << len(flips)
-        got = [exchange(held, low * k) for k in range(1, steps)]
-        if other is None:
-            other = exchange(mine, 1, "section")
-        rel = away_carried & (low * (steps - 1))
-        for k in range(1, steps):
-            held = jnp.where(rel == low * k, got[k - 1], held)
-    tables = [filter_table(), mean_table(), forward_table(), smooth_table(), *lag_table()]
-    tables = [jnp.asarray(t) for t in tables]
-    near, far = crossing(held, last)
-    white, masks, *tables = call(
-        receivers,
-        [shaped(SEGS * ST, 2 * NF), shaped(SEGS * ST, LANES, dtype=F32)]
-        + [shaped(*t.shape) for t in tables],
-        [VMEM] * 2 + [HBM] * len(tables),
-        [mine, other, *tables],
-        [pltpu.SemaphoreType.DMA((len(tables),))],
-        flops=10**9,
-    )
-    near, far, white, masks = lax.optimization_barrier((near, far, white, masks))
-    same = away_wanted & last == 0
-    held = jnp.where(core == section, jnp.where(same, held, near), jnp.where(same, near, far))
+        shifts = [flips[0] * k for k in range(1, 1 << len(flips))][::-1]
+        got = [exchange(held, k) for k in shifts]
+        if white is None:
+            white, masks, *late = call(
+                receivers,
+                [shaped(SEGS * ST, 2 * NF), shaped(SEGS * ST, LANES, dtype=F32)]
+                + [shaped(*t.shape) for t in late],
+                [VMEM] * (2 + EARLY) + [HBM] * len(late),
+                [mine, other, *early, *late],
+                [pltpu.SemaphoreType.DMA((len(late),))],
+                flops=10**9,
+            )
+            *got, white, masks = lax.optimization_barrier((*got, white, masks))
+        rel = away_wanted & sum(flips)
+        for k, piece in zip(shifts, got):
+            held = jnp.where(rel == k, piece, held)
     twin = exchange(held, 1)
     return call(
         correlate,
         shaped(ST, ST, LAGS, dtype=F32),
         [VMEM] * 10,
-        [held, twin, white, masks, *tables],
+        [held, twin, white, masks, *early, *late],
         flops=10**9,
     )
 

time: 23 us -> 22.2 us (0.965)
  Pallas kernels: 5.76 us -> 5.07 us
  starting transfers between devices: 13.2 us -> 12.8 us
  waiting for transfers between devices: 3.62 us -> 3.9 us
    ppermute x7, starting transfers between devices: 9.94 us -> 8.23 us  [exchange(): return lax.ppermute(x, axis, [(i, i ^ flip) for i in range(devices)])]
    ppermute x2, starting transfers between devices: 3.31 us -> 4.62 us  [crossing(): return (lax.ppermute(x, axes, near), lax.ppermute(x, axes, far))]
    pallas_call x3, Pallas kernels: 5.76 us -> 5.07 us  [call(): pl.pallas_call(body, out_shape=out_shape, in_specs=in_specs, out_specs=ja...]
    ppermute x7, waiting for transfers between devices: 3.62 us -> 3.9 us  [exchange(): return lax.ppermute(x, axis, [(i, i ^ flip) for i in range(devices)])]
  transfers between devices with their start and end apart: 9 -> 9, of which waited for: 5 -> 5; matrix products, arithmetic and copies ran while one was open for 0% -> 0% of each run, Pallas kernels for 15% -> 13%
where the time goes in v3:
time: 22.2 us; the launch traced here: 22 us
  starting transfers between devices  12.8 us (58%)
  Pallas kernels  5.07 us (23%)
  waiting for transfers between devices  3.9 us (18%)
    ppermute x7, starting transfers between devices, exchange(): return lax.ppermute(x, axis, [(i, i ^ flip) for i in range(devices)])  8.23 us
    pallas_call x3, Pallas kernels, call(): pl.pallas_call(body, out_shape=out_shape, in_specs=in_specs, out_specs=ja...  5.07 us
    ppermute x2, starting transfers between devices, crossing(): return (lax.ppermute(x, axes, near), lax.ppermute(x, axes, far))  4.62 us
    ppermute x7, waiting for transfers between devices, exchange(): return lax.ppermute(x, axis, [(i, i ^ flip) for i in range(devices)])  3.9 us
  transfers between devices with their start and end apart: 9, of which 5 were waited for; matrix products, arithmetic and copies ran while one was open for 0% of the time, Pallas kernels for 13%

profile of v3, /device:TPU:0, one launch (start us, length us, event | category | flops | bytes accessed | tf_op | source)
XLA Modules:
  0.0 22.0 jit_solution(10202356824486301360)
XLA Ops:
  0.0 0.5 %collective-permute-start = (bf16[8,4096]{1,0:T(8,128)(2,1)}, bf16[8,4096]{1,0:T(8,128)(2,1)S(1)}, u32[]{:S(2)}, u32[]{:S(2)}) collective-permute-start(bf16[8,4096]{1,0:T(8,128)(2,1)} %raw.1), channel_id=1, source_target_pairs={{0,1},{1,0},{2,3},{3,2},{4,5},{5,4},{6,7},{7,6},{8,9},{9,8},{10,11... | collective-permute-start | bytes 196616 | tf_op jit(solution)/shard_map/ppermute | solution.py:272
  0.5 0.1 collective-permute-start.1
  0.5 1.1 %shard_map.91 = (bf16[8,4224]{1,0:T(8,128)(2,1)S(1)}, s32[8,4224]{1,0:T(8,128)S(1)}, s32[8,4224]{1,0:T(8,128)S(1)}, bf16[384,256]{1,0:T(8,128)(2,1)S(1)}, bf16[3...) custom-call(bf16[8,4096]{1,0:T(8,128)(2,1)} %raw.1, s32[4,8]{1,0:T(4,128)} %bitcast.2, s32[16]{0:T(128)} %order.1, ...), custom_call_target="tpu_custom_call" | custom-call | bytes 458944 | tf_op jit(solution)/shard_map/pallas_call | solution.py:255
  1.7 0.2 collective-permute-done.1
  1.8 0.0 collective-permute-done
  1.9 4.0 %collective-permute-start.2 = (bf16[8,4224]{1,0:T(8,128)(2,1)S(1)}, bf16[8,4224]{1,0:T(8,128)(2,1)S(1)}, u32[]{:S(2)}, u32[]{:S(2)}) collective-permute-start(bf16[8,4224]{1,0:T(8,128)(2,1)S(1)} %fusion), channel_id=1, source_target_pairs={{0,8},{1,16},{2,10},{3,18},{4,12},{5,20},{6,14},{7,22},{8,0},{9,24... | collective-permute-start | bytes 202760 | tf_op jit(solution)/shard_map/ppermute | solution.py:288
  5.8 0.7 %collective-permute-start.3 = (bf16[8,4224]{1,0:T(8,128)(2,1)S(1)}, bf16[8,4224]{1,0:T(8,128)(2,1)S(1)}, u32[]{:S(2)}, u32[]{:S(2)}) collective-permute-start(bf16[8,4224]{1,0:T(8,128)(2,1)S(1)} %fusion), channel_id=1, source_target_pairs={{1,24},{3,26},{5,28},{7,30},{9,16},{11,18},{13,20},{15,22},{16,9},... | collective-permute-start | bytes 202760 | tf_op jit(solution)/shard_map/ppermute | solution.py:288
  6.5 4.0 %collective-permute-start.7 = (bf16[8,4224]{1,0:T(8,128)(2,1)S(1)}, bf16[8,4224]{1,0:T(8,128)(2,1)S(1)}, u32[]{:S(2)}, u32[]{:S(2)}) collective-permute-start(bf16[8,4224]{1,0:T(8,128)(2,1)S(1)} %get-tuple-element.31.mine), channel_id=1, source_target_pairs={{0,16},{16,0},{1,17},{17,1},{2,18},{18,2},{3,19},{19,3},{4,20},{20... | collective-permute-start | bytes 202760 | tf_op jit(solution)/shard_map/ppermute | solution.py:272
  10.5 0.0 collective-permute-done.2
  10.5 0.0 collective-permute-done.3
  10.5 2.6 %collective-permute-start.4 = (bf16[8,4224]{1,0:T(8,128)(2,1)S(1)}, bf16[8,4224]{1,0:T(8,128)(2,1)S(1)}, u32[]{:S(2)}, u32[]{:S(2)}) collective-permute-start(bf16[8,4224]{1,0:T(8,128)(2,1)S(1)} %select_select_fusion), channel_id=1, source_target_pairs={{0,6},{1,7},{2,4},{3,5},{4,2},{5,3},{6,0},{7,1},{8,14},{9,15},{10,... | collective-permute-start | bytes 202760 | tf_op jit(solution)/shard_map/ppermute | solution.py:272
  13.1 0.4 %collective-permute-start.5 = (bf16[8,4224]{1,0:T(8,128)(2,1)S(1)}, bf16[8,4224]{1,0:T(8,128)(2,1)S(1)}, u32[]{:S(2)}, u32[]{:S(2)}) collective-permute-start(bf16[8,4224]{1,0:T(8,128)(2,1)S(1)} %select_select_fusion), channel_id=1, source_target_pairs={{0,4},{1,5},{2,6},{3,7},{4,0},{5,1},{6,2},{7,3},{8,12},{9,13},{10,... | collective-permute-start | bytes 202760 | tf_op jit(solution)/shard_map/ppermute | solution.py:272
  13.6 0.5 %collective-permute-start.6 = (bf16[8,4224]{1,0:T(8,128)(2,1)S(1)}, bf16[8,4224]{1,0:T(8,128)(2,1)S(1)}, u32[]{:S(2)}, u32[]{:S(2)}) collective-permute-start(bf16[8,4224]{1,0:T(8,128)(2,1)S(1)} %select_select_fusion), channel_id=1, source_target_pairs={{0,2},{1,3},{2,0},{3,1},{4,6},{5,7},{6,4},{7,5},{8,10},{9,11},{10,... | collective-permute-start | bytes 202760 | tf_op jit(solution)/shard_map/ppermute | solution.py:272
  14.1 0.0 collective-permute-done.7.other
  14.1 1.6 %shard_map.92 = (bf16[64,768]{1,0:T(8,128)(2,1)S(1)}, f32[64,128]{1,0:T(8,128)S(1)}, bf16[256,768]{1,0:T(8,128)(2,1)S(1)}, bf16[768,128]{1,0:T(8,128)(2,1)S(1)}, bf16[768,128]{1,0:T(8,128)(2,1)S(1)}) custom-call(bf16[8,4224]{1,0:T(8,128)(2,1)S(1)} %get-tuple-element.31.mine, bf16[8,4224]{1,0:T(8,128)(2,1)S(1)} %collective-permute-done.7.other, ...), custom_call_target="tpu_custom_call" | custom-call | flops 1000000000 | bytes 1314816 | tf_op jit(solution)/shard_map/pallas_call | solution.py:255
  15.7 0.1 collective-permute-done.4
  15.8 1.8 %collective-permute-done.5 = bf16[8,4224]{1,0:T(8,128)(2,1)S(1)} collective-permute-done((bf16[8,4224]{1,0:T(8,128)(2,1)S(1)}, bf16[8,4224]{1,0:T(8,128)(2,1)S(1)}, u32[]{:S(2)}, u32[]{:S(2)}) %collective-permute-start.5) | collective-permute-done | bytes 67616 | tf_op jit(solution)/shard_map/ppermute | solution.py:272
  17.6 0.7 %collective-permute-done.6 = bf16[8,4224]{1,0:T(8,128)(2,1)S(1)} collective-permute-done((bf16[8,4224]{1,0:T(8,128)(2,1)S(1)}, bf16[8,4224]{1,0:T(8,128)(2,1)S(1)}, u32[]{:S(2)}, u32[]{:S(2)}) %collective-permute-start.6) | collective-permute-done | bytes 67616 | tf_op jit(solution)/shard_map/ppermute | solution.py:272
  18.3 0.1 compare_select_fusion.2.held
  18.4 0.2 collective-permute-start.8
  18.6 1.1 %collective-permute-done.8.twin = bf16[8,4224]{1,0:T(8,128)(2,1)S(1)} collective-permute-done((bf16[8,4224]{1,0:T(8,128)(2,1)S(1)}, bf16[8,4224]{1,0:T(8,128)(2,1)S(1)}, u32[]{:S(2)}, u32[]{:S(2)}) %collective-permute-start.8) | collective-permute-done | bytes 67616 | tf_op jit(solution)/shard_map/ppermute | solution.py:272
  19.7 2.3 %shard_map.93 = f32[8,8,256]{2,1,0:T(8,128)} custom-call(bf16[8,4224]{1,0:T(8,128)(2,1)S(1)} %compare_select_fusion.2.held, bf16[8,4224]{1,0:T(8,128)(2,1)S(1)} %collective-permute-done.8.twin, bf16[64,768]{1,0:T(8,128)(2,1)S(1)} %get-tuple-element.42.white, f32[64,128]{1,0:T(8,128)S(1)} %get-tuple-element.43.masks, ...), custom_call_target="tpu_custom_call" | custom-call | flops 1000000000 | bytes 1445888 | tf_op jit(solution)/shard_map/pallas_call | solution.py:255
  (3 shorter events, 0.1 us)
Async XLA Ops:
  0.0 1.8 %collective-permute-start = (bf16[8,4096]{1,0:T(8,128)(2,1)}, bf16[8,4096]{1,0:T(8,128)(2,1)S(1)}, u32[]{:S(2)}, u32[]{:S(2)}) collective-permute-start(bf16[8,4096]{1,0:T(8,128)(2,1)} %raw.1), channel_id=1, source_target_pairs={{0,1},{1,0},{2,3},{3,2},{4,5},{5,4},{6,7},{7,6},{8,9},{9,8},{10,11... | collective-permute-start | bytes 196616 | tf_op jit(solution)/shard_map/ppermute | solution.py:272
  0.5 1.4 %collective-permute-start.1 = (s32[4,8]{1,0:T(4,128)}, s32[4,8]{1,0:T(4,128)S(1)}, u32[]{:S(2)}, u32[]{:S(2)}) collective-permute-start(s32[4,8]{1,0:T(4,128)} %bitcast.1), channel_id=1, source_target_pairs={{0,1},{1,0},{2,3},{3,2},{4,5},{5,4},{6,7},{7,6},{8,9},{9,8},{10,11... | collective-permute-start | bytes 392 | tf_op jit(solution)/shard_map/ppermute | solution.py:272
  1.9 8.6 %collective-permute-start.2 = (bf16[8,4224]{1,0:T(8,128)(2,1)S(1)}, bf16[8,4224]{1,0:T(8,128)(2,1)S(1)}, u32[]{:S(2)}, u32[]{:S(2)}) collective-permute-start(bf16[8,4224]{1,0:T(8,128)(2,1)S(1)} %fusion), channel_id=1, source_target_pairs={{0,8},{1,16},{2,10},{3,18},{4,12},{5,20},{6,14},{7,22},{8,0},{9,24... | collective-permute-start | bytes 202760 | tf_op jit(solution)/shard_map/ppermute | solution.py:288
  5.8 4.7 %collective-permute-start.3 = (bf16[8,4224]{1,0:T(8,128)(2,1)S(1)}, bf16[8,4224]{1,0:T(8,128)(2,1)S(1)}, u32[]{:S(2)}, u32[]{:S(2)}) collective-permute-start(bf16[8,4224]{1,0:T(8,128)(2,1)S(1)} %fusion), channel_id=1, source_target_pairs={{1,24},{3,26},{5,28},{7,30},{9,16},{11,18},{13,20},{15,22},{16,9},... | collective-permute-start | bytes 202760 | tf_op jit(solution)/shard_map/ppermute | solution.py:288
  6.5 7.6 %collective-permute-start.7 = (bf16[8,4224]{1,0:T(8,128)(2,1)S(1)}, bf16[8,4224]{1,0:T(8,128)(2,1)S(1)}, u32[]{:S(2)}, u32[]{:S(2)}) collective-permute-start(bf16[8,4224]{1,0:T(8,128)(2,1)S(1)} %get-tuple-element.31.mine), channel_id=1, source_target_pairs={{0,16},{16,0},{1,17},{17,1},{2,18},{18,2},{3,19},{19,3},{4,20},{20... | collective-permute-start | bytes 202760 | tf_op jit(solution)/shard_map/ppermute | solution.py:272
  10.5 5.3 %collective-permute-start.4 = (bf16[8,4224]{1,0:T(8,128)(2,1)S(1)}, bf16[8,4224]{1,0:T(8,128)(2,1)S(1)}, u32[]{:S(2)}, u32[]{:S(2)}) collective-permute-start(bf16[8,4224]{1,0:T(8,128)(2,1)S(1)} %select_select_fusion), channel_id=1, source_target_pairs={{0,6},{1,7},{2,4},{3,5},{4,2},{5,3},{6,0},{7,1},{8,14},{9,15},{10,... | collective-permute-start | bytes 202760 | tf_op jit(solution)/shard_map/ppermute | solution.py:272
  13.1 4.5 %collective-permute-start.5 = (bf16[8,4224]{1,0:T(8,128)(2,1)S(1)}, bf16[8,4224]{1,0:T(8,128)(2,1)S(1)}, u32[]{:S(2)}, u32[]{:S(2)}) collective-permute-start(bf16[8,4224]{1,0:T(8,128)(2,1)S(1)} %select_select_fusion), channel_id=1, source_target_pairs={{0,4},{1,5},{2,6},{3,7},{4,0},{5,1},{6,2},{7,3},{8,12},{9,13},{10,... | collective-permute-start | bytes 202760 | tf_op jit(solution)/shard_map/ppermute | solution.py:272
  13.6 4.7 %collective-permute-start.6 = (bf16[8,4224]{1,0:T(8,128)(2,1)S(1)}, bf16[8,4224]{1,0:T(8,128)(2,1)S(1)}, u32[]{:S(2)}, u32[]{:S(2)}) collective-permute-start(bf16[8,4224]{1,0:T(8,128)(2,1)S(1)} %select_select_fusion), channel_id=1, source_target_pairs={{0,2},{1,3},{2,0},{3,1},{4,6},{5,7},{6,4},{7,5},{8,10},{9,11},{10,... | collective-permute-start | bytes 202760 | tf_op jit(solution)/shard_map/ppermute | solution.py:272
  18.4 1.3 %collective-permute-start.8 = (bf16[8,4224]{1,0:T(8,128)(2,1)S(1)}, bf16[8,4224]{1,0:T(8,128)(2,1)S(1)}, u32[]{:S(2)}, u32[]{:S(2)}) collective-permute-start(bf16[8,4224]{1,0:T(8,128)(2,1)S(1)} %compare_select_fusion.2.held), channel_id=1, source_target_pairs={{0,1},{1,0},{2,3},{3,2},{4,5},{5,4},{6,7},{7,6},{8,9},{9,8},{10,11... | collective-permute-start | bytes 202760 | tf_op jit(solution)/shard_map/ppermute | solution.py:272

commit v4 on v3

--- a/solution.py
+++ b/solution.py
@@ -278,13 +278,13 @@
     near, far = [], []
     for s in range(2):
         for b in range(blocks):
-            here = s * blocks + b
+            here, there = s * blocks, (1 - s) * blocks
             if s == b % 2:
-                near.append((here, s * blocks + (b ^ bit)))
+                near.append((here + b, here + (b ^ bit)))
+                far.append((here + b, there + (b ^ 1)))
             else:
-                there = (1 - s) * blocks
-                near.append((here, there + (b ^ 1)))
-                far.append((here, there + (b ^ 1 ^ bit)))
+                near.append((here + b, there + (b ^ 1)))
+                far.append((here + b, there + (b ^ 1 ^ bit)))
     return lax.ppermute(x, axes, near), lax.ppermute(x, axes, far)
 
 

time: 22.2 us -> 20.9 us (0.941)
  starting transfers between devices: 12.8 us -> 10.8 us
  waiting for transfers between devices: 3.9 us -> 4.7 us
    ppermute x7, starting transfers between devices: 8.23 us -> 5.81 us  [exchange(): return lax.ppermute(x, axis, [(i, i ^ flip) for i in range(devices)])]
    ppermute x2, waiting for transfers between devices: 0.01 us -> 1.04 us  [crossing(): return (lax.ppermute(x, axes, near), lax.ppermute(x, axes, far))]
    ppermute x2, starting transfers between devices: 4.62 us -> 4.97 us  [crossing(): return (lax.ppermute(x, axes, near), lax.ppermute(x, axes, far))]
    ppermute x7, waiting for transfers between devices: 3.9 us -> 3.66 us  [exchange(): return lax.ppermute(x, axis, [(i, i ^ flip) for i in range(devices)])]
where the time goes in v4:
time: 20.9 us; the launch traced here: 20.7 us
  starting transfers between devices  10.8 us (52%)
  Pallas kernels  5.07 us (24%)
  waiting for transfers between devices  4.7 us (22%)
    ppermute x7, starting transfers between devices, exchange(): return lax.ppermute(x, axis, [(i, i ^ flip) for i in range(devices)])  5.81 us
    pallas_call x3, Pallas kernels, call(): pl.pallas_call(body, out_shape=out_shape, in_specs=in_specs, out_specs=ja...  5.07 us
    ppermute x2, starting transfers between devices, crossing(): return (lax.ppermute(x, axes, near), lax.ppermute(x, axes, far))  4.97 us
    ppermute x7, waiting for transfers between devices, exchange(): return lax.ppermute(x, axis, [(i, i ^ flip) for i in range(devices)])  3.66 us
    ppermute x2, waiting for transfers between devices, crossing(): return (lax.ppermute(x, axes, near), lax.ppermute(x, axes, far))  1.04 us
  transfers between devices with their start and end apart: 9, of which 5 were waited for; matrix products, arithmetic and copies ran while one was open for 0% of the time, Pallas kernels for 13%

profile of v4, /device:TPU:0, one launch (start us, length us, event | category | flops | bytes accessed | tf_op | source)
XLA Modules:
  0.0 20.7 jit_solution(13756727373564945830)
XLA Ops:
  0.0 0.5 %collective-permute-start = (bf16[8,4096]{1,0:T(8,128)(2,1)}, bf16[8,4096]{1,0:T(8,128)(2,1)S(1)}, u32[]{:S(2)}, u32[]{:S(2)}) collective-permute-start(bf16[8,4096]{1,0:T(8,128)(2,1)} %raw.1), channel_id=1, source_target_pairs={{0,1},{1,0},{2,3},{3,2},{4,5},{5,4},{6,7},{7,6},{8,9},{9,8},{10,11... | collective-permute-start | bytes 196616 | tf_op jit(solution)/shard_map/ppermute | solution.py:272
  0.5 0.1 collective-permute-start.1
  0.5 1.1 %shard_map.91 = (bf16[8,4224]{1,0:T(8,128)(2,1)S(1)}, s32[8,4224]{1,0:T(8,128)S(1)}, s32[8,4224]{1,0:T(8,128)S(1)}, bf16[384,256]{1,0:T(8,128)(2,1)S(1)}, bf16[3...) custom-call(bf16[8,4096]{1,0:T(8,128)(2,1)} %raw.1, s32[4,8]{1,0:T(4,128)} %bitcast.2, s32[16]{0:T(128)} %order.1, ...), custom_call_target="tpu_custom_call" | custom-call | bytes 458944 | tf_op jit(solution)/shard_map/pallas_call | solution.py:255
  1.7 0.2 collective-permute-done.1
  1.8 0.0 collective-permute-done
  1.9 4.0 %collective-permute-start.2 = (bf16[8,4224]{1,0:T(8,128)(2,1)S(1)}, bf16[8,4224]{1,0:T(8,128)(2,1)S(1)}, u32[]{:S(2)}, u32[]{:S(2)}) collective-permute-start(bf16[8,4224]{1,0:T(8,128)(2,1)S(1)} %fusion), channel_id=1, source_target_pairs={{0,8},{1,16},{2,10},{3,18},{4,12},{5,20},{6,14},{7,22},{8,0},{9,24... | collective-permute-start | bytes 202760 | tf_op jit(solution)/shard_map/ppermute | solution.py:288
  5.8 1.0 %collective-permute-start.3 = (bf16[8,4224]{1,0:T(8,128)(2,1)S(1)}, bf16[8,4224]{1,0:T(8,128)(2,1)S(1)}, u32[]{:S(2)}, u32[]{:S(2)}) collective-permute-start(bf16[8,4224]{1,0:T(8,128)(2,1)S(1)} %fusion), channel_id=1, source_target_pairs={{0,17},{1,24},{2,19},{3,26},{4,21},{5,28},{6,23},{7,30},{8,25},{9,... | collective-permute-start | bytes 202760 | tf_op jit(solution)/shard_map/ppermute | solution.py:288
  6.8 1.7 %collective-permute-start.7 = (bf16[8,4224]{1,0:T(8,128)(2,1)S(1)}, bf16[8,4224]{1,0:T(8,128)(2,1)S(1)}, u32[]{:S(2)}, u32[]{:S(2)}) collective-permute-start(bf16[8,4224]{1,0:T(8,128)(2,1)S(1)} %get-tuple-element.31.mine), channel_id=1, source_target_pairs={{0,16},{16,0},{1,17},{17,1},{2,18},{18,2},{3,19},{19,3},{4,20},{20... | collective-permute-start | bytes 202760 | tf_op jit(solution)/shard_map/ppermute | solution.py:272
  8.5 0.0 collective-permute-done.2
  8.5 1.0 %collective-permute-done.3 = bf16[8,4224]{1,0:T(8,128)(2,1)S(1)} collective-permute-done((bf16[8,4224]{1,0:T(8,128)(2,1)S(1)}, bf16[8,4224]{1,0:T(8,128)(2,1)S(1)}, u32[]{:S(2)}, u32[]{:S(2)}) %collective-permute-start.3) | collective-permute-done | bytes 67616 | tf_op jit(solution)/shard_map/ppermute | solution.py:288
  9.6 2.7 %collective-permute-start.4 = (bf16[8,4224]{1,0:T(8,128)(2,1)S(1)}, bf16[8,4224]{1,0:T(8,128)(2,1)S(1)}, u32[]{:S(2)}, u32[]{:S(2)}) collective-permute-start(bf16[8,4224]{1,0:T(8,128)(2,1)S(1)} %select_select_fusion), channel_id=1, source_target_pairs={{0,6},{1,7},{2,4},{3,5},{4,2},{5,3},{6,0},{7,1},{8,14},{9,15},{10,... | collective-permute-start | bytes 202760 | tf_op jit(solution)/shard_map/ppermute | solution.py:272
  12.3 0.3 %collective-permute-start.5 = (bf16[8,4224]{1,0:T(8,128)(2,1)S(1)}, bf16[8,4224]{1,0:T(8,128)(2,1)S(1)}, u32[]{:S(2)}, u32[]{:S(2)}) collective-permute-start(bf16[8,4224]{1,0:T(8,128)(2,1)S(1)} %select_select_fusion), channel_id=1, source_target_pairs={{0,4},{1,5},{2,6},{3,7},{4,0},{5,1},{6,2},{7,3},{8,12},{9,13},{10,... | collective-permute-start | bytes 202760 | tf_op jit(solution)/shard_map/ppermute | solution.py:272
  12.6 0.5 %collective-permute-start.6 = (bf16[8,4224]{1,0:T(8,128)(2,1)S(1)}, bf16[8,4224]{1,0:T(8,128)(2,1)S(1)}, u32[]{:S(2)}, u32[]{:S(2)}) collective-permute-start(bf16[8,4224]{1,0:T(8,128)(2,1)S(1)} %select_select_fusion), channel_id=1, source_target_pairs={{0,2},{1,3},{2,0},{3,1},{4,6},{5,7},{6,4},{7,5},{8,10},{9,11},{10,... | collective-permute-start | bytes 202760 | tf_op jit(solution)/shard_map/ppermute | solution.py:272
  13.2 0.0 collective-permute-done.7.other
  13.2 1.6 %shard_map.92 = (bf16[64,768]{1,0:T(8,128)(2,1)S(1)}, f32[64,128]{1,0:T(8,128)S(1)}, bf16[256,768]{1,0:T(8,128)(2,1)S(1)}, bf16[768,128]{1,0:T(8,128)(2,1)S(1)}, bf16[768,128]{1,0:T(8,128)(2,1)S(1)}) custom-call(bf16[8,4224]{1,0:T(8,128)(2,1)S(1)} %get-tuple-element.31.mine, bf16[8,4224]{1,0:T(8,128)(2,1)S(1)} %collective-permute-done.7.other, ...), custom_call_target="tpu_custom_call" | custom-call | flops 1000000000 | bytes 1314816 | tf_op jit(solution)/shard_map/pallas_call | solution.py:255
  14.8 0.8 %collective-permute-done.4 = bf16[8,4224]{1,0:T(8,128)(2,1)S(1)} collective-permute-done((bf16[8,4224]{1,0:T(8,128)(2,1)S(1)}, bf16[8,4224]{1,0:T(8,128)(2,1)S(1)}, u32[]{:S(2)}, u32[]{:S(2)}) %collective-permute-start.4) | collective-permute-done | bytes 67616 | tf_op jit(solution)/shard_map/ppermute | solution.py:272
  15.6 1.5 %collective-permute-done.5 = bf16[8,4224]{1,0:T(8,128)(2,1)S(1)} collective-permute-done((bf16[8,4224]{1,0:T(8,128)(2,1)S(1)}, bf16[8,4224]{1,0:T(8,128)(2,1)S(1)}, u32[]{:S(2)}, u32[]{:S(2)}) %collective-permute-start.5) | collective-permute-done | bytes 67616 | tf_op jit(solution)/shard_map/ppermute | solution.py:272
  17.0 0.0 collective-permute-done.6
  17.0 0.1 compare_select_fusion.2.held
  17.1 0.1 collective-permute-start.8
  17.2 1.2 %collective-permute-done.8.twin = bf16[8,4224]{1,0:T(8,128)(2,1)S(1)} collective-permute-done((bf16[8,4224]{1,0:T(8,128)(2,1)S(1)}, bf16[8,4224]{1,0:T(8,128)(2,1)S(1)}, u32[]{:S(2)}, u32[]{:S(2)}) %collective-permute-start.8) | collective-permute-done | bytes 67616 | tf_op jit(solution)/shard_map/ppermute | solution.py:272
  18.4 2.3 %shard_map.93 = f32[8,8,256]{2,1,0:T(8,128)} custom-call(bf16[8,4224]{1,0:T(8,128)(2,1)S(1)} %compare_select_fusion.2.held, bf16[8,4224]{1,0:T(8,128)(2,1)S(1)} %collective-permute-done.8.twin, bf16[64,768]{1,0:T(8,128)(2,1)S(1)} %get-tuple-element.42.white, f32[64,128]{1,0:T(8,128)S(1)} %get-tuple-element.43.masks, ...), custom_call_target="tpu_custom_call" | custom-call | flops 1000000000 | bytes 1445888 | tf_op jit(solution)/shard_map/pallas_call | solution.py:255
  (3 shorter events, 0.1 us)
Async XLA Ops:
  0.0 1.8 %collective-permute-start = (bf16[8,4096]{1,0:T(8,128)(2,1)}, bf16[8,4096]{1,0:T(8,128)(2,1)S(1)}, u32[]{:S(2)}, u32[]{:S(2)}) collective-permute-start(bf16[8,4096]{1,0:T(8,128)(2,1)} %raw.1), channel_id=1, source_target_pairs={{0,1},{1,0},{2,3},{3,2},{4,5},{5,4},{6,7},{7,6},{8,9},{9,8},{10,11... | collective-permute-start | bytes 196616 | tf_op jit(solution)/shard_map/ppermute | solution.py:272
  0.5 1.4 %collective-permute-start.1 = (s32[4,8]{1,0:T(4,128)}, s32[4,8]{1,0:T(4,128)S(1)}, u32[]{:S(2)}, u32[]{:S(2)}) collective-permute-start(s32[4,8]{1,0:T(4,128)} %bitcast.1), channel_id=1, source_target_pairs={{0,1},{1,0},{2,3},{3,2},{4,5},{5,4},{6,7},{7,6},{8,9},{9,8},{10,11... | collective-permute-start | bytes 392 | tf_op jit(solution)/shard_map/ppermute | solution.py:272
  1.9 6.6 %collective-permute-start.2 = (bf16[8,4224]{1,0:T(8,128)(2,1)S(1)}, bf16[8,4224]{1,0:T(8,128)(2,1)S(1)}, u32[]{:S(2)}, u32[]{:S(2)}) collective-permute-start(bf16[8,4224]{1,0:T(8,128)(2,1)S(1)} %fusion), channel_id=1, source_target_pairs={{0,8},{1,16},{2,10},{3,18},{4,12},{5,20},{6,14},{7,22},{8,0},{9,24... | collective-permute-start | bytes 202760 | tf_op jit(solution)/shard_map/ppermute | solution.py:288
  5.8 3.7 %collective-permute-start.3 = (bf16[8,4224]{1,0:T(8,128)(2,1)S(1)}, bf16[8,4224]{1,0:T(8,128)(2,1)S(1)}, u32[]{:S(2)}, u32[]{:S(2)}) collective-permute-start(bf16[8,4224]{1,0:T(8,128)(2,1)S(1)} %fusion), channel_id=1, source_target_pairs={{0,17},{1,24},{2,19},{3,26},{4,21},{5,28},{6,23},{7,30},{8,25},{9,... | collective-permute-start | bytes 202760 | tf_op jit(solution)/shard_map/ppermute | solution.py:288
  6.8 6.3 %collective-permute-start.7 = (bf16[8,4224]{1,0:T(8,128)(2,1)S(1)}, bf16[8,4224]{1,0:T(8,128)(2,1)S(1)}, u32[]{:S(2)}, u32[]{:S(2)}) collective-permute-start(bf16[8,4224]{1,0:T(8,128)(2,1)S(1)} %get-tuple-element.31.mine), channel_id=1, source_target_pairs={{0,16},{16,0},{1,17},{17,1},{2,18},{18,2},{3,19},{19,3},{4,20},{20... | collective-permute-start | bytes 202760 | tf_op jit(solution)/shard_map/ppermute | solution.py:272
  9.6 6.0 %collective-permute-start.4 = (bf16[8,4224]{1,0:T(8,128)(2,1)S(1)}, bf16[8,4224]{1,0:T(8,128)(2,1)S(1)}, u32[]{:S(2)}, u32[]{:S(2)}) collective-permute-start(bf16[8,4224]{1,0:T(8,128)(2,1)S(1)} %select_select_fusion), channel_id=1, source_target_pairs={{0,6},{1,7},{2,4},{3,5},{4,2},{5,3},{6,0},{7,1},{8,14},{9,15},{10,... | collective-permute-start | bytes 202760 | tf_op jit(solution)/shard_map/ppermute | solution.py:272
  12.3 4.7 %collective-permute-start.5 = (bf16[8,4224]{1,0:T(8,128)(2,1)S(1)}, bf16[8,4224]{1,0:T(8,128)(2,1)S(1)}, u32[]{:S(2)}, u32[]{:S(2)}) collective-permute-start(bf16[8,4224]{1,0:T(8,128)(2,1)S(1)} %select_select_fusion), channel_id=1, source_target_pairs={{0,4},{1,5},{2,6},{3,7},{4,0},{5,1},{6,2},{7,3},{8,12},{9,13},{10,... | collective-permute-start | bytes 202760 | tf_op jit(solution)/shard_map/ppermute | solution.py:272
  12.6 4.4 %collective-permute-start.6 = (bf16[8,4224]{1,0:T(8,128)(2,1)S(1)}, bf16[8,4224]{1,0:T(8,128)(2,1)S(1)}, u32[]{:S(2)}, u32[]{:S(2)}) collective-permute-start(bf16[8,4224]{1,0:T(8,128)(2,1)S(1)} %select_select_fusion), channel_id=1, source_target_pairs={{0,2},{1,3},{2,0},{3,1},{4,6},{5,7},{6,4},{7,5},{8,10},{9,11},{10,... | collective-permute-start | bytes 202760 | tf_op jit(solution)/shard_map/ppermute | solution.py:272
  17.1 1.3 %collective-permute-start.8 = (bf16[8,4224]{1,0:T(8,128)(2,1)S(1)}, bf16[8,4224]{1,0:T(8,128)(2,1)S(1)}, u32[]{:S(2)}, u32[]{:S(2)}) collective-permute-start(bf16[8,4224]{1,0:T(8,128)(2,1)S(1)} %compare_select_fusion.2.held), channel_id=1, source_target_pairs={{0,1},{1,0},{2,3},{3,2},{4,5},{5,4},{6,7},{7,6},{8,9},{9,8},{10,11... | collective-permute-start | bytes 202760 | tf_op jit(solution)/shard_map/ppermute | solution.py:272

commit v5 on v4

--- a/solution.py
+++ b/solution.py
@@ -21,8 +21,6 @@
 ROWS = SEGS * L // BLK
 PAD = 128
 LANES = 128
-
-EARLY = 3
 
 F32 = jnp.float32
 BF16 = jnp.bfloat16
@@ -157,12 +155,9 @@
     return jnp.concatenate([real * factor, imag * factor], axis=1).astype(BF16)
 
 
-def pack(raw, mask, order, *refs):
-    count = (len(refs) - 6) // 2
-    tables, (mine, wanted, carried), held = refs[:count], refs[count : count + 3], refs[count + 3 : -3]
-    order_here, mask_here, sems = refs[-3:]
+def pack(raw, mask, order, mine, wanted, carried, order_here, mask_here, sems):
     half = raw.shape[1]
-    ends = [(order, order_here), (mask, mask_here), (raw, mine.at[:, pl.ds(0, half)]), *zip(tables, held)]
+    ends = [(order, order_here), (mask, mask_here), (raw, mine.at[:, pl.ds(0, half)])]
     copies = [pltpu.make_async_copy(a, b, sems.at[i]) for i, (a, b) in enumerate(ends)]
     for copy in copies:
         copy.start()
@@ -174,8 +169,7 @@
     copies[1].wait()
     segs, stations = mask.shape
     mine[:segs, half : half + stations] = mask_here[...].astype(F32).astype(BF16)
-    for copy in copies[2:]:
-        copy.wait()
+    copies[2].wait()
 
 
 def ordered(swap, one, two):
@@ -184,24 +178,20 @@
 
 
 def receivers(mine, other, *refs):
-    early, late, held, (white, masks, sems) = refs[:EARLY], refs[EARLY:6], refs[8:-1], (*refs[6:8], refs[-1])
-    copies = [pltpu.make_async_copy(a, b, sems.at[i]) for i, (a, b) in enumerate(zip(late, held))]
+    tables, (white, masks), held, sems = refs[:6], refs[6:8], refs[8:14], refs[14]
+    copies = [pltpu.make_async_copy(a, b, sems.at[i]) for i, (a, b) in enumerate(zip(tables, held))]
     for copy in copies:
         copy.start()
-    waiting = list(copies)
 
     def table(i):
-        if i < EARLY:
-            return early[i][...]
-        copies[i - EARLY].wait()
-        waiting.remove(copies[i - EARLY])
-        return held[i - EARLY][...]
+        copies[i].wait()
+        return held[i][...]
 
     parts = ordered(lax.axis_index("section"), mine, other)
     column = mask_column(mask_rows(parts))
     masks[...] = jnp.broadcast_to(column, masks.shape)
     white[...] = whitened(parts, column, table)
-    for copy in waiting:
+    for copy in copies[4:]:
         copy.wait()
 
 
@@ -296,18 +286,15 @@
     width = half + PAD
     tables = [filter_table(), mean_table(), smooth_table(), forward_table(), *lag_table()]
     tables = [jnp.asarray(t) for t in tables]
-    early, late = tables[:EARLY], tables[EARLY:]
-    mine, away_wanted, away_carried, *early = call(
+    mine, away_wanted, away_carried = call(
         pack,
-        [shaped(ST, width)]
-        + [shaped(ST, width, dtype=jnp.int32)] * 2
-        + [shaped(*t.shape) for t in early],
-        [HBM] * (3 + EARLY),
-        [raw_traces, valid_mask.T, block_order, *early],
+        [shaped(ST, width)] + [shaped(ST, width, dtype=jnp.int32)] * 2,
+        [HBM] * 3,
+        [raw_traces, valid_mask.T, block_order],
         [
             pltpu.SMEM(block_order.shape, jnp.int32),
             pltpu.VMEM(valid_mask.shape[::-1], jnp.int32),
-            pltpu.SemaphoreType.DMA((3 + EARLY,)),
+            pltpu.SemaphoreType.DMA((3,)),
         ],
     )
 
@@ -325,21 +312,22 @@
     near, far = crossing(held, last)
     other = exchange(mine, 1, "section")
     same = away_wanted & last == 0
+    far, near = lax.optimization_barrier((far, near))
     held = jnp.where(core == section, jnp.where(same, held, near), jnp.where(same, near, far))
 
     white = masks = None
     while bits:
         flips, bits = bits[:2], bits[2:]
-        shifts = [flips[0] * k for k in range(1, 1 << len(flips))][::-1]
+        shifts = [flips[0] * k for k in range(1, 1 << len(flips))]
         got = [exchange(held, k) for k in shifts]
         if white is None:
-            white, masks, *late = call(
+            white, masks, *tables = call(
                 receivers,
                 [shaped(SEGS * ST, 2 * NF), shaped(SEGS * ST, LANES, dtype=F32)]
-                + [shaped(*t.shape) for t in late],
-                [VMEM] * (2 + EARLY) + [HBM] * len(late),
-                [mine, other, *early, *late],
-                [pltpu.SemaphoreType.DMA((len(late),))],
+                + [shaped(*t.shape) for t in tables],
+                [VMEM] * 2 + [HBM] * len(tables),
+                [mine, other, *tables],
+                [pltpu.SemaphoreType.DMA((len(tables),))],
                 flops=10**9,
             )
             *got, white, masks = lax.optimization_barrier((*got, white, masks))
@@ -351,7 +339,7 @@
         correlate,
         shaped(ST, ST, LAGS, dtype=F32),
         [VMEM] * 10,
-        [held, twin, white, masks, *early, *late],
+        [held, twin, white, masks, *tables],
         flops=10**9,
     )
 

time: 20.9 us -> 20.8 us (level)
  waiting for transfers between devices: 4.7 us -> 4.2 us
  Pallas kernels: 5.07 us -> 5.55 us
    ppermute x7, waiting for transfers between devices: 3.66 us -> 3.16 us  [exchange(): return lax.ppermute(x, axis, [(i, i ^ flip) for i in range(devices)])]
    pallas_call x3, Pallas kernels: 5.07 us -> 5.55 us  [call(): pl.pallas_call(body, out_shape=out_shape, in_specs=in_specs, out_specs=ja...]
  transfers between devices with their start and end apart: 9 -> 9, of which waited for: 5 -> 5; matrix products, arithmetic and copies ran while one was open for 0% -> 0% of each run, Pallas kernels for 13% -> 16%
where the time goes in v5:
time: 20.8 us; the launch traced here: 20.6 us
  starting transfers between devices  10.6 us (51%)
  Pallas kernels  5.55 us (27%)
  waiting for transfers between devices  4.2 us (20%)
    ppermute x7, starting transfers between devices, exchange(): return lax.ppermute(x, axis, [(i, i ^ flip) for i in range(devices)])  5.66 us
    pallas_call x3, Pallas kernels, call(): pl.pallas_call(body, out_shape=out_shape, in_specs=in_specs, out_specs=ja...  5.55 us
    ppermute x2, starting transfers between devices, crossing(): return (lax.ppermute(x, axes, near), lax.ppermute(x, axes, far))  4.97 us
    ppermute x7, waiting for transfers between devices, exchange(): return lax.ppermute(x, axis, [(i, i ^ flip) for i in range(devices)])  3.16 us
    ppermute x2, waiting for transfers between devices, crossing(): return (lax.ppermute(x, axes, near), lax.ppermute(x, axes, far))  1.04 us
  transfers between devices with their start and end apart: 9, of which 5 were waited for; matrix products, arithmetic and copies ran while one was open for 0% of the time, Pallas kernels for 16%

profile of v5, /device:TPU:0, one launch (start us, length us, event | category | flops | bytes accessed | tf_op | source)
XLA Modules:
  0.0 20.6 jit_solution(9193382251333569283)
XLA Ops:
  0.0 0.5 %collective-permute-start = (bf16[8,4096]{1,0:T(8,128)(2,1)}, bf16[8,4096]{1,0:T(8,128)(2,1)S(1)}, u32[]{:S(2)}, u32[]{:S(2)}) collective-permute-start(bf16[8,4096]{1,0:T(8,128)(2,1)} %raw.1), channel_id=1, source_target_pairs={{0,1},{1,0},{2,3},{3,2},{4,5},{5,4},{6,7},{7,6},{8,9},{9,8},{10,11... | collective-permute-start | bytes 196616 | tf_op jit(solution)/shard_map/ppermute | solution.py:262
  0.5 0.1 collective-permute-start.1
  0.5 0.9 %shard_map.91 = (bf16[8,4224]{1,0:T(8,128)(2,1)S(1)}, s32[8,4224]{1,0:T(8,128)S(1)}, s32[8,4224]{1,0:T(8,128)S(1)}) custom-call(bf16[8,4096]{1,0:T(8,128)(2,1)} %raw.1, s32[4,8]{1,0:T(4,128)} %bitcast.2, s32[16]{0:T(128)} %order.1), custom_call_target="tpu_custom_call" | custom-call | bytes 65728 | tf_op jit(solution)/shard_map/pallas_call | solution.py:245
  1.4 0.4 %collective-permute-done.1 = s32[4,8]{1,0:T(4,128)S(1)} collective-permute-done((s32[4,8]{1,0:T(4,128)}, s32[4,8]{1,0:T(4,128)S(1)}, u32[]{:S(2)}, u32[]{:S(2)}) %collective-permute-start.1) | collective-permute-done | bytes 160 | tf_op jit(solution)/shard_map/ppermute | solution.py:262
  1.8 0.0 collective-permute-done
  1.9 3.8 %collective-permute-start.3 = (bf16[8,4224]{1,0:T(8,128)(2,1)S(1)}, bf16[8,4224]{1,0:T(8,128)(2,1)S(1)}, u32[]{:S(2)}, u32[]{:S(2)}) collective-permute-start(bf16[8,4224]{1,0:T(8,128)(2,1)S(1)} %fusion), channel_id=1, source_target_pairs={{0,8},{1,16},{2,10},{3,18},{4,12},{5,20},{6,14},{7,22},{8,0},{9,24... | collective-permute-start | bytes 202760 | tf_op jit(solution)/shard_map/ppermute | solution.py:278
  5.7 1.2 %collective-permute-start.2 = (bf16[8,4224]{1,0:T(8,128)(2,1)S(1)}, bf16[8,4224]{1,0:T(8,128)(2,1)S(1)}, u32[]{:S(2)}, u32[]{:S(2)}) collective-permute-start(bf16[8,4224]{1,0:T(8,128)(2,1)S(1)} %fusion), channel_id=1, source_target_pairs={{0,17},{1,24},{2,19},{3,26},{4,21},{5,28},{6,23},{7,30},{8,25},{9,... | collective-permute-start | bytes 202760 | tf_op jit(solution)/shard_map/ppermute | solution.py:278
  6.8 1.5 %collective-permute-start.7 = (bf16[8,4224]{1,0:T(8,128)(2,1)S(1)}, bf16[8,4224]{1,0:T(8,128)(2,1)S(1)}, u32[]{:S(2)}, u32[]{:S(2)}) collective-permute-start(bf16[8,4224]{1,0:T(8,128)(2,1)S(1)} %get-tuple-element.33.mine), channel_id=1, source_target_pairs={{0,16},{16,0},{1,17},{17,1},{2,18},{18,2},{3,19},{19,3},{4,20},{20... | collective-permute-start | bytes 202760 | tf_op jit(solution)/shard_map/ppermute | solution.py:262
  8.4 0.0 collective-permute-done.3
  8.4 1.0 %collective-permute-done.2 = bf16[8,4224]{1,0:T(8,128)(2,1)S(1)} collective-permute-done((bf16[8,4224]{1,0:T(8,128)(2,1)S(1)}, bf16[8,4224]{1,0:T(8,128)(2,1)S(1)}, u32[]{:S(2)}, u32[]{:S(2)}) %collective-permute-start.2) | collective-permute-done | bytes 67616 | tf_op jit(solution)/shard_map/ppermute | solution.py:278
  9.5 2.7 %collective-permute-start.6 = (bf16[8,4224]{1,0:T(8,128)(2,1)S(1)}, bf16[8,4224]{1,0:T(8,128)(2,1)S(1)}, u32[]{:S(2)}, u32[]{:S(2)}) collective-permute-start(bf16[8,4224]{1,0:T(8,128)(2,1)S(1)} %select_select_fusion), channel_id=1, source_target_pairs={{0,6},{1,7},{2,4},{3,5},{4,2},{5,3},{6,0},{7,1},{8,14},{9,15},{10,... | collective-permute-start | bytes 202760 | tf_op jit(solution)/shard_map/ppermute | solution.py:262
  12.2 0.3 %collective-permute-start.5 = (bf16[8,4224]{1,0:T(8,128)(2,1)S(1)}, bf16[8,4224]{1,0:T(8,128)(2,1)S(1)}, u32[]{:S(2)}, u32[]{:S(2)}) collective-permute-start(bf16[8,4224]{1,0:T(8,128)(2,1)S(1)} %select_select_fusion), channel_id=1, source_target_pairs={{0,4},{1,5},{2,6},{3,7},{4,0},{5,1},{6,2},{7,3},{8,12},{9,13},{10,... | collective-permute-start | bytes 202760 | tf_op jit(solution)/shard_map/ppermute | solution.py:262
  12.5 0.5 %collective-permute-start.4 = (bf16[8,4224]{1,0:T(8,128)(2,1)S(1)}, bf16[8,4224]{1,0:T(8,128)(2,1)S(1)}, u32[]{:S(2)}, u32[]{:S(2)}) collective-permute-start(bf16[8,4224]{1,0:T(8,128)(2,1)S(1)} %select_select_fusion), channel_id=1, source_target_pairs={{0,2},{1,3},{2,0},{3,1},{4,6},{5,7},{6,4},{7,5},{8,10},{9,11},{10,... | collective-permute-start | bytes 202760 | tf_op jit(solution)/shard_map/ppermute | solution.py:262
  13.0 0.0 collective-permute-done.7.other
  13.0 2.4 %shard_map.92 = (bf16[64,768]{1,0:T(8,128)(2,1)S(1)}, f32[64,128]{1,0:T(8,128)S(1)}, bf16[384,256]{1,0:T(8,128)(2,1)S(1)}, bf16[384,128]{1,0:T(8,128)(2,1)S(1)},...) custom-call(bf16[8,4224]{1,0:T(8,128)(2,1)S(1)} %get-tuple-element.3, ...), custom_call_target="tpu_custom_call" | custom-call | flops 1000000000 | bytes 1314816 | tf_op jit(solution)/shard_map/pallas_call | solution.py:245
  15.4 0.1 collective-permute-done.6
  15.4 1.4 %collective-permute-done.5 = bf16[8,4224]{1,0:T(8,128)(2,1)S(1)} collective-permute-done((bf16[8,4224]{1,0:T(8,128)(2,1)S(1)}, bf16[8,4224]{1,0:T(8,128)(2,1)S(1)}, u32[]{:S(2)}, u32[]{:S(2)}) %collective-permute-start.5) | collective-permute-done | bytes 67616 | tf_op jit(solution)/shard_map/ppermute | solution.py:262
  16.8 0.0 collective-permute-done.4
  16.9 0.1 compare_select_fusion.2.held
  16.9 0.1 collective-permute-start.8
  17.0 1.2 %collective-permute-done.8.twin = bf16[8,4224]{1,0:T(8,128)(2,1)S(1)} collective-permute-done((bf16[8,4224]{1,0:T(8,128)(2,1)S(1)}, bf16[8,4224]{1,0:T(8,128)(2,1)S(1)}, u32[]{:S(2)}, u32[]{:S(2)}) %collective-permute-start.8) | collective-permute-done | bytes 67616 | tf_op jit(solution)/shard_map/ppermute | solution.py:262
  18.3 2.3 %shard_map.93 = f32[8,8,256]{2,1,0:T(8,128)} custom-call(bf16[8,4224]{1,0:T(8,128)(2,1)S(1)} %compare_select_fusion.2.held, bf16[8,4224]{1,0:T(8,128)(2,1)S(1)} %collective-permute-done.8.twin, bf16[64,768]{1,0:T(8,128)(2,1)S(1)} %get-tuple-element.43.white, f32[64,128]{1,0:T(8,128)S(1)} %get-tuple-element.44.masks, ...), custom_call_target="tpu_custom_call" | custom-call | flops 1000000000 | bytes 1445888 | tf_op jit(solution)/shard_map/pallas_call | solution.py:245
  (3 shorter events, 0.1 us)
Async XLA Ops:
  0.0 1.8 %collective-permute-start = (bf16[8,4096]{1,0:T(8,128)(2,1)}, bf16[8,4096]{1,0:T(8,128)(2,1)S(1)}, u32[]{:S(2)}, u32[]{:S(2)}) collective-permute-start(bf16[8,4096]{1,0:T(8,128)(2,1)} %raw.1), channel_id=1, source_target_pairs={{0,1},{1,0},{2,3},{3,2},{4,5},{5,4},{6,7},{7,6},{8,9},{9,8},{10,11... | collective-permute-start | bytes 196616 | tf_op jit(solution)/shard_map/ppermute | solution.py:262
  0.5 1.4 %collective-permute-start.1 = (s32[4,8]{1,0:T(4,128)}, s32[4,8]{1,0:T(4,128)S(1)}, u32[]{:S(2)}, u32[]{:S(2)}) collective-permute-start(s32[4,8]{1,0:T(4,128)} %bitcast.1), channel_id=1, source_target_pairs={{0,1},{1,0},{2,3},{3,2},{4,5},{5,4},{6,7},{7,6},{8,9},{9,8},{10,11... | collective-permute-start | bytes 392 | tf_op jit(solution)/shard_map/ppermute | solution.py:262
  1.9 6.5 %collective-permute-start.3 = (bf16[8,4224]{1,0:T(8,128)(2,1)S(1)}, bf16[8,4224]{1,0:T(8,128)(2,1)S(1)}, u32[]{:S(2)}, u32[]{:S(2)}) collective-permute-start(bf16[8,4224]{1,0:T(8,128)(2,1)S(1)} %fusion), channel_id=1, source_target_pairs={{0,8},{1,16},{2,10},{3,18},{4,12},{5,20},{6,14},{7,22},{8,0},{9,24... | collective-permute-start | bytes 202760 | tf_op jit(solution)/shard_map/ppermute | solution.py:278
  5.7 3.7 %collective-permute-start.2 = (bf16[8,4224]{1,0:T(8,128)(2,1)S(1)}, bf16[8,4224]{1,0:T(8,128)(2,1)S(1)}, u32[]{:S(2)}, u32[]{:S(2)}) collective-permute-start(bf16[8,4224]{1,0:T(8,128)(2,1)S(1)} %fusion), channel_id=1, source_target_pairs={{0,17},{1,24},{2,19},{3,26},{4,21},{5,28},{6,23},{7,30},{8,25},{9,... | collective-permute-start | bytes 202760 | tf_op jit(solution)/shard_map/ppermute | solution.py:278
  6.8 6.2 %collective-permute-start.7 = (bf16[8,4224]{1,0:T(8,128)(2,1)S(1)}, bf16[8,4224]{1,0:T(8,128)(2,1)S(1)}, u32[]{:S(2)}, u32[]{:S(2)}) collective-permute-start(bf16[8,4224]{1,0:T(8,128)(2,1)S(1)} %get-tuple-element.33.mine), channel_id=1, source_target_pairs={{0,16},{16,0},{1,17},{17,1},{2,18},{18,2},{3,19},{19,3},{4,20},{20... | collective-permute-start | bytes 202760 | tf_op jit(solution)/shard_map/ppermute | solution.py:262
  9.5 6.0 %collective-permute-start.6 = (bf16[8,4224]{1,0:T(8,128)(2,1)S(1)}, bf16[8,4224]{1,0:T(8,128)(2,1)S(1)}, u32[]{:S(2)}, u32[]{:S(2)}) collective-permute-start(bf16[8,4224]{1,0:T(8,128)(2,1)S(1)} %select_select_fusion), channel_id=1, source_target_pairs={{0,6},{1,7},{2,4},{3,5},{4,2},{5,3},{6,0},{7,1},{8,14},{9,15},{10,... | collective-permute-start | bytes 202760 | tf_op jit(solution)/shard_map/ppermute | solution.py:262
  12.2 4.7 %collective-permute-start.5 = (bf16[8,4224]{1,0:T(8,128)(2,1)S(1)}, bf16[8,4224]{1,0:T(8,128)(2,1)S(1)}, u32[]{:S(2)}, u32[]{:S(2)}) collective-permute-start(bf16[8,4224]{1,0:T(8,128)(2,1)S(1)} %select_select_fusion), channel_id=1, source_target_pairs={{0,4},{1,5},{2,6},{3,7},{4,0},{5,1},{6,2},{7,3},{8,12},{9,13},{10,... | collective-permute-start | bytes 202760 | tf_op jit(solution)/shard_map/ppermute | solution.py:262
  12.5 4.4 %collective-permute-start.4 = (bf16[8,4224]{1,0:T(8,128)(2,1)S(1)}, bf16[8,4224]{1,0:T(8,128)(2,1)S(1)}, u32[]{:S(2)}, u32[]{:S(2)}) collective-permute-start(bf16[8,4224]{1,0:T(8,128)(2,1)S(1)} %select_select_fusion), channel_id=1, source_target_pairs={{0,2},{1,3},{2,0},{3,1},{4,6},{5,7},{6,4},{7,5},{8,10},{9,11},{10,... | collective-permute-start | bytes 202760 | tf_op jit(solution)/shard_map/ppermute | solution.py:262
  16.9 1.3 %collective-permute-start.8 = (bf16[8,4224]{1,0:T(8,128)(2,1)S(1)}, bf16[8,4224]{1,0:T(8,128)(2,1)S(1)}, u32[]{:S(2)}, u32[]{:S(2)}) collective-permute-start(bf16[8,4224]{1,0:T(8,128)(2,1)S(1)} %compare_select_fusion.2.held), channel_id=1, source_target_pairs={{0,1},{1,0},{2,3},{3,2},{4,5},{5,4},{6,7},{7,6},{8,9},{9,8},{10,11... | collective-permute-start | bytes 202760 | tf_op jit(solution)/shard_map/ppermute | solution.py:262

commit v6 on v5

--- a/solution.py
+++ b/solution.py
@@ -134,7 +134,8 @@
     mean = jnp.concatenate(
         [jnp.concatenate([mean, zero], axis=0), jnp.concatenate([zero, mean], axis=0)], axis=1
     )
-    total = dot(high, mean) + dot(low, mean)
+    both = dot(jnp.concatenate([high, low], axis=0), mean)
+    total = both[: both.shape[0] // 2] + both[both.shape[0] // 2 :]
     normal = filtered[ST : m - ST] / (total * (1.0 / (2 * HW + 1)) + 1e-06)
     real, imag = quarters(dot(normal.astype(BF16), table(3)))
     amplitude = jnp.sqrt(real * real + imag * imag)
@@ -236,7 +237,7 @@
 HBM = pl.BlockSpec(memory_space=pltpu.HBM)
 
 
-def call(body, out_shape, in_specs, arrays, scratch=(), flops=0):
+def call(body, out_shape, in_specs, arrays, scratch=(), flops=0, fused=None):
     size = sum(a.size * a.dtype.itemsize for a in arrays)
     arrays = [
         pltpu.with_memory_space_constraint(a, pltpu.HBM) if spec is HBM else a
@@ -249,7 +250,7 @@
         out_specs=jax.tree.map(lambda _: VMEM, out_shape),
         scratch_shapes=scratch,
         cost_estimate=pl.CostEstimate(flops=flops, bytes_accessed=size, transcendentals=0),
-        compiler_params=pltpu.CompilerParams(vmem_limit_bytes=16 * 1024 * 1024),
+        compiler_params=pltpu.CompilerParams(vmem_limit_bytes=16 * 1024 * 1024, allow_input_fusion=fused),
     )(*arrays)
 
 
@@ -341,6 +342,7 @@
         [VMEM] * 10,
         [held, twin, white, masks, *tables],
         flops=10**9,
+        fused=[True] + [False] * 9,
     )
 
 

time: 20.8 us -> 20.8 us (level)
  no operation moved by 1% of the time
where the time goes in v6:
time: 20.8 us; the launch traced here: 20.6 us
  starting transfers between devices  10.6 us (51%)
  Pallas kernels  5.55 us (27%)
  waiting for transfers between devices  4.2 us (20%)
    ppermute x7, starting transfers between devices, exchange(): return lax.ppermute(x, axis, [(i, i ^ flip) for i in range(devices)])  5.66 us
    pallas_call x3, Pallas kernels, call(): pl.pallas_call(body, out_shape=out_shape, in_specs=in_specs, out_specs=ja...  5.55 us
    ppermute x2, starting transfers between devices, crossing(): return (lax.ppermute(x, axes, near), lax.ppermute(x, axes, far))  4.97 us
    ppermute x7, waiting for transfers between devices, exchange(): return lax.ppermute(x, axis, [(i, i ^ flip) for i in range(devices)])  3.16 us
    ppermute x2, waiting for transfers between devices, crossing(): return (lax.ppermute(x, axes, near), lax.ppermute(x, axes, far))  1.04 us
  transfers between devices with their start and end apart: 9, of which 5 were waited for; matrix products, arithmetic and copies ran while one was open for 0% of the time, Pallas kernels for 16%

profile of v6, /device:TPU:0, one launch (start us, length us, event | category | flops | bytes accessed | tf_op | source)
XLA Modules:
  0.0 20.6 jit_solution(3713037267391731092)
XLA Ops:
  0.0 0.5 %collective-permute-start = (bf16[8,4096]{1,0:T(8,128)(2,1)}, bf16[8,4096]{1,0:T(8,128)(2,1)S(1)}, u32[]{:S(2)}, u32[]{:S(2)}) collective-permute-start(bf16[8,4096]{1,0:T(8,128)(2,1)} %raw.1), channel_id=1, source_target_pairs={{0,1},{1,0},{2,3},{3,2},{4,5},{5,4},{6,7},{7,6},{8,9},{9,8},{10,11... | collective-permute-start | bytes 196616 | tf_op jit(solution)/shard_map/ppermute | solution.py:263
  0.5 0.1 collective-permute-start.1
  0.5 0.9 %shard_map.91 = (bf16[8,4224]{1,0:T(8,128)(2,1)S(1)}, s32[8,4224]{1,0:T(8,128)S(1)}, s32[8,4224]{1,0:T(8,128)S(1)}) custom-call(bf16[8,4096]{1,0:T(8,128)(2,1)} %raw.1, s32[4,8]{1,0:T(4,128)} %bitcast.2, s32[16]{0:T(128)} %order.1), custom_call_target="tpu_custom_call" | custom-call | bytes 65728 | tf_op jit(solution)/shard_map/pallas_call | solution.py:246
  1.4 0.4 %collective-permute-done.1 = s32[4,8]{1,0:T(4,128)S(1)} collective-permute-done((s32[4,8]{1,0:T(4,128)}, s32[4,8]{1,0:T(4,128)S(1)}, u32[]{:S(2)}, u32[]{:S(2)}) %collective-permute-start.1) | collective-permute-done | bytes 160 | tf_op jit(solution)/shard_map/ppermute | solution.py:263
  1.8 0.0 collective-permute-done
  1.9 3.8 %collective-permute-start.3 = (bf16[8,4224]{1,0:T(8,128)(2,1)S(1)}, bf16[8,4224]{1,0:T(8,128)(2,1)S(1)}, u32[]{:S(2)}, u32[]{:S(2)}) collective-permute-start(bf16[8,4224]{1,0:T(8,128)(2,1)S(1)} %fusion), channel_id=1, source_target_pairs={{0,8},{1,16},{2,10},{3,18},{4,12},{5,20},{6,14},{7,22},{8,0},{9,24... | collective-permute-start | bytes 202760 | tf_op jit(solution)/shard_map/ppermute | solution.py:279
  5.7 1.2 %collective-permute-start.2 = (bf16[8,4224]{1,0:T(8,128)(2,1)S(1)}, bf16[8,4224]{1,0:T(8,128)(2,1)S(1)}, u32[]{:S(2)}, u32[]{:S(2)}) collective-permute-start(bf16[8,4224]{1,0:T(8,128)(2,1)S(1)} %fusion), channel_id=1, source_target_pairs={{0,17},{1,24},{2,19},{3,26},{4,21},{5,28},{6,23},{7,30},{8,25},{9,... | collective-permute-start | bytes 202760 | tf_op jit(solution)/shard_map/ppermute | solution.py:279
  6.8 1.5 %collective-permute-start.7 = (bf16[8,4224]{1,0:T(8,128)(2,1)S(1)}, bf16[8,4224]{1,0:T(8,128)(2,1)S(1)}, u32[]{:S(2)}, u32[]{:S(2)}) collective-permute-start(bf16[8,4224]{1,0:T(8,128)(2,1)S(1)} %get-tuple-element.33.mine), channel_id=1, source_target_pairs={{0,16},{16,0},{1,17},{17,1},{2,18},{18,2},{3,19},{19,3},{4,20},{20... | collective-permute-start | bytes 202760 | tf_op jit(solution)/shard_map/ppermute | solution.py:263
  8.4 0.0 collective-permute-done.3
  8.4 1.0 %collective-permute-done.2 = bf16[8,4224]{1,0:T(8,128)(2,1)S(1)} collective-permute-done((bf16[8,4224]{1,0:T(8,128)(2,1)S(1)}, bf16[8,4224]{1,0:T(8,128)(2,1)S(1)}, u32[]{:S(2)}, u32[]{:S(2)}) %collective-permute-start.2) | collective-permute-done | bytes 67616 | tf_op jit(solution)/shard_map/ppermute | solution.py:279
  9.5 2.7 %collective-permute-start.6 = (bf16[8,4224]{1,0:T(8,128)(2,1)S(1)}, bf16[8,4224]{1,0:T(8,128)(2,1)S(1)}, u32[]{:S(2)}, u32[]{:S(2)}) collective-permute-start(bf16[8,4224]{1,0:T(8,128)(2,1)S(1)} %select_select_fusion), channel_id=1, source_target_pairs={{0,6},{1,7},{2,4},{3,5},{4,2},{5,3},{6,0},{7,1},{8,14},{9,15},{10,... | collective-permute-start | bytes 202760 | tf_op jit(solution)/shard_map/ppermute | solution.py:263
  12.2 0.3 %collective-permute-start.5 = (bf16[8,4224]{1,0:T(8,128)(2,1)S(1)}, bf16[8,4224]{1,0:T(8,128)(2,1)S(1)}, u32[]{:S(2)}, u32[]{:S(2)}) collective-permute-start(bf16[8,4224]{1,0:T(8,128)(2,1)S(1)} %select_select_fusion), channel_id=1, source_target_pairs={{0,4},{1,5},{2,6},{3,7},{4,0},{5,1},{6,2},{7,3},{8,12},{9,13},{10,... | collective-permute-start | bytes 202760 | tf_op jit(solution)/shard_map/ppermute | solution.py:263
  12.5 0.5 %collective-permute-start.4 = (bf16[8,4224]{1,0:T(8,128)(2,1)S(1)}, bf16[8,4224]{1,0:T(8,128)(2,1)S(1)}, u32[]{:S(2)}, u32[]{:S(2)}) collective-permute-start(bf16[8,4224]{1,0:T(8,128)(2,1)S(1)} %select_select_fusion), channel_id=1, source_target_pairs={{0,2},{1,3},{2,0},{3,1},{4,6},{5,7},{6,4},{7,5},{8,10},{9,11},{10,... | collective-permute-start | bytes 202760 | tf_op jit(solution)/shard_map/ppermute | solution.py:263
  13.0 0.0 collective-permute-done.7.other
  13.0 2.4 %shard_map.92 = (bf16[64,768]{1,0:T(8,128)(2,1)S(1)}, f32[64,128]{1,0:T(8,128)S(1)}, bf16[384,256]{1,0:T(8,128)(2,1)S(1)}, bf16[384,128]{1,0:T(8,128)(2,1)S(1)},...) custom-call(bf16[8,4224]{1,0:T(8,128)(2,1)S(1)} %get-tuple-element.3, ...), custom_call_target="tpu_custom_call" | custom-call | flops 1000000000 | bytes 1314816 | tf_op jit(solution)/shard_map/pallas_call | solution.py:246
  15.4 0.1 collective-permute-done.6
  15.4 1.4 %collective-permute-done.5 = bf16[8,4224]{1,0:T(8,128)(2,1)S(1)} collective-permute-done((bf16[8,4224]{1,0:T(8,128)(2,1)S(1)}, bf16[8,4224]{1,0:T(8,128)(2,1)S(1)}, u32[]{:S(2)}, u32[]{:S(2)}) %collective-permute-start.5) | collective-permute-done | bytes 67616 | tf_op jit(solution)/shard_map/ppermute | solution.py:263
  16.8 0.0 collective-permute-done.4
  16.9 0.1 compare_select_fusion.2.held
  16.9 0.1 collective-permute-start.8
  17.0 1.2 %collective-permute-done.8.twin = bf16[8,4224]{1,0:T(8,128)(2,1)S(1)} collective-permute-done((bf16[8,4224]{1,0:T(8,128)(2,1)S(1)}, bf16[8,4224]{1,0:T(8,128)(2,1)S(1)}, u32[]{:S(2)}, u32[]{:S(2)}) %collective-permute-start.8) | collective-permute-done | bytes 67616 | tf_op jit(solution)/shard_map/ppermute | solution.py:263
  18.3 2.3 %shard_map.93 = f32[8,8,256]{2,1,0:T(8,128)} custom-call(bf16[8,4224]{1,0:T(8,128)(2,1)S(1)} %compare_select_fusion.2.held, bf16[8,4224]{1,0:T(8,128)(2,1)S(1)} %collective-permute-done.8.twin, bf16[64,768]{1,0:T(8,128)(2,1)S(1)} %get-tuple-element.43.white, f32[64,128]{1,0:T(8,128)S(1)} %get-tuple-element.44.masks, ...), custom_call_target="tpu_custom_call" | custom-call | flops 1000000000 | bytes 1445888 | tf_op jit(solution)/shard_map/pallas_call | solution.py:246
  (3 shorter events, 0.1 us)
Async XLA Ops:
  0.0 1.8 %collective-permute-start = (bf16[8,4096]{1,0:T(8,128)(2,1)}, bf16[8,4096]{1,0:T(8,128)(2,1)S(1)}, u32[]{:S(2)}, u32[]{:S(2)}) collective-permute-start(bf16[8,4096]{1,0:T(8,128)(2,1)} %raw.1), channel_id=1, source_target_pairs={{0,1},{1,0},{2,3},{3,2},{4,5},{5,4},{6,7},{7,6},{8,9},{9,8},{10,11... | collective-permute-start | bytes 196616 | tf_op jit(solution)/shard_map/ppermute | solution.py:263
  0.5 1.4 %collective-permute-start.1 = (s32[4,8]{1,0:T(4,128)}, s32[4,8]{1,0:T(4,128)S(1)}, u32[]{:S(2)}, u32[]{:S(2)}) collective-permute-start(s32[4,8]{1,0:T(4,128)} %bitcast.1), channel_id=1, source_target_pairs={{0,1},{1,0},{2,3},{3,2},{4,5},{5,4},{6,7},{7,6},{8,9},{9,8},{10,11... | collective-permute-start | bytes 392 | tf_op jit(solution)/shard_map/ppermute | solution.py:263
  1.9 6.5 %collective-permute-start.3 = (bf16[8,4224]{1,0:T(8,128)(2,1)S(1)}, bf16[8,4224]{1,0:T(8,128)(2,1)S(1)}, u32[]{:S(2)}, u32[]{:S(2)}) collective-permute-start(bf16[8,4224]{1,0:T(8,128)(2,1)S(1)} %fusion), channel_id=1, source_target_pairs={{0,8},{1,16},{2,10},{3,18},{4,12},{5,20},{6,14},{7,22},{8,0},{9,24... | collective-permute-start | bytes 202760 | tf_op jit(solution)/shard_map/ppermute | solution.py:279
  5.7 3.7 %collective-permute-start.2 = (bf16[8,4224]{1,0:T(8,128)(2,1)S(1)}, bf16[8,4224]{1,0:T(8,128)(2,1)S(1)}, u32[]{:S(2)}, u32[]{:S(2)}) collective-permute-start(bf16[8,4224]{1,0:T(8,128)(2,1)S(1)} %fusion), channel_id=1, source_target_pairs={{0,17},{1,24},{2,19},{3,26},{4,21},{5,28},{6,23},{7,30},{8,25},{9,... | collective-permute-start | bytes 202760 | tf_op jit(solution)/shard_map/ppermute | solution.py:279
  6.8 6.2 %collective-permute-start.7 = (bf16[8,4224]{1,0:T(8,128)(2,1)S(1)}, bf16[8,4224]{1,0:T(8,128)(2,1)S(1)}, u32[]{:S(2)}, u32[]{:S(2)}) collective-permute-start(bf16[8,4224]{1,0:T(8,128)(2,1)S(1)} %get-tuple-element.33.mine), channel_id=1, source_target_pairs={{0,16},{16,0},{1,17},{17,1},{2,18},{18,2},{3,19},{19,3},{4,20},{20... | collective-permute-start | bytes 202760 | tf_op jit(solution)/shard_map/ppermute | solution.py:263
  9.5 6.0 %collective-permute-start.6 = (bf16[8,4224]{1,0:T(8,128)(2,1)S(1)}, bf16[8,4224]{1,0:T(8,128)(2,1)S(1)}, u32[]{:S(2)}, u32[]{:S(2)}) collective-permute-start(bf16[8,4224]{1,0:T(8,128)(2,1)S(1)} %select_select_fusion), channel_id=1, source_target_pairs={{0,6},{1,7},{2,4},{3,5},{4,2},{5,3},{6,0},{7,1},{8,14},{9,15},{10,... | collective-permute-start | bytes 202760 | tf_op jit(solution)/shard_map/ppermute | solution.py:263
  12.2 4.7 %collective-permute-start.5 = (bf16[8,4224]{1,0:T(8,128)(2,1)S(1)}, bf16[8,4224]{1,0:T(8,128)(2,1)S(1)}, u32[]{:S(2)}, u32[]{:S(2)}) collective-permute-start(bf16[8,4224]{1,0:T(8,128)(2,1)S(1)} %select_select_fusion), channel_id=1, source_target_pairs={{0,4},{1,5},{2,6},{3,7},{4,0},{5,1},{6,2},{7,3},{8,12},{9,13},{10,... | collective-permute-start | bytes 202760 | tf_op jit(solution)/shard_map/ppermute | solution.py:263
  12.5 4.4 %collective-permute-start.4 = (bf16[8,4224]{1,0:T(8,128)(2,1)S(1)}, bf16[8,4224]{1,0:T(8,128)(2,1)S(1)}, u32[]{:S(2)}, u32[]{:S(2)}) collective-permute-start(bf16[8,4224]{1,0:T(8,128)(2,1)S(1)} %select_select_fusion), channel_id=1, source_target_pairs={{0,2},{1,3},{2,0},{3,1},{4,6},{5,7},{6,4},{7,5},{8,10},{9,11},{10,... | collective-permute-start | bytes 202760 | tf_op jit(solution)/shard_map/ppermute | solution.py:263
  16.9 1.3 %collective-permute-start.8 = (bf16[8,4224]{1,0:T(8,128)(2,1)S(1)}, bf16[8,4224]{1,0:T(8,128)(2,1)S(1)}, u32[]{:S(2)}, u32[]{:S(2)}) collective-permute-start(bf16[8,4224]{1,0:T(8,128)(2,1)S(1)} %compare_select_fusion.2.held), channel_id=1, source_target_pairs={{0,1},{1,0},{2,3},{3,2},{4,5},{5,4},{6,7},{7,6},{8,9},{9,8},{10,11... | collective-permute-start | bytes 202760 | tf_op jit(solution)/shard_map/ppermute | solution.py:263

commit v7 on v5

--- a/solution.py
+++ b/solution.py
@@ -262,6 +262,16 @@
     return lax.ppermute(x, axis, [(i, i ^ flip) for i in range(devices)])
 
 
+def exchange_by_class(x, one, two):
+    blocks = lax.axis_size("blk")
+    pairs = [
+        (s * blocks + b, s * blocks + (b ^ (one if s == b % 2 else two)))
+        for s in range(2)
+        for b in range(blocks)
+    ]
+    return lax.ppermute(x, ("section", "blk"), pairs)
+
+
 def crossing(x, bit):
     axes = ("section", "blk")
     blocks = lax.axis_size("blk")
@@ -319,7 +329,8 @@
     while bits:
         flips, bits = bits[:2], bits[2:]
         shifts = [flips[0] * k for k in range(1, 1 << len(flips))]
-        got = [exchange(held, k) for k in shifts]
+        turned = [*shifts[:2][::-1], *shifts[2:]]
+        got = [exchange_by_class(held, *k) for k in zip(shifts, turned)]
         if white is None:
             white, masks, *tables = call(
                 receivers,
@@ -332,8 +343,10 @@
             )
             *got, white, masks = lax.optimization_barrier((*got, white, masks))
         rel = away_wanted & sum(flips)
-        for k, piece in zip(shifts, got):
-            held = jnp.where(rel == k, piece, held)
+        one = two = held
+        for k, m, piece in zip(shifts, turned, got):
+            one, two = jnp.where(rel == k, piece, one), jnp.where(rel == m, piece, two)
+        held = jnp.where(core == section, one, two)
     twin = exchange(held, 1)
     return call(
         correlate,

time: 20.8 us -> 20.8 us (level)
    ppermute x0 -> x3, starting transfers between devices: none -> 3.55 us  [exchange_by_class(): return lax.ppermute(x, ('section', 'blk'), pairs)]
    ppermute x7 -> x4, starting transfers between devices: 5.66 us -> 2.1 us  [exchange(): return lax.ppermute(x, axis, [(i, i ^ flip) for i in range(devices)])]
    ppermute x0 -> x3, waiting for transfers between devices: none -> 1.53 us  [exchange_by_class(): return lax.ppermute(x, ('section', 'blk'), pairs)]
    ppermute x7 -> x4, waiting for transfers between devices: 3.16 us -> 1.67 us  [exchange(): return lax.ppermute(x, axis, [(i, i ^ flip) for i in range(devices)])]
  transfers between devices with their start and end apart: 9 -> 9, of which waited for: 5 -> 4; matrix products, arithmetic and copies ran while one was open for 0% -> 0% of each run, Pallas kernels for 16% -> 16%
where the time goes in v7:
time: 20.8 us; the launch traced here: 20.6 us
  starting transfers between devices  10.6 us (51%)
  Pallas kernels  5.55 us (27%)
  waiting for transfers between devices  4.24 us (20%)
    pallas_call x3, Pallas kernels, call(): pl.pallas_call(body, out_shape=out_shape, in_specs=in_specs, out_specs=ja...  5.55 us
    ppermute x2, starting transfers between devices, crossing(): return (lax.ppermute(x, axes, near), lax.ppermute(x, axes, far))  4.97 us
    ppermute x3, starting transfers between devices, exchange_by_class(): return lax.ppermute(x, ('section', 'blk'), pairs)  3.55 us
    ppermute x4, starting transfers between devices, exchange(): return lax.ppermute(x, axis, [(i, i ^ flip) for i in range(devices)])  2.1 us
    ppermute x4, waiting for transfers between devices, exchange(): return lax.ppermute(x, axis, [(i, i ^ flip) for i in range(devices)])  1.67 us
    ppermute x3, waiting for transfers between devices, exchange_by_class(): return lax.ppermute(x, ('section', 'blk'), pairs)  1.53 us
    ppermute x2, waiting for transfers between devices, crossing(): return (lax.ppermute(x, axes, near), lax.ppermute(x, axes, far))  1.04 us
  transfers between devices with their start and end apart: 9, of which 4 were waited for; matrix products, arithmetic and copies ran while one was open for 0% of the time, Pallas kernels for 16%

profile of v7, /device:TPU:0, one launch (start us, length us, event | category | flops | bytes accessed | tf_op | source)
XLA Modules:
  0.0 20.6 jit_solution(3561560579563205455)
XLA Ops:
  0.0 0.5 %collective-permute-start = (bf16[8,4096]{1,0:T(8,128)(2,1)}, bf16[8,4096]{1,0:T(8,128)(2,1)S(1)}, u32[]{:S(2)}, u32[]{:S(2)}) collective-permute-start(bf16[8,4096]{1,0:T(8,128)(2,1)} %raw.1), channel_id=1, source_target_pairs={{0,1},{1,0},{2,3},{3,2},{4,5},{5,4},{6,7},{7,6},{8,9},{9,8},{10,11... | collective-permute-start | bytes 196616 | tf_op jit(solution)/shard_map/ppermute | solution.py:262
  0.5 0.1 collective-permute-start.1
  0.5 0.9 %shard_map.91 = (bf16[8,4224]{1,0:T(8,128)(2,1)S(1)}, s32[8,4224]{1,0:T(8,128)S(1)}, s32[8,4224]{1,0:T(8,128)S(1)}) custom-call(bf16[8,4096]{1,0:T(8,128)(2,1)} %raw.1, s32[4,8]{1,0:T(4,128)} %bitcast.2, s32[16]{0:T(128)} %order.1), custom_call_target="tpu_custom_call" | custom-call | bytes 65728 | tf_op jit(solution)/shard_map/pallas_call | solution.py:245
  1.4 0.4 %collective-permute-done.1 = s32[4,8]{1,0:T(4,128)S(1)} collective-permute-done((s32[4,8]{1,0:T(4,128)}, s32[4,8]{1,0:T(4,128)S(1)}, u32[]{:S(2)}, u32[]{:S(2)}) %collective-permute-start.1) | collective-permute-done | bytes 160 | tf_op jit(solution)/shard_map/ppermute | solution.py:262
  1.8 0.0 collective-permute-done
  1.9 3.8 %collective-permute-start.3 = (bf16[8,4224]{1,0:T(8,128)(2,1)S(1)}, bf16[8,4224]{1,0:T(8,128)(2,1)S(1)}, u32[]{:S(2)}, u32[]{:S(2)}) collective-permute-start(bf16[8,4224]{1,0:T(8,128)(2,1)S(1)} %fusion), channel_id=1, source_target_pairs={{0,8},{1,16},{2,10},{3,18},{4,12},{5,20},{6,14},{7,22},{8,0},{9,24... | collective-permute-start | bytes 202760 | tf_op jit(solution)/shard_map/ppermute | solution.py:288
  5.7 1.2 %collective-permute-start.2 = (bf16[8,4224]{1,0:T(8,128)(2,1)S(1)}, bf16[8,4224]{1,0:T(8,128)(2,1)S(1)}, u32[]{:S(2)}, u32[]{:S(2)}) collective-permute-start(bf16[8,4224]{1,0:T(8,128)(2,1)S(1)} %fusion), channel_id=1, source_target_pairs={{0,17},{1,24},{2,19},{3,26},{4,21},{5,28},{6,23},{7,30},{8,25},{9,... | collective-permute-start | bytes 202760 | tf_op jit(solution)/shard_map/ppermute | solution.py:288
  6.8 1.5 %collective-permute-start.7 = (bf16[8,4224]{1,0:T(8,128)(2,1)S(1)}, bf16[8,4224]{1,0:T(8,128)(2,1)S(1)}, u32[]{:S(2)}, u32[]{:S(2)}) collective-permute-start(bf16[8,4224]{1,0:T(8,128)(2,1)S(1)} %get-tuple-element.33.mine), channel_id=1, source_target_pairs={{0,16},{16,0},{1,17},{17,1},{2,18},{18,2},{3,19},{19,3},{4,20},{20... | collective-permute-start | bytes 202760 | tf_op jit(solution)/shard_map/ppermute | solution.py:262
  8.4 0.0 collective-permute-done.3
  8.4 1.0 %collective-permute-done.2 = bf16[8,4224]{1,0:T(8,128)(2,1)S(1)} collective-permute-done((bf16[8,4224]{1,0:T(8,128)(2,1)S(1)}, bf16[8,4224]{1,0:T(8,128)(2,1)S(1)}, u32[]{:S(2)}, u32[]{:S(2)}) %collective-permute-start.2) | collective-permute-done | bytes 67616 | tf_op jit(solution)/shard_map/ppermute | solution.py:288
  9.5 2.7 %collective-permute-start.6 = (bf16[8,4224]{1,0:T(8,128)(2,1)S(1)}, bf16[8,4224]{1,0:T(8,128)(2,1)S(1)}, u32[]{:S(2)}, u32[]{:S(2)}) collective-permute-start(bf16[8,4224]{1,0:T(8,128)(2,1)S(1)} %select_select_fusion.1), channel_id=1, source_target_pairs={{0,6},{1,7},{2,4},{3,5},{4,2},{5,3},{6,0},{7,1},{8,14},{9,15},{10,... | collective-permute-start | bytes 202760 | tf_op jit(solution)/shard_map/ppermute | solution.py:272
  12.2 0.3 %collective-permute-start.5 = (bf16[8,4224]{1,0:T(8,128)(2,1)S(1)}, bf16[8,4224]{1,0:T(8,128)(2,1)S(1)}, u32[]{:S(2)}, u32[]{:S(2)}) collective-permute-start(bf16[8,4224]{1,0:T(8,128)(2,1)S(1)} %select_select_fusion.1), channel_id=1, source_target_pairs={{0,4},{1,3},{2,6},{3,1},{4,0},{5,7},{6,2},{7,5},{8,12},{9,11},{10,... | collective-permute-start | bytes 202760 | tf_op jit(solution)/shard_map/ppermute | solution.py:272
  12.5 0.5 %collective-permute-start.4 = (bf16[8,4224]{1,0:T(8,128)(2,1)S(1)}, bf16[8,4224]{1,0:T(8,128)(2,1)S(1)}, u32[]{:S(2)}, u32[]{:S(2)}) collective-permute-start(bf16[8,4224]{1,0:T(8,128)(2,1)S(1)} %select_select_fusion.1), channel_id=1, source_target_pairs={{0,2},{1,5},{2,0},{3,7},{4,6},{5,1},{6,4},{7,3},{8,10},{9,13},{10,... | collective-permute-start | bytes 202760 | tf_op jit(solution)/shard_map/ppermute | solution.py:272
  13.0 0.0 collective-permute-done.7.other
  13.0 2.4 %shard_map.92 = (bf16[64,768]{1,0:T(8,128)(2,1)S(1)}, f32[64,128]{1,0:T(8,128)S(1)}, bf16[384,256]{1,0:T(8,128)(2,1)S(1)}, bf16[384,128]{1,0:T(8,128)(2,1)S(1)},...) custom-call(bf16[8,4224]{1,0:T(8,128)(2,1)S(1)} %get-tuple-element.3, ...), custom_call_target="tpu_custom_call" | custom-call | flops 1000000000 | bytes 1314816 | tf_op jit(solution)/shard_map/pallas_call | solution.py:245
  15.4 0.0 collective-permute-done.6
  15.4 1.5 %collective-permute-done.5 = bf16[8,4224]{1,0:T(8,128)(2,1)S(1)} collective-permute-done((bf16[8,4224]{1,0:T(8,128)(2,1)S(1)}, bf16[8,4224]{1,0:T(8,128)(2,1)S(1)}, u32[]{:S(2)}, u32[]{:S(2)}) %collective-permute-start.5) | collective-permute-done | bytes 67616 | tf_op jit(solution)/shard_map/ppermute | solution.py:272
  16.9 0.0 collective-permute-done.4
  16.9 0.1 select_select_fusion.held
  17.0 0.1 collective-permute-start.8
  17.1 1.2 %collective-permute-done.8.twin = bf16[8,4224]{1,0:T(8,128)(2,1)S(1)} collective-permute-done((bf16[8,4224]{1,0:T(8,128)(2,1)S(1)}, bf16[8,4224]{1,0:T(8,128)(2,1)S(1)}, u32[]{:S(2)}, u32[]{:S(2)}) %collective-permute-start.8) | collective-permute-done | bytes 67616 | tf_op jit(solution)/shard_map/ppermute | solution.py:262
  18.3 2.3 %shard_map.93 = f32[8,8,256]{2,1,0:T(8,128)} custom-call(bf16[8,4224]{1,0:T(8,128)(2,1)S(1)} %select_select_fusion.held, bf16[8,4224]{1,0:T(8,128)(2,1)S(1)} %collective-permute-done.8.twin, bf16[64,768]{1,0:T(8,128)(2,1)S(1)} %get-tuple-element.43.white, f32[64,128]{1,0:T(8,128)S(1)} %get-tuple-element.44.masks, ...), custom_call_target="tpu_custom_call" | custom-call | flops 1000000000 | bytes 1445888 | tf_op jit(solution)/shard_map/pallas_call | solution.py:245
  (3 shorter events, 0.1 us)
Async XLA Ops:
  0.0 1.8 %collective-permute-start = (bf16[8,4096]{1,0:T(8,128)(2,1)}, bf16[8,4096]{1,0:T(8,128)(2,1)S(1)}, u32[]{:S(2)}, u32[]{:S(2)}) collective-permute-start(bf16[8,4096]{1,0:T(8,128)(2,1)} %raw.1), channel_id=1, source_target_pairs={{0,1},{1,0},{2,3},{3,2},{4,5},{5,4},{6,7},{7,6},{8,9},{9,8},{10,11... | collective-permute-start | bytes 196616 | tf_op jit(solution)/shard_map/ppermute | solution.py:262
  0.5 1.4 %collective-permute-start.1 = (s32[4,8]{1,0:T(4,128)}, s32[4,8]{1,0:T(4,128)S(1)}, u32[]{:S(2)}, u32[]{:S(2)}) collective-permute-start(s32[4,8]{1,0:T(4,128)} %bitcast.1), channel_id=1, source_target_pairs={{0,1},{1,0},{2,3},{3,2},{4,5},{5,4},{6,7},{7,6},{8,9},{9,8},{10,11... | collective-permute-start | bytes 392 | tf_op jit(solution)/shard_map/ppermute | solution.py:262
  1.9 6.5 %collective-permute-start.3 = (bf16[8,4224]{1,0:T(8,128)(2,1)S(1)}, bf16[8,4224]{1,0:T(8,128)(2,1)S(1)}, u32[]{:S(2)}, u32[]{:S(2)}) collective-permute-start(bf16[8,4224]{1,0:T(8,128)(2,1)S(1)} %fusion), channel_id=1, source_target_pairs={{0,8},{1,16},{2,10},{3,18},{4,12},{5,20},{6,14},{7,22},{8,0},{9,24... | collective-permute-start | bytes 202760 | tf_op jit(solution)/shard_map/ppermute | solution.py:288
  5.7 3.7 %collective-permute-start.2 = (bf16[8,4224]{1,0:T(8,128)(2,1)S(1)}, bf16[8,4224]{1,0:T(8,128)(2,1)S(1)}, u32[]{:S(2)}, u32[]{:S(2)}) collective-permute-start(bf16[8,4224]{1,0:T(8,128)(2,1)S(1)} %fusion), channel_id=1, source_target_pairs={{0,17},{1,24},{2,19},{3,26},{4,21},{5,28},{6,23},{7,30},{8,25},{9,... | collective-permute-start | bytes 202760 | tf_op jit(solution)/shard_map/ppermute | solution.py:288
  6.8 6.2 %collective-permute-start.7 = (bf16[8,4224]{1,0:T(8,128)(2,1)S(1)}, bf16[8,4224]{1,0:T(8,128)(2,1)S(1)}, u32[]{:S(2)}, u32[]{:S(2)}) collective-permute-start(bf16[8,4224]{1,0:T(8,128)(2,1)S(1)} %get-tuple-element.33.mine), channel_id=1, source_target_pairs={{0,16},{16,0},{1,17},{17,1},{2,18},{18,2},{3,19},{19,3},{4,20},{20... | collective-permute-start | bytes 202760 | tf_op jit(solution)/shard_map/ppermute | solution.py:262
  9.5 5.9 %collective-permute-start.6 = (bf16[8,4224]{1,0:T(8,128)(2,1)S(1)}, bf16[8,4224]{1,0:T(8,128)(2,1)S(1)}, u32[]{:S(2)}, u32[]{:S(2)}) collective-permute-start(bf16[8,4224]{1,0:T(8,128)(2,1)S(1)} %select_select_fusion.1), channel_id=1, source_target_pairs={{0,6},{1,7},{2,4},{3,5},{4,2},{5,3},{6,0},{7,1},{8,14},{9,15},{10,... | collective-permute-start | bytes 202760 | tf_op jit(solution)/shard_map/ppermute | solution.py:272
  12.2 4.7 %collective-permute-start.5 = (bf16[8,4224]{1,0:T(8,128)(2,1)S(1)}, bf16[8,4224]{1,0:T(8,128)(2,1)S(1)}, u32[]{:S(2)}, u32[]{:S(2)}) collective-permute-start(bf16[8,4224]{1,0:T(8,128)(2,1)S(1)} %select_select_fusion.1), channel_id=1, source_target_pairs={{0,4},{1,3},{2,6},{3,1},{4,0},{5,7},{6,2},{7,5},{8,12},{9,11},{10,... | collective-permute-start | bytes 202760 | tf_op jit(solution)/shard_map/ppermute | solution.py:272
  12.5 4.4 %collective-permute-start.4 = (bf16[8,4224]{1,0:T(8,128)(2,1)S(1)}, bf16[8,4224]{1,0:T(8,128)(2,1)S(1)}, u32[]{:S(2)}, u32[]{:S(2)}) collective-permute-start(bf16[8,4224]{1,0:T(8,128)(2,1)S(1)} %select_select_fusion.1), channel_id=1, source_target_pairs={{0,2},{1,5},{2,0},{3,7},{4,6},{5,1},{6,4},{7,3},{8,10},{9,13},{10,... | collective-permute-start | bytes 202760 | tf_op jit(solution)/shard_map/ppermute | solution.py:272
  17.0 1.3 %collective-permute-start.8 = (bf16[8,4224]{1,0:T(8,128)(2,1)S(1)}, bf16[8,4224]{1,0:T(8,128)(2,1)S(1)}, u32[]{:S(2)}, u32[]{:S(2)}) collective-permute-start(bf16[8,4224]{1,0:T(8,128)(2,1)S(1)} %select_select_fusion.held), channel_id=1, source_target_pairs={{0,1},{1,0},{2,3},{3,2},{4,5},{5,4},{6,7},{7,6},{8,9},{9,8},{10,11... | collective-permute-start | bytes 202760 | tf_op jit(solution)/shard_map/ppermute | solution.py:262

commit v8 on v7

--- a/solution.py
+++ b/solution.py
@@ -236,7 +236,7 @@
 HBM = pl.BlockSpec(memory_space=pltpu.HBM)
 
 
-def call(body, out_shape, in_specs, arrays, scratch=(), flops=0):
+def call(body, out_shape, in_specs, arrays, scratch=(), flops=0, fused=None):
     size = sum(a.size * a.dtype.itemsize for a in arrays)
     arrays = [
         pltpu.with_memory_space_constraint(a, pltpu.HBM) if spec is HBM else a
@@ -249,7 +249,7 @@
         out_specs=jax.tree.map(lambda _: VMEM, out_shape),
         scratch_shapes=scratch,
         cost_estimate=pl.CostEstimate(flops=flops, bytes_accessed=size, transcendentals=0),
-        compiler_params=pltpu.CompilerParams(vmem_limit_bytes=16 * 1024 * 1024),
+        compiler_params=pltpu.CompilerParams(vmem_limit_bytes=16 * 1024 * 1024, allow_input_fusion=fused),
     )(*arrays)
 
 
@@ -354,6 +354,7 @@
         [VMEM] * 10,
         [held, twin, white, masks, *tables],
         flops=10**9,
+        fused=[True] + [False] * 9,
     )
 
 

time: 20.8 us -> 20.8 us (level)
  no operation moved by 1% of the time
where the time goes in v8:
time: 20.8 us; the launch traced here: 20.6 us
  starting transfers between devices  10.6 us (51%)
  Pallas kernels  5.55 us (27%)
  waiting for transfers between devices  4.24 us (20%)
    pallas_call x3, Pallas kernels, call(): pl.pallas_call(body, out_shape=out_shape, in_specs=in_specs, out_specs=ja...  5.55 us
    ppermute x2, starting transfers between devices, crossing(): return (lax.ppermute(x, axes, near), lax.ppermute(x, axes, far))  4.97 us
    ppermute x3, starting transfers between devices, exchange_by_class(): return lax.ppermute(x, ('section', 'blk'), pairs)  3.55 us
    ppermute x4, starting transfers between devices, exchange(): return lax.ppermute(x, axis, [(i, i ^ flip) for i in range(devices)])  2.1 us
    ppermute x4, waiting for transfers between devices, exchange(): return lax.ppermute(x, axis, [(i, i ^ flip) for i in range(devices)])  1.67 us
    ppermute x3, waiting for transfers between devices, exchange_by_class(): return lax.ppermute(x, ('section', 'blk'), pairs)  1.53 us
    ppermute x2, waiting for transfers between devices, crossing(): return (lax.ppermute(x, axes, near), lax.ppermute(x, axes, far))  1.04 us
  transfers between devices with their start and end apart: 9, of which 4 were waited for; matrix products, arithmetic and copies ran while one was open for 0% of the time, Pallas kernels for 16%

profile of v8, /device:TPU:0, one launch (start us, length us, event | category | flops | bytes accessed | tf_op | source)
XLA Modules:
  0.0 20.6 jit_solution(3561560579563205455)
XLA Ops:
  0.0 0.5 %collective-permute-start = (bf16[8,4096]{1,0:T(8,128)(2,1)}, bf16[8,4096]{1,0:T(8,128)(2,1)S(1)}, u32[]{:S(2)}, u32[]{:S(2)}) collective-permute-start(bf16[8,4096]{1,0:T(8,128)(2,1)} %raw.1), channel_id=1, source_target_pairs={{0,1},{1,0},{2,3},{3,2},{4,5},{5,4},{6,7},{7,6},{8,9},{9,8},{10,11... | collective-permute-start | bytes 196616 | tf_op jit(solution)/shard_map/ppermute | solution.py:262
  0.5 0.1 collective-permute-start.1
  0.5 0.9 %shard_map.91 = (bf16[8,4224]{1,0:T(8,128)(2,1)S(1)}, s32[8,4224]{1,0:T(8,128)S(1)}, s32[8,4224]{1,0:T(8,128)S(1)}) custom-call(bf16[8,4096]{1,0:T(8,128)(2,1)} %raw.1, s32[4,8]{1,0:T(4,128)} %bitcast.2, s32[16]{0:T(128)} %order.1), custom_call_target="tpu_custom_call" | custom-call | bytes 65728 | tf_op jit(solution)/shard_map/pallas_call | solution.py:245
  1.4 0.4 %collective-permute-done.1 = s32[4,8]{1,0:T(4,128)S(1)} collective-permute-done((s32[4,8]{1,0:T(4,128)}, s32[4,8]{1,0:T(4,128)S(1)}, u32[]{:S(2)}, u32[]{:S(2)}) %collective-permute-start.1) | collective-permute-done | bytes 160 | tf_op jit(solution)/shard_map/ppermute | solution.py:262
  1.8 0.0 collective-permute-done
  1.9 3.8 %collective-permute-start.3 = (bf16[8,4224]{1,0:T(8,128)(2,1)S(1)}, bf16[8,4224]{1,0:T(8,128)(2,1)S(1)}, u32[]{:S(2)}, u32[]{:S(2)}) collective-permute-start(bf16[8,4224]{1,0:T(8,128)(2,1)S(1)} %fusion), channel_id=1, source_target_pairs={{0,8},{1,16},{2,10},{3,18},{4,12},{5,20},{6,14},{7,22},{8,0},{9,24... | collective-permute-start | bytes 202760 | tf_op jit(solution)/shard_map/ppermute | solution.py:288
  5.7 1.2 %collective-permute-start.2 = (bf16[8,4224]{1,0:T(8,128)(2,1)S(1)}, bf16[8,4224]{1,0:T(8,128)(2,1)S(1)}, u32[]{:S(2)}, u32[]{:S(2)}) collective-permute-start(bf16[8,4224]{1,0:T(8,128)(2,1)S(1)} %fusion), channel_id=1, source_target_pairs={{0,17},{1,24},{2,19},{3,26},{4,21},{5,28},{6,23},{7,30},{8,25},{9,... | collective-permute-start | bytes 202760 | tf_op jit(solution)/shard_map/ppermute | solution.py:288
  6.8 1.5 %collective-permute-start.7 = (bf16[8,4224]{1,0:T(8,128)(2,1)S(1)}, bf16[8,4224]{1,0:T(8,128)(2,1)S(1)}, u32[]{:S(2)}, u32[]{:S(2)}) collective-permute-start(bf16[8,4224]{1,0:T(8,128)(2,1)S(1)} %get-tuple-element.33.mine), channel_id=1, source_target_pairs={{0,16},{16,0},{1,17},{17,1},{2,18},{18,2},{3,19},{19,3},{4,20},{20... | collective-permute-start | bytes 202760 | tf_op jit(solution)/shard_map/ppermute | solution.py:262
  8.4 0.0 collective-permute-done.3
  8.4 1.0 %collective-permute-done.2 = bf16[8,4224]{1,0:T(8,128)(2,1)S(1)} collective-permute-done((bf16[8,4224]{1,0:T(8,128)(2,1)S(1)}, bf16[8,4224]{1,0:T(8,128)(2,1)S(1)}, u32[]{:S(2)}, u32[]{:S(2)}) %collective-permute-start.2) | collective-permute-done | bytes 67616 | tf_op jit(solution)/shard_map/ppermute | solution.py:288
  9.5 2.7 %collective-permute-start.6 = (bf16[8,4224]{1,0:T(8,128)(2,1)S(1)}, bf16[8,4224]{1,0:T(8,128)(2,1)S(1)}, u32[]{:S(2)}, u32[]{:S(2)}) collective-permute-start(bf16[8,4224]{1,0:T(8,128)(2,1)S(1)} %select_select_fusion.1), channel_id=1, source_target_pairs={{0,6},{1,7},{2,4},{3,5},{4,2},{5,3},{6,0},{7,1},{8,14},{9,15},{10,... | collective-permute-start | bytes 202760 | tf_op jit(solution)/shard_map/ppermute | solution.py:272
  12.2 0.3 %collective-permute-start.5 = (bf16[8,4224]{1,0:T(8,128)(2,1)S(1)}, bf16[8,4224]{1,0:T(8,128)(2,1)S(1)}, u32[]{:S(2)}, u32[]{:S(2)}) collective-permute-start(bf16[8,4224]{1,0:T(8,128)(2,1)S(1)} %select_select_fusion.1), channel_id=1, source_target_pairs={{0,4},{1,3},{2,6},{3,1},{4,0},{5,7},{6,2},{7,5},{8,12},{9,11},{10,... | collective-permute-start | bytes 202760 | tf_op jit(solution)/shard_map/ppermute | solution.py:272
  12.5 0.5 %collective-permute-start.4 = (bf16[8,4224]{1,0:T(8,128)(2,1)S(1)}, bf16[8,4224]{1,0:T(8,128)(2,1)S(1)}, u32[]{:S(2)}, u32[]{:S(2)}) collective-permute-start(bf16[8,4224]{1,0:T(8,128)(2,1)S(1)} %select_select_fusion.1), channel_id=1, source_target_pairs={{0,2},{1,5},{2,0},{3,7},{4,6},{5,1},{6,4},{7,3},{8,10},{9,13},{10,... | collective-permute-start | bytes 202760 | tf_op jit(solution)/shard_map/ppermute | solution.py:272
  13.0 0.0 collective-permute-done.7.other
  13.0 2.4 %shard_map.92 = (bf16[64,768]{1,0:T(8,128)(2,1)S(1)}, f32[64,128]{1,0:T(8,128)S(1)}, bf16[384,256]{1,0:T(8,128)(2,1)S(1)}, bf16[384,128]{1,0:T(8,128)(2,1)S(1)},...) custom-call(bf16[8,4224]{1,0:T(8,128)(2,1)S(1)} %get-tuple-element.3, ...), custom_call_target="tpu_custom_call" | custom-call | flops 1000000000 | bytes 1314816 | tf_op jit(solution)/shard_map/pallas_call | solution.py:245
  15.4 0.0 collective-permute-done.6
  15.4 1.5 %collective-permute-done.5 = bf16[8,4224]{1,0:T(8,128)(2,1)S(1)} collective-permute-done((bf16[8,4224]{1,0:T(8,128)(2,1)S(1)}, bf16[8,4224]{1,0:T(8,128)(2,1)S(1)}, u32[]{:S(2)}, u32[]{:S(2)}) %collective-permute-start.5) | collective-permute-done | bytes 67616 | tf_op jit(solution)/shard_map/ppermute | solution.py:272
  16.9 0.0 collective-permute-done.4
  16.9 0.1 select_select_fusion.held
  17.0 0.1 collective-permute-start.8
  17.1 1.2 %collective-permute-done.8.twin = bf16[8,4224]{1,0:T(8,128)(2,1)S(1)} collective-permute-done((bf16[8,4224]{1,0:T(8,128)(2,1)S(1)}, bf16[8,4224]{1,0:T(8,128)(2,1)S(1)}, u32[]{:S(2)}, u32[]{:S(2)}) %collective-permute-start.8) | collective-permute-done | bytes 67616 | tf_op jit(solution)/shard_map/ppermute | solution.py:262
  18.3 2.3 %shard_map.93 = f32[8,8,256]{2,1,0:T(8,128)} custom-call(bf16[8,4224]{1,0:T(8,128)(2,1)S(1)} %select_select_fusion.held, bf16[8,4224]{1,0:T(8,128)(2,1)S(1)} %collective-permute-done.8.twin, bf16[64,768]{1,0:T(8,128)(2,1)S(1)} %get-tuple-element.43.white, f32[64,128]{1,0:T(8,128)S(1)} %get-tuple-element.44.masks, ...), custom_call_target="tpu_custom_call" | custom-call | flops 1000000000 | bytes 1445888 | tf_op jit(solution)/shard_map/pallas_call | solution.py:245
  (3 shorter events, 0.1 us)
Async XLA Ops:
  0.0 1.8 %collective-permute-start = (bf16[8,4096]{1,0:T(8,128)(2,1)}, bf16[8,4096]{1,0:T(8,128)(2,1)S(1)}, u32[]{:S(2)}, u32[]{:S(2)}) collective-permute-start(bf16[8,4096]{1,0:T(8,128)(2,1)} %raw.1), channel_id=1, source_target_pairs={{0,1},{1,0},{2,3},{3,2},{4,5},{5,4},{6,7},{7,6},{8,9},{9,8},{10,11... | collective-permute-start | bytes 196616 | tf_op jit(solution)/shard_map/ppermute | solution.py:262
  0.5 1.4 %collective-permute-start.1 = (s32[4,8]{1,0:T(4,128)}, s32[4,8]{1,0:T(4,128)S(1)}, u32[]{:S(2)}, u32[]{:S(2)}) collective-permute-start(s32[4,8]{1,0:T(4,128)} %bitcast.1), channel_id=1, source_target_pairs={{0,1},{1,0},{2,3},{3,2},{4,5},{5,4},{6,7},{7,6},{8,9},{9,8},{10,11... | collective-permute-start | bytes 392 | tf_op jit(solution)/shard_map/ppermute | solution.py:262
  1.9 6.5 %collective-permute-start.3 = (bf16[8,4224]{1,0:T(8,128)(2,1)S(1)}, bf16[8,4224]{1,0:T(8,128)(2,1)S(1)}, u32[]{:S(2)}, u32[]{:S(2)}) collective-permute-start(bf16[8,4224]{1,0:T(8,128)(2,1)S(1)} %fusion), channel_id=1, source_target_pairs={{0,8},{1,16},{2,10},{3,18},{4,12},{5,20},{6,14},{7,22},{8,0},{9,24... | collective-permute-start | bytes 202760 | tf_op jit(solution)/shard_map/ppermute | solution.py:288
  5.7 3.7 %collective-permute-start.2 = (bf16[8,4224]{1,0:T(8,128)(2,1)S(1)}, bf16[8,4224]{1,0:T(8,128)(2,1)S(1)}, u32[]{:S(2)}, u32[]{:S(2)}) collective-permute-start(bf16[8,4224]{1,0:T(8,128)(2,1)S(1)} %fusion), channel_id=1, source_target_pairs={{0,17},{1,24},{2,19},{3,26},{4,21},{5,28},{6,23},{7,30},{8,25},{9,... | collective-permute-start | bytes 202760 | tf_op jit(solution)/shard_map/ppermute | solution.py:288
  6.8 6.2 %collective-permute-start.7 = (bf16[8,4224]{1,0:T(8,128)(2,1)S(1)}, bf16[8,4224]{1,0:T(8,128)(2,1)S(1)}, u32[]{:S(2)}, u32[]{:S(2)}) collective-permute-start(bf16[8,4224]{1,0:T(8,128)(2,1)S(1)} %get-tuple-element.33.mine), channel_id=1, source_target_pairs={{0,16},{16,0},{1,17},{17,1},{2,18},{18,2},{3,19},{19,3},{4,20},{20... | collective-permute-start | bytes 202760 | tf_op jit(solution)/shard_map/ppermute | solution.py:262
  9.5 5.9 %collective-permute-start.6 = (bf16[8,4224]{1,0:T(8,128)(2,1)S(1)}, bf16[8,4224]{1,0:T(8,128)(2,1)S(1)}, u32[]{:S(2)}, u32[]{:S(2)}) collective-permute-start(bf16[8,4224]{1,0:T(8,128)(2,1)S(1)} %select_select_fusion.1), channel_id=1, source_target_pairs={{0,6},{1,7},{2,4},{3,5},{4,2},{5,3},{6,0},{7,1},{8,14},{9,15},{10,... | collective-permute-start | bytes 202760 | tf_op jit(solution)/shard_map/ppermute | solution.py:272
  12.2 4.7 %collective-permute-start.5 = (bf16[8,4224]{1,0:T(8,128)(2,1)S(1)}, bf16[8,4224]{1,0:T(8,128)(2,1)S(1)}, u32[]{:S(2)}, u32[]{:S(2)}) collective-permute-start(bf16[8,4224]{1,0:T(8,128)(2,1)S(1)} %select_select_fusion.1), channel_id=1, source_target_pairs={{0,4},{1,3},{2,6},{3,1},{4,0},{5,7},{6,2},{7,5},{8,12},{9,11},{10,... | collective-permute-start | bytes 202760 | tf_op jit(solution)/shard_map/ppermute | solution.py:272
  12.5 4.4 %collective-permute-start.4 = (bf16[8,4224]{1,0:T(8,128)(2,1)S(1)}, bf16[8,4224]{1,0:T(8,128)(2,1)S(1)}, u32[]{:S(2)}, u32[]{:S(2)}) collective-permute-start(bf16[8,4224]{1,0:T(8,128)(2,1)S(1)} %select_select_fusion.1), channel_id=1, source_target_pairs={{0,2},{1,5},{2,0},{3,7},{4,6},{5,1},{6,4},{7,3},{8,10},{9,13},{10,... | collective-permute-start | bytes 202760 | tf_op jit(solution)/shard_map/ppermute | solution.py:272
  17.0 1.3 %collective-permute-start.8 = (bf16[8,4224]{1,0:T(8,128)(2,1)S(1)}, bf16[8,4224]{1,0:T(8,128)(2,1)S(1)}, u32[]{:S(2)}, u32[]{:S(2)}) collective-permute-start(bf16[8,4224]{1,0:T(8,128)(2,1)S(1)} %select_select_fusion.held), channel_id=1, source_target_pairs={{0,1},{1,0},{2,3},{3,2},{4,5},{5,4},{6,7},{7,6},{8,9},{9,8},{10,11... | collective-permute-start | bytes 202760 | tf_op jit(solution)/shard_map/ppermute | solution.py:262

commit v9 on v5

--- a/solution.py
+++ b/solution.py
@@ -228,7 +228,7 @@
     both = dot(jnp.concatenate([high, low], axis=0), lag_high[...])
     lagged = both[: 2 * size] + both[2 * size :] + dot(high, lag_low[...])
     lagged = jnp.concatenate([lagged[:size], lagged[size:]], axis=1)
-    lagged = lagged / jnp.maximum(jnp.concatenate(counts, axis=0), 1.0)
+    lagged = lagged * (1.0 / jnp.maximum(jnp.concatenate(counts, axis=0), 1.0))
     out[...] = lagged.reshape(ST, ST, LAGS)
 
 

time: 20.8 us -> 20.8 us (level)
  no operation moved by 1% of the time
where the time goes in v9:
time: 20.8 us; the launch traced here: 20.6 us
  starting transfers between devices  10.6 us (51%)
  Pallas kernels  5.55 us (27%)
  waiting for transfers between devices  4.2 us (20%)
    ppermute x7, starting transfers between devices, exchange(): return lax.ppermute(x, axis, [(i, i ^ flip) for i in range(devices)])  5.66 us
    pallas_call x3, Pallas kernels, call(): pl.pallas_call(body, out_shape=out_shape, in_specs=in_specs, out_specs=ja...  5.55 us
    ppermute x2, starting transfers between devices, crossing(): return (lax.ppermute(x, axes, near), lax.ppermute(x, axes, far))  4.97 us
    ppermute x7, waiting for transfers between devices, exchange(): return lax.ppermute(x, axis, [(i, i ^ flip) for i in range(devices)])  3.16 us
    ppermute x2, waiting for transfers between devices, crossing(): return (lax.ppermute(x, axes, near), lax.ppermute(x, axes, far))  1.04 us
  transfers between devices with their start and end apart: 9, of which 5 were waited for; matrix products, arithmetic and copies ran while one was open for 0% of the time, Pallas kernels for 16%

profile of v9, /device:TPU:0, one launch (start us, length us, event | category | flops | bytes accessed | tf_op | source)
XLA Modules:
  0.0 20.6 jit_solution(4324100553142382366)
XLA Ops:
  0.0 0.5 %collective-permute-start = (bf16[8,4096]{1,0:T(8,128)(2,1)}, bf16[8,4096]{1,0:T(8,128)(2,1)S(1)}, u32[]{:S(2)}, u32[]{:S(2)}) collective-permute-start(bf16[8,4096]{1,0:T(8,128)(2,1)} %raw.1), channel_id=1, source_target_pairs={{0,1},{1,0},{2,3},{3,2},{4,5},{5,4},{6,7},{7,6},{8,9},{9,8},{10,11... | collective-permute-start | bytes 196616 | tf_op jit(solution)/shard_map/ppermute | solution.py:262
  0.5 0.1 collective-permute-start.1
  0.5 0.9 %shard_map.91 = (bf16[8,4224]{1,0:T(8,128)(2,1)S(1)}, s32[8,4224]{1,0:T(8,128)S(1)}, s32[8,4224]{1,0:T(8,128)S(1)}) custom-call(bf16[8,4096]{1,0:T(8,128)(2,1)} %raw.1, s32[4,8]{1,0:T(4,128)} %bitcast.2, s32[16]{0:T(128)} %order.1), custom_call_target="tpu_custom_call" | custom-call | bytes 65728 | tf_op jit(solution)/shard_map/pallas_call | solution.py:245
  1.4 0.4 %collective-permute-done.1 = s32[4,8]{1,0:T(4,128)S(1)} collective-permute-done((s32[4,8]{1,0:T(4,128)}, s32[4,8]{1,0:T(4,128)S(1)}, u32[]{:S(2)}, u32[]{:S(2)}) %collective-permute-start.1) | collective-permute-done | bytes 160 | tf_op jit(solution)/shard_map/ppermute | solution.py:262
  1.8 0.0 collective-permute-done
  1.9 3.8 %collective-permute-start.3 = (bf16[8,4224]{1,0:T(8,128)(2,1)S(1)}, bf16[8,4224]{1,0:T(8,128)(2,1)S(1)}, u32[]{:S(2)}, u32[]{:S(2)}) collective-permute-start(bf16[8,4224]{1,0:T(8,128)(2,1)S(1)} %fusion), channel_id=1, source_target_pairs={{0,8},{1,16},{2,10},{3,18},{4,12},{5,20},{6,14},{7,22},{8,0},{9,24... | collective-permute-start | bytes 202760 | tf_op jit(solution)/shard_map/ppermute | solution.py:278
  5.7 1.2 %collective-permute-start.2 = (bf16[8,4224]{1,0:T(8,128)(2,1)S(1)}, bf16[8,4224]{1,0:T(8,128)(2,1)S(1)}, u32[]{:S(2)}, u32[]{:S(2)}) collective-permute-start(bf16[8,4224]{1,0:T(8,128)(2,1)S(1)} %fusion), channel_id=1, source_target_pairs={{0,17},{1,24},{2,19},{3,26},{4,21},{5,28},{6,23},{7,30},{8,25},{9,... | collective-permute-start | bytes 202760 | tf_op jit(solution)/shard_map/ppermute | solution.py:278
  6.8 1.5 %collective-permute-start.7 = (bf16[8,4224]{1,0:T(8,128)(2,1)S(1)}, bf16[8,4224]{1,0:T(8,128)(2,1)S(1)}, u32[]{:S(2)}, u32[]{:S(2)}) collective-permute-start(bf16[8,4224]{1,0:T(8,128)(2,1)S(1)} %get-tuple-element.33.mine), channel_id=1, source_target_pairs={{0,16},{16,0},{1,17},{17,1},{2,18},{18,2},{3,19},{19,3},{4,20},{20... | collective-permute-start | bytes 202760 | tf_op jit(solution)/shard_map/ppermute | solution.py:262
  8.4 0.0 collective-permute-done.3
  8.4 1.0 %collective-permute-done.2 = bf16[8,4224]{1,0:T(8,128)(2,1)S(1)} collective-permute-done((bf16[8,4224]{1,0:T(8,128)(2,1)S(1)}, bf16[8,4224]{1,0:T(8,128)(2,1)S(1)}, u32[]{:S(2)}, u32[]{:S(2)}) %collective-permute-start.2) | collective-permute-done | bytes 67616 | tf_op jit(solution)/shard_map/ppermute | solution.py:278
  9.5 2.7 %collective-permute-start.6 = (bf16[8,4224]{1,0:T(8,128)(2,1)S(1)}, bf16[8,4224]{1,0:T(8,128)(2,1)S(1)}, u32[]{:S(2)}, u32[]{:S(2)}) collective-permute-start(bf16[8,4224]{1,0:T(8,128)(2,1)S(1)} %select_select_fusion), channel_id=1, source_target_pairs={{0,6},{1,7},{2,4},{3,5},{4,2},{5,3},{6,0},{7,1},{8,14},{9,15},{10,... | collective-permute-start | bytes 202760 | tf_op jit(solution)/shard_map/ppermute | solution.py:262
  12.2 0.3 %collective-permute-start.5 = (bf16[8,4224]{1,0:T(8,128)(2,1)S(1)}, bf16[8,4224]{1,0:T(8,128)(2,1)S(1)}, u32[]{:S(2)}, u32[]{:S(2)}) collective-permute-start(bf16[8,4224]{1,0:T(8,128)(2,1)S(1)} %select_select_fusion), channel_id=1, source_target_pairs={{0,4},{1,5},{2,6},{3,7},{4,0},{5,1},{6,2},{7,3},{8,12},{9,13},{10,... | collective-permute-start | bytes 202760 | tf_op jit(solution)/shard_map/ppermute | solution.py:262
  12.5 0.5 %collective-permute-start.4 = (bf16[8,4224]{1,0:T(8,128)(2,1)S(1)}, bf16[8,4224]{1,0:T(8,128)(2,1)S(1)}, u32[]{:S(2)}, u32[]{:S(2)}) collective-permute-start(bf16[8,4224]{1,0:T(8,128)(2,1)S(1)} %select_select_fusion), channel_id=1, source_target_pairs={{0,2},{1,3},{2,0},{3,1},{4,6},{5,7},{6,4},{7,5},{8,10},{9,11},{10,... | collective-permute-start | bytes 202760 | tf_op jit(solution)/shard_map/ppermute | solution.py:262
  13.0 0.0 collective-permute-done.7.other
  13.0 2.4 %shard_map.92 = (bf16[64,768]{1,0:T(8,128)(2,1)S(1)}, f32[64,128]{1,0:T(8,128)S(1)}, bf16[384,256]{1,0:T(8,128)(2,1)S(1)}, bf16[384,128]{1,0:T(8,128)(2,1)S(1)},...) custom-call(bf16[8,4224]{1,0:T(8,128)(2,1)S(1)} %get-tuple-element.3, ...), custom_call_target="tpu_custom_call" | custom-call | flops 1000000000 | bytes 1314816 | tf_op jit(solution)/shard_map/pallas_call | solution.py:245
  15.4 0.1 collective-permute-done.6
  15.4 1.4 %collective-permute-done.5 = bf16[8,4224]{1,0:T(8,128)(2,1)S(1)} collective-permute-done((bf16[8,4224]{1,0:T(8,128)(2,1)S(1)}, bf16[8,4224]{1,0:T(8,128)(2,1)S(1)}, u32[]{:S(2)}, u32[]{:S(2)}) %collective-permute-start.5) | collective-permute-done | bytes 67616 | tf_op jit(solution)/shard_map/ppermute | solution.py:262
  16.8 0.0 collective-permute-done.4
  16.9 0.1 compare_select_fusion.2.held
  16.9 0.1 collective-permute-start.8
  17.0 1.2 %collective-permute-done.8.twin = bf16[8,4224]{1,0:T(8,128)(2,1)S(1)} collective-permute-done((bf16[8,4224]{1,0:T(8,128)(2,1)S(1)}, bf16[8,4224]{1,0:T(8,128)(2,1)S(1)}, u32[]{:S(2)}, u32[]{:S(2)}) %collective-permute-start.8) | collective-permute-done | bytes 67616 | tf_op jit(solution)/shard_map/ppermute | solution.py:262
  18.3 2.3 %shard_map.93 = f32[8,8,256]{2,1,0:T(8,128)} custom-call(bf16[8,4224]{1,0:T(8,128)(2,1)S(1)} %compare_select_fusion.2.held, bf16[8,4224]{1,0:T(8,128)(2,1)S(1)} %collective-permute-done.8.twin, bf16[64,768]{1,0:T(8,128)(2,1)S(1)} %get-tuple-element.43.white, f32[64,128]{1,0:T(8,128)S(1)} %get-tuple-element.44.masks, ...), custom_call_target="tpu_custom_call" | custom-call | flops 1000000000 | bytes 1445888 | tf_op jit(solution)/shard_map/pallas_call | solution.py:245
  (3 shorter events, 0.1 us)
Async XLA Ops:
  0.0 1.8 %collective-permute-start = (bf16[8,4096]{1,0:T(8,128)(2,1)}, bf16[8,4096]{1,0:T(8,128)(2,1)S(1)}, u32[]{:S(2)}, u32[]{:S(2)}) collective-permute-start(bf16[8,4096]{1,0:T(8,128)(2,1)} %raw.1), channel_id=1, source_target_pairs={{0,1},{1,0},{2,3},{3,2},{4,5},{5,4},{6,7},{7,6},{8,9},{9,8},{10,11... | collective-permute-start | bytes 196616 | tf_op jit(solution)/shard_map/ppermute | solution.py:262
  0.5 1.4 %collective-permute-start.1 = (s32[4,8]{1,0:T(4,128)}, s32[4,8]{1,0:T(4,128)S(1)}, u32[]{:S(2)}, u32[]{:S(2)}) collective-permute-start(s32[4,8]{1,0:T(4,128)} %bitcast.1), channel_id=1, source_target_pairs={{0,1},{1,0},{2,3},{3,2},{4,5},{5,4},{6,7},{7,6},{8,9},{9,8},{10,11... | collective-permute-start | bytes 392 | tf_op jit(solution)/shard_map/ppermute | solution.py:262
  1.9 6.5 %collective-permute-start.3 = (bf16[8,4224]{1,0:T(8,128)(2,1)S(1)}, bf16[8,4224]{1,0:T(8,128)(2,1)S(1)}, u32[]{:S(2)}, u32[]{:S(2)}) collective-permute-start(bf16[8,4224]{1,0:T(8,128)(2,1)S(1)} %fusion), channel_id=1, source_target_pairs={{0,8},{1,16},{2,10},{3,18},{4,12},{5,20},{6,14},{7,22},{8,0},{9,24... | collective-permute-start | bytes 202760 | tf_op jit(solution)/shard_map/ppermute | solution.py:278
  5.7 3.7 %collective-permute-start.2 = (bf16[8,4224]{1,0:T(8,128)(2,1)S(1)}, bf16[8,4224]{1,0:T(8,128)(2,1)S(1)}, u32[]{:S(2)}, u32[]{:S(2)}) collective-permute-start(bf16[8,4224]{1,0:T(8,128)(2,1)S(1)} %fusion), channel_id=1, source_target_pairs={{0,17},{1,24},{2,19},{3,26},{4,21},{5,28},{6,23},{7,30},{8,25},{9,... | collective-permute-start | bytes 202760 | tf_op jit(solution)/shard_map/ppermute | solution.py:278
  6.8 6.2 %collective-permute-start.7 = (bf16[8,4224]{1,0:T(8,128)(2,1)S(1)}, bf16[8,4224]{1,0:T(8,128)(2,1)S(1)}, u32[]{:S(2)}, u32[]{:S(2)}) collective-permute-start(bf16[8,4224]{1,0:T(8,128)(2,1)S(1)} %get-tuple-element.33.mine), channel_id=1, source_target_pairs={{0,16},{16,0},{1,17},{17,1},{2,18},{18,2},{3,19},{19,3},{4,20},{20... | collective-permute-start | bytes 202760 | tf_op jit(solution)/shard_map/ppermute | solution.py:262
  9.5 6.0 %collective-permute-start.6 = (bf16[8,4224]{1,0:T(8,128)(2,1)S(1)}, bf16[8,4224]{1,0:T(8,128)(2,1)S(1)}, u32[]{:S(2)}, u32[]{:S(2)}) collective-permute-start(bf16[8,4224]{1,0:T(8,128)(2,1)S(1)} %select_select_fusion), channel_id=1, source_target_pairs={{0,6},{1,7},{2,4},{3,5},{4,2},{5,3},{6,0},{7,1},{8,14},{9,15},{10,... | collective-permute-start | bytes 202760 | tf_op jit(solution)/shard_map/ppermute | solution.py:262
  12.2 4.7 %collective-permute-start.5 = (bf16[8,4224]{1,0:T(8,128)(2,1)S(1)}, bf16[8,4224]{1,0:T(8,128)(2,1)S(1)}, u32[]{:S(2)}, u32[]{:S(2)}) collective-permute-start(bf16[8,4224]{1,0:T(8,128)(2,1)S(1)} %select_select_fusion), channel_id=1, source_target_pairs={{0,4},{1,5},{2,6},{3,7},{4,0},{5,1},{6,2},{7,3},{8,12},{9,13},{10,... | collective-permute-start | bytes 202760 | tf_op jit(solution)/shard_map/ppermute | solution.py:262
  12.5 4.4 %collective-permute-start.4 = (bf16[8,4224]{1,0:T(8,128)(2,1)S(1)}, bf16[8,4224]{1,0:T(8,128)(2,1)S(1)}, u32[]{:S(2)}, u32[]{:S(2)}) collective-permute-start(bf16[8,4224]{1,0:T(8,128)(2,1)S(1)} %select_select_fusion), channel_id=1, source_target_pairs={{0,2},{1,3},{2,0},{3,1},{4,6},{5,7},{6,4},{7,5},{8,10},{9,11},{10,... | collective-permute-start | bytes 202760 | tf_op jit(solution)/shard_map/ppermute | solution.py:262
  16.9 1.3 %collective-permute-start.8 = (bf16[8,4224]{1,0:T(8,128)(2,1)S(1)}, bf16[8,4224]{1,0:T(8,128)(2,1)S(1)}, u32[]{:S(2)}, u32[]{:S(2)}) collective-permute-start(bf16[8,4224]{1,0:T(8,128)(2,1)S(1)} %compare_select_fusion.2.held), channel_id=1, source_target_pairs={{0,1},{1,0},{2,3},{3,2},{4,5},{5,4},{6,7},{7,6},{8,9},{9,8},{10,11... | collective-permute-start | bytes 202760 | tf_op jit(solution)/shard_map/ppermute | solution.py:262
